TPU v7x, 32 devices: a whole 2x2x4 slice. The times are simulated.
32 devices in a mesh: row: 8 (over z, core), col: 4 (over y, x).
Axes of the slice: x: 2, y: 2, z: 4, core: 2. Of those that a mesh axis runs over, the one named last changes fastest.
Arguments:
- context: bfloat16 [128, 8192], P('col', 'row'), may hold values from -6 to 6
- weight: bfloat16 [8192, 16384], P('row', 'col'), may hold values from -0.0625 to 0.0625
- feature_bias: float32 [16384], P('col'), may hold values from -3 to 3
- covariance: float32 [16384, 16384], P('row', 'col'), may hold values from -0.5 to 2.5, as said below
- prior_mean: float32 [16384], P('row'), may hold values from -6 to 6
- rewards: float32 [128], replicated, may hold values from -12 to 12
Outputs:
- posterior_cov: float32 [16384, 16384], P('row', 'col')
- posterior_mean: float32 [16384], P('row')
Inputs may be any that keep to these rules, and one draw needn't show every extreme that they name: covariance is exactly symmetric and positive definite.
All inputs are finite; a program needn't handle non-finite values.
Results may differ from a plain program's by a relative error of at most 0.00042.
Values may be sent and summed in bfloat16 or wider, within the bound.
No kernel may reach another device: no remote copies, remote signals or barrier semaphores. Data moves between devices by JAX's collectives and lax.ppermute only.
A program may use at most 128 MiB of HBM per device.

v0:
```python
import jax
import jax.numpy as jnp
from jax import lax
from jax.sharding import PartitionSpec as P


def broadcast(array, axis, root):
    mine = lax.axis_index(axis) == root
    return lax.psum(jnp.where(mine, array, jnp.zeros_like(array)), axis)


def per_device(context, weight, feature_bias, covariance, prior_mean, rewards):
    highest = lax.Precision.HIGHEST
    group_ratio = lax.axis_size("row") // lax.axis_size("col")
    row_index = lax.axis_index("row")
    col_index = lax.axis_index("col")
    row_width = covariance.shape[0]
    tokens = lax.all_gather(context, "col", axis=0, tiled=True)
    partial_value = jnp.dot(tokens, weight, preferred_element_type=jnp.float32)
    summed = lax.psum_scatter(partial_value, "row", scatter_dimension=0, tiled=True)
    features = jnp.tanh(summed + feature_bias[None, :]).astype(jnp.bfloat16)
    phi_col = lax.all_gather(features, "row", axis=0, tiled=True)
    phi_held = broadcast(phi_col, "col", row_index // group_ratio)
    phi_row = lax.dynamic_slice_in_dim(phi_held, row_index % group_ratio * row_width, row_width, 1)
    col32 = phi_col.astype(jnp.float32)
    row32 = phi_row.astype(jnp.float32)
    panel_part = jnp.einsum("ik,bk->ib", covariance, col32, precision=highest)
    mean_part = jnp.dot(row32, prior_mean, precision=highest)
    panel = lax.psum(panel_part, "col")
    gram_part = jnp.dot(row32, panel, precision=highest)
    gram_matrix, predicted = lax.psum((gram_part, mean_part), "row")
    order = gram_matrix.shape[0]
    gram_matrix = gram_matrix + jnp.eye(order, dtype=jnp.float32)
    lower_factor = jnp.linalg.cholesky(gram_matrix)
    lower_inverse = lax.linalg.triangular_solve(
        lower_factor, jnp.eye(order, dtype=jnp.float32), left_side=True, lower=True
    )
    inverse_gram = jnp.dot(lower_inverse.T, lower_inverse, precision=highest)
    coeffs = jnp.dot(inverse_gram, rewards - predicted, precision=highest)
    gain_rows = jnp.dot(panel, inverse_gram, precision=highest)
    posterior_mean = prior_mean + jnp.dot(panel, coeffs, precision=highest)
    pieces = []
    for member in range(group_ratio):
        pieces.append(broadcast(panel, "row", col_index * group_ratio + member))
    far_panel = jnp.concatenate(pieces, 0)
    update = jnp.einsum("ib,jb->ij", gain_rows, far_panel, precision=highest)
    posterior_cov = covariance - update
    return (posterior_cov, posterior_mean)


def solution(mesh):
    return jax.shard_map(
        per_device,
        mesh=mesh,
        in_specs=(P("col", "row"), P("row", "col"), P("col"), P("row", "col"), P("row"), P()),
        out_specs=(P("row", "col"), P("row")),
        check_vma=False,
    )
```

profile of v0, /device:TPU:0, one launch (start us, length us, event | category | flops | bytes accessed | tf_op | source)
XLA Modules:
  0.0 354.1 jit_solution(6449057653795028076)
XLA Ops:
  7.2 0.0 reduce-scatter.2.cloned.1.call-start
  7.2 10.7 %all_gather.6 = bf16[128,1024]{1,0:T(8,128)(2,1)S(1)} all-gather(bf16[32,1024]{1,0:T(8,128)(2,1)} %param.6), channel_id=1, replica_groups=mesh['row'=8,'col'=4] {'col'}, dimensions={0}, use_global_device_ids=true | all-gather | bytes 327680 | tf_op jit(solution)/shard_map/all_gather | solution.py:18
  17.9 0.0 copy-start.3
  17.9 6.0 %fusion.15 = f32[128,4096]{1,0:T(8,128)} fusion(bf16[128,1024]{1,0:T(8,128)(2,1)S(1)} %all_gather.6, bf16[1024,4096]{1,0:T(8,128)(2,1)} %param.7), kind=kOutput, calls=%fused_computation.30 | convolution fusion | flops 1073741824 | bytes 10747904 | tf_op jit(solution)/shard_map/dot_general | solution.py:19
  23.9 0.0 reduce-scatter.2.cloned.1.call-update
  23.9 0.0 all-gather.2.cloned.1.call-start
  24.0 36.3 %reduce-scatter.2.cloned.1.call-done = f32[16,4096]{1,0:T(8,128)} async-done(((f32[128,4096]{1,0:T(8,128)}), f32[16,4096]{1,0:T(8,128)}) %reduce-scatter.2.cloned.1.call-update) | async-done | bytes 262160 | tf_op jit(solution)/shard_map/reduce_scatter | solution.py:20
  60.3 0.0 copy-done.3
  60.3 1.6 tanh_convert_fusion
  61.9 0.0 all-gather.2.cloned.1.call-update
  62.0 0.0 all-reduce.5.cloned.1.call-start
  62.0 21.1 %all-gather.2.cloned.1.call-done = bf16[128,4096]{1,0:T(8,128)(2,1)} async-done(((bf16[16,4096]{1,0:T(8,128)(2,1)}), bf16[128,4096]{1,0:T(8,128)(2,1)}) %all-gather.2.cloned.1.call-update) | async-done | bytes 1048592 | tf_op jit(solution)/shard_map/all_gather | solution.py:22
  83.1 0.0 copy-start.1
  83.1 23.3 %convolution_bitcast_fusion = f32[2048,128]{0,1:T(8,128)} fusion(bf16[128,4096]{1,0:T(8,128)(2,1)} %all-gather.2.cloned.1.call-done, f32[2048,4096]{1,0:T(8,128)} %param.9), kind=kOutput, calls=%fused_computation.1 | convolution fusion | flops 12884901888 | bytes 35651584 | tf_op jit(solution)/shard_map/ik,bk->ib/dot_general | solution.py:27
  106.5 0.0 copy-start.2
  106.5 0.0 copy-start.4
  106.5 0.0 all-reduce.5.cloned.1.call-update
  106.5 0.0 all-reduce.7.cloned.1.call-start
  106.6 0.0 copy-done.1
  106.6 1.1 broadcast_select_fusion
  107.6 0.0 all-reduce.7.cloned.1.call-update
  107.7 0.0 all-reduce.9.cloned.1.call-start
  107.7 51.1 %all-reduce.5.cloned.1.call-done = f32[2048,128]{0,1:T(8,128)} async-done(((f32[2048,128]{0,1:T(8,128)}), f32[2048,128]{0,1:T(8,128)}) %all-reduce.5.cloned.1.call-update) | async-done | bytes 1048592 | tf_op jit(solution)/shard_map/psum | solution.py:29
  158.8 0.0 copy-start
  158.8 55.5 %all-reduce.7.cloned.1.call-done = bf16[128,4096]{1,0:T(8,128)(2,1)} async-done(((bf16[128,4096]{1,0:T(8,128)(2,1)}), bf16[128,4096]{1,0:T(8,128)(2,1)}) %all-reduce.7.cloned.1.call-update) | async-done | bytes 1048592 | tf_op jit(solution)/shard_map/psum | solution.py:9
  214.3 2.7 fusion.4
  217.0 2.8 broadcast_select_fusion.2
  219.8 0.0 all-reduce.9.cloned.1.call-update
  219.8 0.0 copy-done.2
  219.8 1.6 convolution_bitcast_fusion.2
  221.4 17.0 %psum.47 = f32[128]{0:T(128)S(1)} all-reduce(f32[128]{0:T(128)S(1)} %convolution_bitcast_fusion.2), channel_id=1, replica_groups=mesh['row'=8,'col'=4] {'row'}, use_global_device_ids=true, to_apply=%region_8.9 | all-reduce | flops 128 | bytes 1024 | tf_op jit(solution)/shard_map/psum | solution.py:31
  238.3 47.3 %all-reduce.9.cloned.1.call-done = (f32[128,128]{1,0:T(8,128)}, f32[2048,128]{0,1:T(8,128)}, f32[2048,128]{0,1:T(8,128)}) async-done(((f32[128,128]{1,0:T(8,128)}, f32[2048,128]{0,1:T(8,128)}, f32[2048,128]{0,1:T(8,128)}), (f32[128,128]{1,0:T(8,128)}, f32[2048,128]{0,1:T(8,128)}, f32[2048,128]{0,1:T(8,128)})) %all-reduce.9.cloned.1.call-update) | async-done | bytes 2162704 | tf_op jit(solution)/shard_map/psum | solution.py:31
  285.6 0.9 convert_add_fusion
  286.5 0.1 copy.8
  286.6 0.9 fusion.9
  287.4 11.7 %cholesky.18 = f32[128,128]{1,0:T(8,128)S(1)} custom-call(f32[128,128]{1,0:T(8,128)S(1)} %fusion.9), custom_call_target="Cholesky" | custom-call | tf_op jit(solution)/shard_map/jit(cholesky)/cholesky | solution.py:34
  299.2 0.6 compare_reduce_fusion
  299.8 0.7 fusion.6
  300.5 9.8 %custom-call.6 = f32[1,128,128]{1,2,0:T(8,128)S(1)} custom-call(f32[1,128,128]{2,1,0:T(8,128)S(1)} %fusion.6), custom_call_target="InvertDiagBlocksLowerTriangular" | custom-call | tf_op jit(solution)/shard_map/triangular_solve | solution.py:35
  310.3 0.2 fusion.7
  310.5 0.3 fusion.16
  310.8 0.0 copy-done.4
  310.9 0.2 convolution_bitcast_fusion.1
  311.0 0.0 copy-done
  311.0 0.7 fusion.18
  311.7 0.6 add.57
  312.3 1.8 fusion.17
  314.2 33.4 %convolution_subtract_fusion = f32[2048,4096]{1,0:T(8,128)} fusion(f32[2048,4096]{1,0:T(8,128)} %param.9, f32[2048,128]{1,0:T(8,128)S(1)} %fusion.17, f32[2048,128]{0,1:T(8,128)} %get-tuple-element.3, f32[2048,128]{0,1:T(8,128)} %get-tuple-element.4), kind=kOutput, calls=%fused_computation | convolution fusion | flops 12893814784 | bytes 70254592 | tf_op jit(solution)/shard_map/ib,jb->ij/dot_general | solution.py:46
  (1 shorter events, 0.0 us)
Async XLA Ops:
  7.2 53.1 %reduce-scatter.2.cloned.1.call-start = ((), (), s32[]{:S(2)}) async-start(), calls=%async_computation.1 | async-start | bytes 2359296 | tf_op jit(solution)/shard_map/reduce_scatter | solution.py:20
  17.9 42.4 %copy-start.3 = (f32[4096]{0:T(1024)S(1)}, f32[4096]{0:T(1024)}, u32[]{:S(2)}) copy-start(f32[4096]{0:T(1024)} %param.8) | copy-start | bytes 49156
  23.9 59.2 %all-gather.2.cloned.1.call-start = ((), (), s32[]{:S(2)}) async-start(), calls=%async_computation.2 | async-start | bytes 1179648 | tf_op jit(solution)/shard_map/all_gather | solution.py:22
  62.0 96.9 %all-reduce.5.cloned.1.call-start = ((), (), s32[]{:S(2)}) async-start(), calls=%async_computation.3 | async-start | bytes 2097152 | tf_op jit(solution)/shard_map/psum | solution.py:29
  83.1 23.4 %copy-start.1 = (bf16[128,4096]{1,0:T(8,128)(2,1)S(1)}, bf16[128,4096]{1,0:T(8,128)(2,1)}, u32[]{:S(2)}) copy-start(bf16[128,4096]{1,0:T(8,128)(2,1)} %all-gather.2.cloned.1.call-done) | copy-start | bytes 3145732
  106.5 113.4 %copy-start.2 = (f32[2048]{0:T(1024)S(1)}, f32[2048]{0:T(1024)}, u32[]{:S(2)}) copy-start(f32[2048]{0:T(1024)} %param.10) | copy-start | bytes 24580
  106.5 204.4 %copy-start.4 = (f32[128]{0:T(128)S(1)}, f32[128]{0:T(128)}, u32[]{:S(2)}) copy-start(f32[128]{0:T(128)} %param.11) | copy-start | bytes 1540
  106.5 107.8 %all-reduce.7.cloned.1.call-start = ((), (), s32[]{:S(2)}) async-start(), calls=%async_computation.4 | async-start | bytes 2097152 | tf_op jit(solution)/shard_map/psum | solution.py:9
  107.7 177.9 %all-reduce.9.cloned.1.call-start = ((), (), s32[]{:S(2)}) async-start(), calls=%async_computation.5 | async-start | bytes 4325376 | tf_op jit(solution)/shard_map/psum | solution.py:31
  158.8 152.2 %copy-start = (f32[2048,128]{0,1:T(8,128)S(1)}, f32[2048,128]{0,1:T(8,128)}, u32[]{:S(2)}) copy-start(f32[2048,128]{0,1:T(8,128)} %all-reduce.5.cloned.1.call-done) | copy-start | bytes 3145732
Sparse Core Ops, SparseCore 0:
  24.1 36.1 reduce-scatter.1
  62.5 20.6 all-gather.1
  106.6 52.1 all-reduce.4
  161.7 52.5 all-reduce.6
  219.9 65.6 all-reduce.8
where the time goes:
time: 355 us; the launch traced here: 354 us
  waiting for transfers between devices  211 us (59%)
  matrix products  70.2 us (20%)
  other arithmetic  30.7 us (9%)
  blocking collectives  27.7 us (8%)
  between operations  13.9 us (4%)
    psum x1, waiting for transfers between devices, broadcast(): return lax.psum(jnp.where(mine, array, jnp.zeros_like(array)), axis)  55.5 us
    psum x1, waiting for transfers between devices, per_device(): panel = lax.psum(panel_part, 'col')  51.1 us
    psum x1, waiting for transfers between devices, per_device(): gram_matrix, predicted = lax.psum((gram_part, mean_part), 'row')  47.3 us
    reduce_scatter x1, waiting for transfers between devices, per_device(): lax.psum_scatter(partial_value, 'row', scatter_dimension=0, tiled=True)  36.3 us
    dot_general x1, matrix products, per_device(): update = jnp.einsum('ib,jb->ij', gain_rows, far_panel, precision=highest)  33.4 us
    dot_general x1, matrix products, per_device(): panel_part = jnp.einsum('ik,bk->ib', covariance, col32, precision=highest)  23.3 us
    all_gather x1, waiting for transfers between devices, per_device(): phi_col = lax.all_gather(features, 'row', axis=0, tiled=True)  21.1 us
    psum x1, blocking collectives, per_device(): gram_matrix, predicted = lax.psum((gram_part, mean_part), 'row')  17 us
  transfers between devices with their start and end apart: 5, of which 5 were waited for; matrix products, arithmetic and copies ran while one was open for 1% of the time, Pallas kernels for 0%

commit v1 on v0

--- a/solution.py
+++ b/solution.py
@@ -1,7 +1,37 @@
+import functools
+
 import jax
 import jax.numpy as jnp
 from jax import lax
+from jax.experimental import pallas as pl
+from jax.experimental.pallas import tpu as pltpu
 from jax.sharding import PartitionSpec as P
+
+F32 = jnp.float32
+BF16 = jnp.bfloat16
+MIB = 1 << 20
+NT = (((1,), (1,)), ((), ()))
+TN = (((0,), (0,)), ((), ()))
+
+
+def dot(a, b, dims=(((1,), (0,)), ((), ()))):
+    return lax.dot_general(a, b, dims, preferred_element_type=F32)
+
+
+def split2(x):
+    hi = x.astype(BF16)
+    return hi, (x - hi.astype(F32)).astype(BF16)
+
+
+def split3(x):
+    hi = x.astype(BF16)
+    rest = x - hi.astype(F32)
+    mid = rest.astype(BF16)
+    return hi, mid, (rest - mid.astype(F32)).astype(BF16)
+
+
+def vmem(n):
+    return [pl.BlockSpec(memory_space=pltpu.VMEM)] * n
 
 
 def broadcast(array, axis, root):
@@ -9,7 +39,7 @@
     return lax.psum(jnp.where(mine, array, jnp.zeros_like(array)), axis)
 
 
-def per_device(context, weight, feature_bias, covariance, prior_mean, rewards):
+def plain(context, weight, feature_bias, covariance, prior_mean, rewards):
     highest = lax.Precision.HIGHEST
     group_ratio = lax.axis_size("row") // lax.axis_size("col")
     row_index = lax.axis_index("row")
@@ -48,6 +78,379 @@
     return (posterior_cov, posterior_mean)
 
 
+def swap_col(x, step):
+    n = lax.axis_size("col")
+    return lax.ppermute(x, "col", [(i, i ^ step) for i in range(n)])
+
+
+def swap_outer(x, step):
+    n, inner = lax.axis_size("row"), lax.axis_size("row") // lax.axis_size("col")
+    return lax.ppermute(x, "row", [(i, i ^ (step * inner)) for i in range(n)])
+
+
+def swap_inner(x, step):
+    return lax.ppermute(x, "row", [(i, i ^ step) for i in range(lax.axis_size("row"))])
+
+
+def transpose(x):
+    cols = lax.axis_size("col")
+    inner = lax.axis_size("row") // cols
+    pairs = []
+    for outer in range(cols):
+        for k in range(inner):
+            for col in range(cols):
+                pairs.append(((outer * inner + k) * cols + col, (col * inner + k) * cols + outer))
+    return lax.ppermute(x, ("row", "col"), pairs)
+
+
+def total(x):
+    step = 1
+    while step < lax.axis_size("row"):
+        x = x + lax.ppermute(x, "row", [(i, i ^ step) for i in range(lax.axis_size("row"))])
+        step *= 2
+    step = 1
+    while step < lax.axis_size("col"):
+        x = x + swap_col(x, step)
+        step *= 2
+    return x
+
+
+def places():
+    cols = lax.axis_size("col")
+    inner = lax.axis_size("row") // cols
+    row = lax.axis_index("row")
+    return row // inner, row % inner, lax.axis_index("col"), inner, cols
+
+
+def span(index, size):
+    return pl.ds(pl.multiple_of(index * size, size), size)
+
+
+def call(kernel, name, limit, operands, in_specs, out_specs, out_shape, scratch_shapes=(), flops=0, size=0):
+    return pl.pallas_call(
+        kernel,
+        in_specs=in_specs,
+        out_specs=out_specs,
+        out_shape=out_shape,
+        scratch_shapes=scratch_shapes,
+        cost_estimate=pl.CostEstimate(flops=flops, bytes_accessed=size, transcendentals=0),
+        compiler_params=pltpu.CompilerParams(vmem_limit_bytes=limit * MIB),
+        name=name,
+    )(*operands)
+
+
+def hold_kernel(in_ref, out_ref, sem):
+    copy = pltpu.make_async_copy(in_ref, out_ref, sem)
+    copy.start()
+    copy.wait()
+
+
+def hold(x, name):
+    return call(
+        hold_kernel,
+        name,
+        1,
+        (x,),
+        [pl.BlockSpec(memory_space=pl.ANY)],
+        pl.BlockSpec(memory_space=pltpu.VMEM),
+        pltpu.VMEM(x.shape, x.dtype),
+        [pltpu.SemaphoreType.DMA],
+        size=x.size * x.dtype.itemsize,
+    )
+
+
+def in_vmem(x):
+    return pltpu.with_memory_space_constraint(x, pltpu.VMEM)
+
+
+def preact_kernel(step, *refs):
+    *blocks, w_ref, out_ref, held = refs
+    _, inner_index, col, _, _ = places()
+    rows = blocks[0].shape[0]
+    width = out_ref.shape[1]
+    tile = min(512, width)
+    for s, block in enumerate(blocks):
+        held[span(col ^ s, rows), :] = block[...].astype(F32)
+    tokens = held[...].astype(BF16)
+    first = (inner_index ^ step) * (width // tile)
+    for t in range(width // tile):
+        out_ref[:, t * tile : (t + 1) * tile] = dot(tokens, w_ref[:, span(first + t, tile)])
+
+
+def preact_part(step, blocks, weight, width):
+    rows, depth = blocks[0].shape
+    n = len(blocks)
+    return call(
+        functools.partial(preact_kernel, step),
+        "preact_part",
+        8,
+        (*blocks, in_vmem(weight)),
+        vmem(n + 1),
+        vmem(1)[0],
+        jax.ShapeDtypeStruct((rows * n, width), F32),
+        [pltpu.VMEM((rows * n, depth), F32)],
+        2 * rows * n * depth * width,
+        2 * depth * width,
+    )
+
+
+def scatter_kernel(n, *refs):
+    sums, outs = refs[:n], refs[n:]
+    outer, *_ = places()
+    width = outs[0].shape[1]
+    for s, out in enumerate(outs):
+        here = span(outer ^ s, width)
+        out[...] = sum(x[:, here] for x in sums)
+
+
+def scatter(sums, count):
+    rows, width = sums[0].shape
+    shape = jax.ShapeDtypeStruct((rows, width // count), F32)
+    return call(
+        functools.partial(scatter_kernel, len(sums)), "scatter", 8, sums, vmem(len(sums)), vmem(count), [shape] * count, size=8 * rows * width
+    )
+
+
+def feature_kernel(bias_ref, *refs):
+    *parts, out_ref = refs
+    outer, inner_index, _, _, cols = places()
+    here = span(inner_index * cols + outer, out_ref.shape[1])
+    out_ref[...] = jnp.tanh(sum(p[...] for p in parts) + bias_ref[:, here]).astype(BF16)
+
+
+def features_of(bias, parts):
+    rows, width = parts[0].shape
+    return call(
+        feature_kernel,
+        "features",
+        8,
+        (bias.reshape(1, bias.shape[0]), *parts),
+        vmem(1 + len(parts)),
+        vmem(1)[0],
+        jax.ShapeDtypeStruct((rows, width), BF16),
+        size=16 * rows * width,
+    )
+
+
+def panel_kernel(steps, last, c_ref, *refs):
+    n = len(steps)
+    shards, rest = refs[:n], refs[n:]
+    outer, inner_index, col, _, cols = places()
+    acc_ref = None if len(rest) == (cols if last else 1) else rest[0]
+    outs = rest[-cols:] if last else rest[-1:]
+    width = shards[0].shape[1]
+    quarter = c_ref.shape[0] // cols
+    rows = min(256, quarter)
+    per = quarter // rows
+    for q in range(cols):
+        block = (col ^ q) if last else q
+
+        @pl.loop(0, per)
+        def _(i, q=q, block=block):
+            here = span(block * per + i, rows)
+            sums = None if acc_ref is None else acc_ref[here, :]
+            for shard, (s, k) in zip(shards, steps):
+                hi, lo = split2(c_ref[here, span((inner_index ^ k) * cols + (outer ^ s), width)])
+                phi = shard[...]
+                term = dot(hi, phi, NT) + dot(lo, phi, NT)
+                sums = term if sums is None else sums + term
+            if last:
+                outs[q][span(i, rows), :] = sums.astype(outs[q].dtype)
+            else:
+                outs[0][here, :] = sums
+
+
+def panel_part(covariance, shards, steps, acc=None, send=None):
+    n = len(shards)
+    batch, width = shards[0].shape
+    rows = covariance.shape[0]
+    cols = lax.axis_size("col")
+    operands = [in_vmem(covariance), *shards] + ([] if acc is None else [acc])
+    if send is None:
+        shape = [jax.ShapeDtypeStruct((rows, batch), F32)]
+    else:
+        shape = [jax.ShapeDtypeStruct((rows // cols, batch), send if s else F32) for s in range(cols)]
+    outs = call(
+        functools.partial(panel_kernel, tuple(steps), send is not None),
+        "panel_part",
+        12,
+        operands,
+        vmem(len(operands)),
+        vmem(len(shape)),
+        shape,
+        (),
+        4 * rows * width * n * batch,
+        4 * rows * width * n,
+    )
+    return outs[0] if send is None else outs
+
+
+def gram_kernel(phi_ref, mean_ref, *refs):
+    *parts, panel_ref, gram_ref = refs
+    _, _, col, _, _ = places()
+    panel = parts[0][...]
+    for part in parts[1:]:
+        panel = panel + part[...].astype(F32)
+    panel_ref[...] = panel.astype(BF16)
+    phi = phi_ref[...]
+    batch = phi.shape[0]
+    gram_ref[:batch, :] = sum(dot(phi, piece) for piece in split3(panel))
+    mean = jnp.broadcast_to(mean_ref[:, span(col, panel.shape[0])], (8, panel.shape[0]))
+    gram_ref[batch:, :] = sum(dot(piece, phi, NT) for piece in split3(mean))
+
+
+def gram_part(phi, mean, parts):
+    rows, batch = parts[0].shape
+    return call(
+        gram_kernel,
+        "gram_part",
+        8,
+        (phi, mean.reshape(1, mean.shape[0]), *parts),
+        vmem(2 + len(parts)),
+        vmem(2),
+        [jax.ShapeDtypeStruct((rows, batch), BF16), jax.ShapeDtypeStruct((batch + 8, batch), F32)],
+    )
+
+
+def inverse_kernel(gram_ref, rewards_ref, inverse_ref, coeffs_ref, held):
+    n = rewards_ref.shape[1]
+    highest = lax.Precision.HIGHEST
+    lane = lax.broadcasted_iota(jnp.int32, (8, n), 1)
+    sub = lax.broadcasted_iota(jnp.int32, (8, n), 0)
+    i = lax.broadcasted_iota(jnp.int32, (n, n), 0)
+    j = lax.broadcasted_iota(jnp.int32, (n, n), 1)
+    held[...] = gram_ref[:n, :] + jnp.where(i == j, 1.0, 0.0)
+    for first in range(0, n, 8):
+        block = held[first : first + 8, :]
+        inside = (lane >= first) & (lane < first + 8)
+        eye = jnp.where(lane == sub + first, 1.0, 0.0)
+        x, y = block, eye
+        for t in range(8):
+            column = jnp.broadcast_to(x[:, first + t : first + t + 1], (8, n))
+            pivot = 1.0 / jnp.broadcast_to(x[t : t + 1, first + t : first + t + 1], (8, n))
+            row_x = jnp.broadcast_to(x[t : t + 1, :], (8, n)) * pivot
+            row_y = jnp.broadcast_to(y[t : t + 1, :], (8, n)) * pivot
+            x = jnp.where(sub == t, row_x, x - column * row_x)
+            y = jnp.where(sub == t, row_y, y - column * row_y)
+        spread = jnp.where(inside, -y, x)
+        rest = jnp.where((j >= first) & (j < first + 8), 0.0, held[...])
+        held[...] = rest - lax.dot_general(block, spread, TN, precision=highest, preferred_element_type=F32)
+        held[first : first + 8, :] = spread
+    inverse = -held[...]
+    inverse_ref[...] = inverse
+    gap = jnp.broadcast_to(rewards_ref[...] - gram_ref[n : n + 1, :], (8, n))
+    coeffs_ref[...] = lax.dot_general(gap, inverse, (((1,), (0,)), ((), ())), precision=highest, preferred_element_type=F32)
+
+
+def inverse_and_coeffs(gram, rewards):
+    n = rewards.shape[0]
+    return call(
+        inverse_kernel,
+        "inverse",
+        8,
+        (gram, rewards.reshape(1, n)),
+        vmem(2),
+        vmem(2),
+        [jax.ShapeDtypeStruct((n, n), F32), jax.ShapeDtypeStruct((8, n), F32)],
+        [pltpu.VMEM((n, n), F32)],
+    )
+
+
+def update_kernel(near, far, tile, *refs):
+    c_ref, inverse_ref, coeffs_ref, mean_ref = refs[:4]
+    near_refs = refs[4 : 4 + near]
+    far_refs = refs[4 + near : 4 + near + far]
+    out_ref, new_mean_ref, gain, panel, other = refs[4 + near + far :]
+    outer, inner_index, col, _, cols = places()
+    batch = inverse_ref.shape[0]
+    quarter = near_refs[0].shape[0]
+    for s, part in enumerate(near_refs):
+        panel[span(col ^ s, quarter), :] = part[...]
+    for s, part in enumerate(far_refs):
+        here = span((inner_index ^ (s // cols)) * cols + (outer ^ (s % cols)), quarter)
+        other[here, :batch] = part[...]
+        other[here, batch:] = part[...]
+    hi, lo = split2(inverse_ref[...])
+    rows = panel[...]
+    product = dot(rows, hi) + dot(rows, lo)
+    hi, lo = split2(product)
+    gain[:, :batch] = hi
+    gain[:, batch:] = lo
+    new_mean_ref[...] = mean_ref[...] + sum(dot(p, rows, NT) for p in split3(coeffs_ref[...]))[:1]
+
+    def body(step, block):
+        here = span(step.index[0], tile)
+        block[...] = c_ref[here, :] - dot(gain[here, :], other[...], NT)
+
+    pltpu.emit_pipeline(
+        body,
+        grid=(c_ref.shape[0] // tile,),
+        in_specs=[],
+        out_specs=[pl.BlockSpec((tile, c_ref.shape[1]), lambda i: (i, 0))],
+        _explicit_indices=True,
+    )(out_ref)
+
+
+def update(covariance, inverse, coeffs, mean, near, far):
+    rows, cols = covariance.shape
+    batch = inverse.shape[0]
+    return call(
+        functools.partial(update_kernel, len(near), len(far), min(256, rows)),
+        "update",
+        20,
+        (in_vmem(covariance), inverse, coeffs, mean.reshape(1, rows), *near, *far),
+        vmem(4 + len(near) + len(far)),
+        [pl.BlockSpec(memory_space=pl.ANY), vmem(1)[0]],
+        [jax.ShapeDtypeStruct((rows, cols), F32), jax.ShapeDtypeStruct((1, rows), F32)],
+        [
+            pltpu.VMEM((rows, 2 * batch), BF16),
+            pltpu.VMEM((rows, batch), BF16),
+            pltpu.VMEM((cols, 2 * batch), BF16),
+        ],
+    )
+
+
+def per_device(context, weight, feature_bias, covariance, prior_mean, rewards):
+    cols = lax.axis_size("col")
+    inner = lax.axis_size("row") // cols
+    rows, block = covariance.shape
+    part = block // inner
+    if (part // cols) % 128 or (rows // cols) % 128:
+        return plain(context, weight, feature_bias, covariance, prior_mean, rewards)
+
+    blocks = [context] + [swap_col(context, s) for s in range(1, cols)]
+    w_held = hold(weight, "hold_weight")
+    sums = []
+    for k in range(inner - 1, -1, -1):
+        piece = preact_part(k, blocks, w_held, part)
+        sums.append(swap_inner(piece, k) if k else piece)
+    pieces = scatter(sums, cols)
+    summed = [pieces[0]] + [swap_outer(pieces[s], s) for s in range(1, cols)]
+    features = features_of(feature_bias, summed)
+
+    held = hold(covariance, "hold_covariance")
+    shards = [features] + [swap_outer(features, s) for s in range(1, cols)]
+    panel = panel_part(held, shards, [(s, 0) for s in range(cols)])
+    for k in range(1, inner):
+        others = [swap_inner(s, k) for s in shards]
+        panel = panel_part(
+            held, others, [(s, k) for s in range(cols)], panel, F32 if k == inner - 1 else None
+        )
+
+    far_features = transpose(features)
+    parts = [panel[0]] + [swap_col(panel[s], s) for s in range(1, cols)]
+    own_panel, gram = gram_part(far_features, prior_mean, parts)
+    near = [own_panel] + [swap_col(own_panel, s) for s in range(1, cols)]
+    turned = transpose(own_panel)
+    far = [turned] + [swap_outer(turned, s) for s in range(1, cols)]
+    for k in range(1, inner):
+        far += [swap_inner(f, k) for f in far[:cols]]
+
+    inverse, coeffs = inverse_and_coeffs(total(gram), rewards)
+    new_cov, new_mean = update(held, inverse, coeffs, prior_mean, near, far)
+    return new_cov, new_mean.reshape(rows)
+
+
 def solution(mesh):
     return jax.shard_map(
         per_device,

time: 355 us -> 167 us (0.47)
  waiting for transfers between devices: 211 us -> 47 us
  matrix products: 70.2 us -> 0 us
  Pallas kernels: 0 us -> 56.6 us
  starting transfers between devices: 0.21 us -> 46.8 us
  other arithmetic: 30.7 us -> 0.05 us
  blocking collectives: 27.7 us -> 0 us
  local copies, waits for them, and re-layouts: 0.11 us -> 15.6 us
  between operations: 13.9 us -> 0.93 us
    psum x3 -> x0, waiting for transfers between devices: 154 us -> none  [the longest x1 55.5 us: broadcast(): return lax.psum(jnp.where(mine, array, jnp.zeros_like(array)), axis)]
    dot_general x9 -> x0, matrix products: 70 us -> none  [the longest x1 33.4 us: per_device(): update = jnp.einsum('ib,jb->ij', gain_rows, far_panel, precision=highest)]
    pallas_call x0 -> x11, Pallas kernels: none -> 56.6 us  [call(): pl.pallas_call(kernel, in_specs=in_specs, out_specs=out_specs, out_shape=...]
    ppermute x0 -> x34, waiting for transfers between devices: none -> 47 us  [the longest x9 23.7 us: swap_outer(): return lax.ppermute(x, 'row', [(i, i ^ step * inner) for i in range(n)])]
    ppermute x0 -> x34, starting transfers between devices: none -> 46.8 us  [the longest x11 21.7 us: swap_col(): return lax.ppermute(x, 'col', [(i, i ^ step) for i in range(n)])]
    reduce_scatter x1 -> x0, waiting for transfers between devices: 36.3 us -> none  [per_device(): lax.psum_scatter(partial_value, 'row', scatter_dimension=0, tiled=True)]
    another operation x5 -> x0, other arithmetic: 22.9 us -> none  [the longest x3 12.4 us: per_device(): lower_factor = jnp.linalg.cholesky(gram_matrix)]
    all_gather x1 -> x0, waiting for transfers between devices: 21.1 us -> none  [per_device(): phi_col = lax.all_gather(features, 'row', axis=0, tiled=True)]
  transfers between devices with their start and end apart: 5 -> 34, of which waited for: 5 -> 11; matrix products, arithmetic and copies ran while one was open for 1% -> 0% of each run, Pallas kernels for 0% -> 21%
where the time goes in v1:
time: 167 us
  Pallas kernels  56.6 us (34%)
  waiting for transfers between devices  47 us (28%)
  starting transfers between devices  46.8 us (28%)
  local copies, waits for them, and re-layouts  15.6 us (9%)
    pallas_call x11, Pallas kernels, call(): pl.pallas_call(kernel, in_specs=in_specs, out_specs=out_specs, out_shape=...  56.6 us
    ppermute x9, waiting for transfers between devices, swap_outer(): return lax.ppermute(x, 'row', [(i, i ^ step * inner) for i in range(n)])  23.7 us
    ppermute x11, starting transfers between devices, swap_col(): return lax.ppermute(x, 'col', [(i, i ^ step) for i in range(n)])  21.7 us
    ppermute x9, starting transfers between devices, swap_outer(): return lax.ppermute(x, 'row', [(i, i ^ step * inner) for i in range(n)])  18.5 us
    unnamed x16, local copies, waits for them, and re-layouts  15.6 us
    ppermute x11, waiting for transfers between devices, swap_col(): return lax.ppermute(x, 'col', [(i, i ^ step) for i in range(n)])  14.7 us
    ppermute x3, waiting for transfers between devices, total(): lax.ppermute(x, 'row', [(i, i ^ step) for i in range(lax.axis_size('row'))])  7.43 us
  transfers between devices with their start and end apart: 34, of which 11 were waited for; matrix products, arithmetic and copies ran while one was open for 0% of the time, Pallas kernels for 21%

profile of v1, /device:TPU:0, one launch (start us, length us, event | category | flops | bytes accessed | tf_op | source)
XLA Modules:
  0.0 167.0 jit_solution(8068331751383205836)
XLA Ops:
  0.6 4.0 %collective-permute-start.2 = (bf16[32,1024]{1,0:T(8,128)(2,1)}, bf16[32,1024]{1,0:T(8,128)(2,1)S(1)}, u32[]{:S(2)}, u32[]{:S(2)}) collective-permute-start(bf16[32,1024]{1,0:T(8,128)(2,1)} %refs_0_.3), channel_id=1, source_target_pairs={{0,3},{1,2},{2,1},{3,0},{4,7},{5,6},{6,5},{7,4},{8,11},{9,10},{10,... | collective-permute-start | bytes 196616 | tf_op jit(solution)/shard_map/ppermute | solution.py:83
  4.6 0.5 collective-permute-start.1
  5.1 0.1 collective-permute-start
  5.2 3.4 %copy-done.2 = bf16[1024,4096]{1,0:T(8,128)(2,1)S(1)} copy-done((bf16[1024,4096]{1,0:T(8,128)(2,1)S(1)}, bf16[1024,4096]{1,0:T(8,128)(2,1)}, u32[]{:S(2)}) %copy-start.2) | copy-done | bytes 8388632
  8.6 0.6 hold_weight.1.refs_4_
  9.2 0.0 collective-permute-done.2.refs_3_
  9.2 0.0 collective-permute-done.1.refs_2_
  9.2 0.4 collective-permute-done.refs_1_
  9.6 0.8 copy-done.3
  10.4 0.8 preact_part.2
  11.2 0.1 collective-permute-start.3
  11.3 0.0 copy-start.4
  11.3 0.8 copy-done.4
  12.1 0.8 preact_part.3.refs_1_
  12.9 1.0 collective-permute-done.3.refs_0_
  13.9 0.1 scatter.1
  14.0 1.7 %collective-permute-start.4 = (f32[128,512]{1,0:T(8,128)S(1)}, f32[128,512]{1,0:T(8,128)S(1)}, u32[]{:S(2)}, u32[]{:S(2)}) collective-permute-start(f32[128,512]{1,0:T(8,128)S(1)} %get-tuple-element.17), channel_id=1, source_target_pairs={{0,8},{4,12},{8,0},{12,4},{16,24},{20,28},{24,16},{28,20},{1,9},{5... | collective-permute-start | bytes 786440 | tf_op jit(solution)/shard_map/ppermute | solution.py:88
  15.7 2.6 %collective-permute-start.5 = (f32[128,512]{1,0:T(8,128)S(1)}, f32[128,512]{1,0:T(8,128)S(1)}, u32[]{:S(2)}, u32[]{:S(2)}) collective-permute-start(f32[128,512]{1,0:T(8,128)S(1)} %get-tuple-element.18), channel_id=1, source_target_pairs={{0,16},{4,20},{8,24},{12,28},{16,0},{20,4},{24,8},{28,12},{1,17},{... | collective-permute-start | bytes 786440 | tf_op jit(solution)/shard_map/ppermute | solution.py:88
  18.3 0.2 collective-permute-start.6
  18.5 9.0 %collective-permute-done.4.refs_1_ = f32[128,512]{1,0:T(8,128)S(1)} collective-permute-done((f32[128,512]{1,0:T(8,128)S(1)}, f32[128,512]{1,0:T(8,128)S(1)}, u32[]{:S(2)}, u32[]{:S(2)}) %collective-permute-start.4) | collective-permute-done | bytes 262176 | tf_op jit(solution)/shard_map/ppermute | solution.py:88
  27.5 9.6 %collective-permute-done.5.refs_2_ = f32[128,512]{1,0:T(8,128)S(1)} collective-permute-done((f32[128,512]{1,0:T(8,128)S(1)}, f32[128,512]{1,0:T(8,128)S(1)}, u32[]{:S(2)}, u32[]{:S(2)}) %collective-permute-start.5) | collective-permute-done | bytes 262176 | tf_op jit(solution)/shard_map/ppermute | solution.py:88
  37.0 0.1 features.1.refs_0_
  37.1 2.5 %collective-permute-start.13 = (bf16[128,512]{1,0:T(8,128)(2,1)S(1)}, bf16[128,512]{1,0:T(8,128)(2,1)S(1)}, u32[]{:S(2)}, u32[]{:S(2)}) collective-permute-start(bf16[128,512]{1,0:T(8,128)(2,1)S(1)} %features.1.refs_0_), channel_id=1, source_target_pairs={{0,24},{4,28},{8,16},{12,20},{16,8},{20,12},{24,0},{28,4},{1,25},{... | collective-permute-start | bytes 393224 | tf_op jit(solution)/shard_map/ppermute | solution.py:88
  39.7 6.9 %collective-permute-start.11 = (bf16[128,512]{1,0:T(8,128)(2,1)S(1)}, bf16[128,512]{1,0:T(8,128)(2,1)S(1)}, u32[]{:S(2)}, u32[]{:S(2)}) collective-permute-start(bf16[128,512]{1,0:T(8,128)(2,1)S(1)} %features.1.refs_0_), channel_id=1, source_target_pairs={{0,16},{4,20},{8,24},{12,28},{16,0},{20,4},{24,8},{28,12},{1,17},{... | collective-permute-start | bytes 393224 | tf_op jit(solution)/shard_map/ppermute | solution.py:88
  46.6 0.1 collective-permute-start.9
  46.7 10.6 %hold_covariance.1.c_ref.refs_0_ = f32[2048,4096]{1,0:T(8,128)S(1)} custom-call(f32[2048,4096]{1,0:T(8,128)} %in_ref.2), custom_call_target="tpu_custom_call" | custom-call | bytes 33554432 | tf_op jit(solution)/shard_map/hold_covariance/pallas_call | solution.py:130
  57.2 0.0 copy-start
  57.2 0.0 copy-start.5
  57.3 0.0 copy-start.7
  57.3 0.1 collective-permute-start.8
  57.4 0.5 collective-permute-start.14
  57.9 0.1 collective-permute-start.12
  57.9 0.4 collective-permute-start.10
  58.4 5.7 %panel_part.2.refs_4_ = f32[2048,128]{1,0:T(8,128)S(1)} custom-call(f32[2048,4096]{1,0:T(8,128)S(1)} %hold_covariance.1.c_ref.refs_0_, bf16[128,512]{1,0:T(8,128)(2,1)S(1)} %features.1.refs_0_, bf16[128,512]{1,0:T(8,128)(2,1)S(1)} %collective-permute-done.9.refs_1_, bf16[128,512]{1,0:T(8,128)(2,1)S(1)} %collective-permute-done.11.refs_2_, ...), custom_call_target="tpu_custom_call" | custom-call | flops 2147483648 | bytes 16777216 | tf_op jit(solution)/shard_map/panel_part/pallas_call | solution.py:130
  64.1 5.7 %panel_part.3 = (f32[512,128]{1,0:T(8,128)S(1)}, f32[512,128]{1,0:T(8,128)S(1)}, f32[512,128]{1,0:T(8,128)S(1)}, f32[512,128]{1,0:T(8,128)S(1)}) custom-call(f32[2048,4096]{1,0:T(8,128)S(1)} %hold_covariance.1.c_ref.refs_0_, bf16[128,512]{1,0:T(8,128)(2,1)S(1)} %collective-permute-done.8.refs_0_, bf16[128,512]{1,0:T(8,128)(2,1)S(1)} %collective-permute-done.10.refs_1_, ...), custom_call_target="tpu_custom_call" | custom-call | flops 2147483648 | bytes 16777216 | tf_op jit(solution)/shard_map/panel_part/pallas_call | solution.py:130
  69.9 1.6 collective-permute-start.15
  71.4 1.5 collective-permute-start.16
  73.0 0.5 collective-permute-start.17
  73.4 0.7 collective-permute-start.7
  74.1 5.0 %collective-permute-done.15.refs_1_ = f32[512,128]{1,0:T(8,128)S(1)} collective-permute-done((f32[512,128]{1,0:T(8,128)S(1)}, f32[512,128]{1,0:T(8,128)S(1)}, u32[]{:S(2)}, u32[]{:S(2)}) %collective-permute-start.15) | collective-permute-done | bytes 262176 | tf_op jit(solution)/shard_map/ppermute | solution.py:83
  79.2 7.8 %collective-permute-done.16.refs_2_ = f32[512,128]{1,0:T(8,128)S(1)} collective-permute-done((f32[512,128]{1,0:T(8,128)S(1)}, f32[512,128]{1,0:T(8,128)S(1)}, u32[]{:S(2)}, u32[]{:S(2)}) %collective-permute-start.16) | collective-permute-done | bytes 262176 | tf_op jit(solution)/shard_map/ppermute | solution.py:83
  86.9 1.6 collective-permute-done.17.refs_3_
  88.5 0.4 gram_part.1
  88.9 0.1 collective-permute-start.18
  88.9 1.2 collective-permute-done.18
  90.2 0.1 collective-permute-start.19
  90.3 4.3 %collective-permute-done.19 = f32[136,128]{1,0:T(8,128)S(1)} collective-permute-done((f32[136,128]{1,0:T(8,128)S(1)}, f32[136,128]{1,0:T(8,128)S(1)}, u32[]{:S(2)}, u32[]{:S(2)}) %collective-permute-start.19) | collective-permute-done | bytes 69664 | tf_op jit(solution)/shard_map/ppermute | solution.py:109
  94.6 3.1 %collective-permute-start.20 = (f32[136,128]{1,0:T(8,128)S(1)}, f32[136,128]{1,0:T(8,128)S(1)}, u32[]{:S(2)}, u32[]{:S(2)}) collective-permute-start(f32[136,128]{1,0:T(8,128)S(1)} %add.16), channel_id=1, source_target_pairs={{0,16},{4,20},{8,24},{12,28},{16,0},{20,4},{24,8},{28,12},{1,17},{... | collective-permute-start | bytes 208904 | tf_op jit(solution)/shard_map/ppermute | solution.py:109
  97.7 0.8 collective-permute-start.26
  98.6 1.9 %collective-permute-done.20 = f32[136,128]{1,0:T(8,128)S(1)} collective-permute-done((f32[136,128]{1,0:T(8,128)S(1)}, f32[136,128]{1,0:T(8,128)S(1)}, u32[]{:S(2)}, u32[]{:S(2)}) %collective-permute-start.20) | collective-permute-done | bytes 69664 | tf_op jit(solution)/shard_map/ppermute | solution.py:109
  100.5 6.9 %collective-permute-start.21 = (f32[136,128]{1,0:T(8,128)S(1)}, f32[136,128]{1,0:T(8,128)S(1)}, u32[]{:S(2)}, u32[]{:S(2)}) collective-permute-start(f32[136,128]{1,0:T(8,128)S(1)} %add.17), channel_id=1, source_target_pairs={{0,1},{1,0},{2,3},{3,2},{4,5},{5,4},{6,7},{7,6},{8,9},{9,8},{10,11... | collective-permute-start | bytes 208904 | tf_op jit(solution)/shard_map/ppermute | solution.py:83
  107.4 1.5 collective-permute-start.24
  109.0 0.7 collective-permute-start.29
  109.6 3.9 %collective-permute-start.28 = (bf16[512,128]{1,0:T(8,128)(2,1)S(1)}, bf16[512,128]{1,0:T(8,128)(2,1)S(1)}, u32[]{:S(2)}, u32[]{:S(2)}) collective-permute-start(bf16[512,128]{1,0:T(8,128)(2,1)S(1)} %collective-permute-done.26.refs_8_), channel_id=1, source_target_pairs={{0,16},{4,20},{8,24},{12,28},{16,0},{20,4},{24,8},{28,12},{1,17},{... | collective-permute-start | bytes 393224 | tf_op jit(solution)/shard_map/ppermute | solution.py:88
  113.5 4.3 %collective-permute-start.22 = (f32[136,128]{1,0:T(8,128)S(1)}, f32[136,128]{1,0:T(8,128)S(1)}, u32[]{:S(2)}, u32[]{:S(2)}) collective-permute-start(f32[136,128]{1,0:T(8,128)S(1)} %add.18), channel_id=1, source_target_pairs={{0,2},{1,3},{2,0},{3,1},{4,6},{5,7},{6,4},{7,5},{8,10},{9,11},{10,... | collective-permute-start | bytes 208904 | tf_op jit(solution)/shard_map/ppermute | solution.py:83
  117.9 0.7 collective-permute-start.23
  118.6 5.1 %collective-permute-done.28.refs_10_ = bf16[512,128]{1,0:T(8,128)(2,1)S(1)} collective-permute-done((bf16[512,128]{1,0:T(8,128)(2,1)S(1)}, bf16[512,128]{1,0:T(8,128)(2,1)S(1)}, u32[]{:S(2)}, u32[]{:S(2)}) %collective-permute-start.28) | collective-permute-done | bytes 131104 | tf_op jit(solution)/shard_map/ppermute | solution.py:88
  123.8 0.5 collective-permute-start.32
  124.3 0.1 collective-permute-start.31
  124.4 17.8 %inverse.1 = (f32[128,128]{1,0:T(8,128)S(1)}, f32[8,128]{1,0:T(8,128)S(1)}) custom-call(f32[136,128]{1,0:T(8,128)S(1)} %add.19.gram_ref, f32[1,128]{1,0:T(1,128)S(1)} %bitcast.7), custom_call_target="tpu_custom_call" | custom-call | tf_op jit(solution)/shard_map/inverse/pallas_call | solution.py:130
  142.1 0.1 collective-permute-done.33.refs_15_
  142.2 0.0 copy-start.1
  142.2 10.5 %copy-done.1 = f32[2048,4096]{1,0:T(8,128)S(1)} copy-done((f32[2048,4096]{1,0:T(8,128)S(1)}, f32[2048,4096]{1,0:T(8,128)}, u32[]{:S(2)}) %copy-start.1) | copy-done | bytes 33554456
  152.8 14.2 %update.1 = (f32[2048,4096]{1,0:T(8,128)}, f32[1,2048]{1,0:T(1,128)}) custom-call(f32[2048,4096]{1,0:T(8,128)S(1)} %copy-done.1, f32[128,128]{1,0:T(8,128)S(1)} %get-tuple-element.25.refs_1_, f32[8,128]{1,0:T(8,128)S(1)} %get-tuple-element.26.refs_2_, f32[1,2048]{1,0:T(1,128)S(1)} %bitcast.5, bf16[512,128]{1,0:T(8,128)(2,1)S(1)} %get-tuple-element.27.refs_4_, ...), custom_call_target="tpu_custom_call" | custom-call | tf_op jit(solution)/shard_map/update/pallas_call | solution.py:130
  (36 shorter events, 0.1 us)
Async XLA Ops:
  0.6 8.6 %collective-permute-start.2 = (bf16[32,1024]{1,0:T(8,128)(2,1)}, bf16[32,1024]{1,0:T(8,128)(2,1)S(1)}, u32[]{:S(2)}, u32[]{:S(2)}) collective-permute-start(bf16[32,1024]{1,0:T(8,128)(2,1)} %refs_0_.3), channel_id=1, source_target_pairs={{0,3},{1,2},{2,1},{3,0},{4,7},{5,6},{6,5},{7,4},{8,11},{9,10},{10,... | collective-permute-start | bytes 196616 | tf_op jit(solution)/shard_map/ppermute | solution.py:83
  4.6 4.6 %collective-permute-start.1 = (bf16[32,1024]{1,0:T(8,128)(2,1)}, bf16[32,1024]{1,0:T(8,128)(2,1)S(1)}, u32[]{:S(2)}, u32[]{:S(2)}) collective-permute-start(bf16[32,1024]{1,0:T(8,128)(2,1)} %refs_0_.3), channel_id=1, source_target_pairs={{0,2},{1,3},{2,0},{3,1},{4,6},{5,7},{6,4},{7,5},{8,10},{9,11},{10,... | collective-permute-start | bytes 196616 | tf_op jit(solution)/shard_map/ppermute | solution.py:83
  5.1 4.5 %collective-permute-start = (bf16[32,1024]{1,0:T(8,128)(2,1)}, bf16[32,1024]{1,0:T(8,128)(2,1)S(1)}, u32[]{:S(2)}, u32[]{:S(2)}) collective-permute-start(bf16[32,1024]{1,0:T(8,128)(2,1)} %refs_0_.3), channel_id=1, source_target_pairs={{0,1},{1,0},{2,3},{3,2},{4,5},{5,4},{6,7},{7,6},{8,9},{9,8},{10,11... | collective-permute-start | bytes 196616 | tf_op jit(solution)/shard_map/ppermute | solution.py:83
  5.2 3.4 %copy-start.2 = (bf16[1024,4096]{1,0:T(8,128)(2,1)S(1)}, bf16[1024,4096]{1,0:T(8,128)(2,1)}, u32[]{:S(2)}) copy-start(bf16[1024,4096]{1,0:T(8,128)(2,1)} %in_ref.3) | copy-start | bytes 25165828
  8.6 28.4 %copy-start.6 = (f32[4096]{0:T(1024)S(1)}, f32[4096]{0:T(1024)}, u32[]{:S(2)}) copy-start(f32[4096]{0:T(1024)} %param.8) | copy-start | bytes 49156
  9.6 0.8 copy-start.3
  11.2 2.7 %collective-permute-start.3 = (f32[128,2048]{1,0:T(8,128)S(1)}, f32[128,2048]{1,0:T(8,128)S(1)}, u32[]{:S(2)}, u32[]{:S(2)}) collective-permute-start(f32[128,2048]{1,0:T(8,128)S(1)} %preact_part.2), channel_id=1, source_target_pairs={{0,4},{4,0},{8,12},{12,8},{16,20},{20,16},{24,28},{28,24},{1,5},{5... | collective-permute-start | bytes 3145736 | tf_op jit(solution)/shard_map/ppermute | solution.py:92
  11.3 0.8 copy-start.4
  14.0 13.4 %collective-permute-start.4 = (f32[128,512]{1,0:T(8,128)S(1)}, f32[128,512]{1,0:T(8,128)S(1)}, u32[]{:S(2)}, u32[]{:S(2)}) collective-permute-start(f32[128,512]{1,0:T(8,128)S(1)} %get-tuple-element.17), channel_id=1, source_target_pairs={{0,8},{4,12},{8,0},{12,4},{16,24},{20,28},{24,16},{28,20},{1,9},{5... | collective-permute-start | bytes 786440 | tf_op jit(solution)/shard_map/ppermute | solution.py:88
  15.7 21.3 %collective-permute-start.5 = (f32[128,512]{1,0:T(8,128)S(1)}, f32[128,512]{1,0:T(8,128)S(1)}, u32[]{:S(2)}, u32[]{:S(2)}) collective-permute-start(f32[128,512]{1,0:T(8,128)S(1)} %get-tuple-element.18), channel_id=1, source_target_pairs={{0,16},{4,20},{8,24},{12,28},{16,0},{20,4},{24,8},{28,12},{1,17},{... | collective-permute-start | bytes 786440 | tf_op jit(solution)/shard_map/ppermute | solution.py:88
  18.3 18.7 %collective-permute-start.6 = (f32[128,512]{1,0:T(8,128)S(1)}, f32[128,512]{1,0:T(8,128)S(1)}, u32[]{:S(2)}, u32[]{:S(2)}) collective-permute-start(f32[128,512]{1,0:T(8,128)S(1)} %get-tuple-element.19), channel_id=1, source_target_pairs={{0,24},{4,28},{8,16},{12,20},{16,8},{20,12},{24,0},{28,4},{1,25},{... | collective-permute-start | bytes 786440 | tf_op jit(solution)/shard_map/ppermute | solution.py:88
  37.1 20.2 %collective-permute-start.13 = (bf16[128,512]{1,0:T(8,128)(2,1)S(1)}, bf16[128,512]{1,0:T(8,128)(2,1)S(1)}, u32[]{:S(2)}, u32[]{:S(2)}) collective-permute-start(bf16[128,512]{1,0:T(8,128)(2,1)S(1)} %features.1.refs_0_), channel_id=1, source_target_pairs={{0,24},{4,28},{8,16},{12,20},{16,8},{20,12},{24,0},{28,4},{1,25},{... | collective-permute-start | bytes 393224 | tf_op jit(solution)/shard_map/ppermute | solution.py:88
  39.7 18.2 %collective-permute-start.11 = (bf16[128,512]{1,0:T(8,128)(2,1)S(1)}, bf16[128,512]{1,0:T(8,128)(2,1)S(1)}, u32[]{:S(2)}, u32[]{:S(2)}) collective-permute-start(bf16[128,512]{1,0:T(8,128)(2,1)S(1)} %features.1.refs_0_), channel_id=1, source_target_pairs={{0,16},{4,20},{8,24},{12,28},{16,0},{20,4},{24,8},{28,12},{1,17},{... | collective-permute-start | bytes 393224 | tf_op jit(solution)/shard_map/ppermute | solution.py:88
  46.6 11.4 %collective-permute-start.9 = (bf16[128,512]{1,0:T(8,128)(2,1)S(1)}, bf16[128,512]{1,0:T(8,128)(2,1)S(1)}, u32[]{:S(2)}, u32[]{:S(2)}) collective-permute-start(bf16[128,512]{1,0:T(8,128)(2,1)S(1)} %features.1.refs_0_), channel_id=1, source_target_pairs={{0,8},{4,12},{8,0},{12,4},{16,24},{20,28},{24,16},{28,20},{1,9},{5... | collective-permute-start | bytes 393224 | tf_op jit(solution)/shard_map/ppermute | solution.py:88
  57.2 12.7 %copy-start = (f32[2048,4096]{1,0:T(8,128)}, f32[2048,4096]{1,0:T(8,128)S(1)}, u32[]{:S(2)}) copy-start(f32[2048,4096]{1,0:T(8,128)S(1)} %hold_covariance.1.c_ref.refs_0_) | copy-start | bytes 100663296
  57.2 31.3 %copy-start.5 = (f32[2048]{0:T(1024)S(1)}, f32[2048]{0:T(1024)}, u32[]{:S(2)}) copy-start(f32[2048]{0:T(1024)} %param.10) | copy-start | bytes 24580
  57.3 67.1 %copy-start.7 = (f32[128]{0:T(128)S(1)}, f32[128]{0:T(128)}, u32[]{:S(2)}) copy-start(f32[128]{0:T(128)} %param.11) | copy-start | bytes 1540
  57.3 6.8 %collective-permute-start.8 = (bf16[128,512]{1,0:T(8,128)(2,1)S(1)}, bf16[128,512]{1,0:T(8,128)(2,1)S(1)}, u32[]{:S(2)}, u32[]{:S(2)}) collective-permute-start(bf16[128,512]{1,0:T(8,128)(2,1)S(1)} %features.1.refs_0_), channel_id=1, source_target_pairs={{0,4},{4,0},{8,12},{12,8},{16,20},{20,16},{24,28},{28,24},{1,5},{5... | collective-permute-start | bytes 393224 | tf_op jit(solution)/shard_map/ppermute | solution.py:92
  57.4 6.7 %collective-permute-start.14 = (bf16[128,512]{1,0:T(8,128)(2,1)S(1)}, bf16[128,512]{1,0:T(8,128)(2,1)S(1)}, u32[]{:S(2)}, u32[]{:S(2)}) collective-permute-start(bf16[128,512]{1,0:T(8,128)(2,1)S(1)} %collective-permute-done.13.refs_3_), channel_id=1, source_target_pairs={{0,4},{4,0},{8,12},{12,8},{16,20},{20,16},{24,28},{28,24},{1,5},{5... | collective-permute-start | bytes 393224 | tf_op jit(solution)/shard_map/ppermute | solution.py:92
  57.9 6.3 %collective-permute-start.12 = (bf16[128,512]{1,0:T(8,128)(2,1)S(1)}, bf16[128,512]{1,0:T(8,128)(2,1)S(1)}, u32[]{:S(2)}, u32[]{:S(2)}) collective-permute-start(bf16[128,512]{1,0:T(8,128)(2,1)S(1)} %collective-permute-done.11.refs_2_), channel_id=1, source_target_pairs={{0,4},{4,0},{8,12},{12,8},{16,20},{20,16},{24,28},{28,24},{1,5},{5... | collective-permute-start | bytes 393224 | tf_op jit(solution)/shard_map/ppermute | solution.py:92
  57.9 6.2 %collective-permute-start.10 = (bf16[128,512]{1,0:T(8,128)(2,1)S(1)}, bf16[128,512]{1,0:T(8,128)(2,1)S(1)}, u32[]{:S(2)}, u32[]{:S(2)}) collective-permute-start(bf16[128,512]{1,0:T(8,128)(2,1)S(1)} %collective-permute-done.9.refs_1_), channel_id=1, source_target_pairs={{0,4},{4,0},{8,12},{12,8},{16,20},{20,16},{24,28},{28,24},{1,5},{5... | collective-permute-start | bytes 393224 | tf_op jit(solution)/shard_map/ppermute | solution.py:92
  69.9 9.3 %collective-permute-start.15 = (f32[512,128]{1,0:T(8,128)S(1)}, f32[512,128]{1,0:T(8,128)S(1)}, u32[]{:S(2)}, u32[]{:S(2)}) collective-permute-start(f32[512,128]{1,0:T(8,128)S(1)} %get-tuple-element.21), channel_id=1, source_target_pairs={{0,1},{1,0},{2,3},{3,2},{4,5},{5,4},{6,7},{7,6},{8,9},{9,8},{10,11... | collective-permute-start | bytes 786440 | tf_op jit(solution)/shard_map/ppermute | solution.py:83
  71.4 15.5 %collective-permute-start.16 = (f32[512,128]{1,0:T(8,128)S(1)}, f32[512,128]{1,0:T(8,128)S(1)}, u32[]{:S(2)}, u32[]{:S(2)}) collective-permute-start(f32[512,128]{1,0:T(8,128)S(1)} %get-tuple-element.22), channel_id=1, source_target_pairs={{0,2},{1,3},{2,0},{3,1},{4,6},{5,7},{6,4},{7,5},{8,10},{9,11},{10,... | collective-permute-start | bytes 786440 | tf_op jit(solution)/shard_map/ppermute | solution.py:83
  73.0 15.5 %collective-permute-start.17 = (f32[512,128]{1,0:T(8,128)S(1)}, f32[512,128]{1,0:T(8,128)S(1)}, u32[]{:S(2)}, u32[]{:S(2)}) collective-permute-start(f32[512,128]{1,0:T(8,128)S(1)} %get-tuple-element.23), channel_id=1, source_target_pairs={{0,3},{1,2},{2,1},{3,0},{4,7},{5,6},{6,5},{7,4},{8,11},{9,10},{10,... | collective-permute-start | bytes 786440 | tf_op jit(solution)/shard_map/ppermute | solution.py:83
  73.4 0.7 collective-permute-start.7
  88.9 1.3 collective-permute-start.18
  90.2 4.4 %collective-permute-start.19 = (f32[136,128]{1,0:T(8,128)S(1)}, f32[136,128]{1,0:T(8,128)S(1)}, u32[]{:S(2)}, u32[]{:S(2)}) collective-permute-start(f32[136,128]{1,0:T(8,128)S(1)} %add.15), channel_id=1, source_target_pairs={{0,8},{4,12},{8,0},{12,4},{16,24},{20,28},{24,16},{28,20},{1,9},{5... | collective-permute-start | bytes 208904 | tf_op jit(solution)/shard_map/ppermute | solution.py:109
  94.6 5.9 %collective-permute-start.20 = (f32[136,128]{1,0:T(8,128)S(1)}, f32[136,128]{1,0:T(8,128)S(1)}, u32[]{:S(2)}, u32[]{:S(2)}) collective-permute-start(f32[136,128]{1,0:T(8,128)S(1)} %add.16), channel_id=1, source_target_pairs={{0,16},{4,20},{8,24},{12,28},{16,0},{20,4},{24,8},{28,12},{1,17},{... | collective-permute-start | bytes 208904 | tf_op jit(solution)/shard_map/ppermute | solution.py:109
  97.7 11.2 %collective-permute-start.26 = (bf16[512,128]{1,0:T(8,128)(2,1)S(1)}, bf16[512,128]{1,0:T(8,128)(2,1)S(1)}, u32[]{:S(2)}, u32[]{:S(2)}) collective-permute-start(bf16[512,128]{1,0:T(8,128)(2,1)S(1)} %get-tuple-element.27.refs_4_), channel_id=1, source_target_pairs={{0,0},{1,8},{2,16},{3,24},{4,4},{5,12},{6,20},{7,28},{8,1},{9,9},{... | collective-permute-start | bytes 393224 | tf_op jit(solution)/shard_map/ppermute | solution.py:103
  100.5 13.0 %collective-permute-start.21 = (f32[136,128]{1,0:T(8,128)S(1)}, f32[136,128]{1,0:T(8,128)S(1)}, u32[]{:S(2)}, u32[]{:S(2)}) collective-permute-start(f32[136,128]{1,0:T(8,128)S(1)} %add.17), channel_id=1, source_target_pairs={{0,1},{1,0},{2,3},{3,2},{4,5},{5,4},{6,7},{7,6},{8,9},{9,8},{10,11... | collective-permute-start | bytes 208904 | tf_op jit(solution)/shard_map/ppermute | solution.py:83
  107.4 6.1 %collective-permute-start.25 = (bf16[512,128]{1,0:T(8,128)(2,1)S(1)}, bf16[512,128]{1,0:T(8,128)(2,1)S(1)}, u32[]{:S(2)}, u32[]{:S(2)}) collective-permute-start(bf16[512,128]{1,0:T(8,128)(2,1)S(1)} %get-tuple-element.27.refs_4_), channel_id=1, source_target_pairs={{0,3},{1,2},{2,1},{3,0},{4,7},{5,6},{6,5},{7,4},{8,11},{9,10},{10,... | collective-permute-start | bytes 393224 | tf_op jit(solution)/shard_map/ppermute | solution.py:83
  107.4 10.4 %collective-permute-start.24 = (bf16[512,128]{1,0:T(8,128)(2,1)S(1)}, bf16[512,128]{1,0:T(8,128)(2,1)S(1)}, u32[]{:S(2)}, u32[]{:S(2)}) collective-permute-start(bf16[512,128]{1,0:T(8,128)(2,1)S(1)} %get-tuple-element.27.refs_4_), channel_id=1, source_target_pairs={{0,2},{1,3},{2,0},{3,1},{4,6},{5,7},{6,4},{7,5},{8,10},{9,11},{10,... | collective-permute-start | bytes 393224 | tf_op jit(solution)/shard_map/ppermute | solution.py:83
  109.0 9.7 %collective-permute-start.29 = (bf16[512,128]{1,0:T(8,128)(2,1)S(1)}, bf16[512,128]{1,0:T(8,128)(2,1)S(1)}, u32[]{:S(2)}, u32[]{:S(2)}) collective-permute-start(bf16[512,128]{1,0:T(8,128)(2,1)S(1)} %collective-permute-done.26.refs_8_), channel_id=1, source_target_pairs={{0,24},{4,28},{8,16},{12,20},{16,8},{20,12},{24,0},{28,4},{1,25},{... | collective-permute-start | bytes 393224 | tf_op jit(solution)/shard_map/ppermute | solution.py:88
  109.6 14.1 %collective-permute-start.28 = (bf16[512,128]{1,0:T(8,128)(2,1)S(1)}, bf16[512,128]{1,0:T(8,128)(2,1)S(1)}, u32[]{:S(2)}, u32[]{:S(2)}) collective-permute-start(bf16[512,128]{1,0:T(8,128)(2,1)S(1)} %collective-permute-done.26.refs_8_), channel_id=1, source_target_pairs={{0,16},{4,20},{8,24},{12,28},{16,0},{20,4},{24,8},{28,12},{1,17},{... | collective-permute-start | bytes 393224 | tf_op jit(solution)/shard_map/ppermute | solution.py:88
  113.5 10.3 %collective-permute-start.27 = (bf16[512,128]{1,0:T(8,128)(2,1)S(1)}, bf16[512,128]{1,0:T(8,128)(2,1)S(1)}, u32[]{:S(2)}, u32[]{:S(2)}) collective-permute-start(bf16[512,128]{1,0:T(8,128)(2,1)S(1)} %collective-permute-done.26.refs_8_), channel_id=1, source_target_pairs={{0,8},{4,12},{8,0},{12,4},{16,24},{20,28},{24,16},{28,20},{1,9},{5... | collective-permute-start | bytes 393224 | tf_op jit(solution)/shard_map/ppermute | solution.py:88
  113.5 10.8 %collective-permute-start.22 = (f32[136,128]{1,0:T(8,128)S(1)}, f32[136,128]{1,0:T(8,128)S(1)}, u32[]{:S(2)}, u32[]{:S(2)}) collective-permute-start(f32[136,128]{1,0:T(8,128)S(1)} %add.18), channel_id=1, source_target_pairs={{0,2},{1,3},{2,0},{3,1},{4,6},{5,7},{6,4},{7,5},{8,10},{9,11},{10,... | collective-permute-start | bytes 208904 | tf_op jit(solution)/shard_map/ppermute | solution.py:83
  117.9 24.3 %collective-permute-start.23 = (bf16[512,128]{1,0:T(8,128)(2,1)S(1)}, bf16[512,128]{1,0:T(8,128)(2,1)S(1)}, u32[]{:S(2)}, u32[]{:S(2)}) collective-permute-start(bf16[512,128]{1,0:T(8,128)(2,1)S(1)} %get-tuple-element.27.refs_4_), channel_id=1, source_target_pairs={{0,1},{1,0},{2,3},{3,2},{4,5},{5,4},{6,7},{7,6},{8,9},{9,8},{10,11... | collective-permute-start | bytes 393224 | tf_op jit(solution)/shard_map/ppermute | solution.py:83
  118.6 23.5 %collective-permute-start.30 = (bf16[512,128]{1,0:T(8,128)(2,1)S(1)}, bf16[512,128]{1,0:T(8,128)(2,1)S(1)}, u32[]{:S(2)}, u32[]{:S(2)}) collective-permute-start(bf16[512,128]{1,0:T(8,128)(2,1)S(1)} %collective-permute-done.26.refs_8_), channel_id=1, source_target_pairs={{0,4},{4,0},{8,12},{12,8},{16,20},{20,16},{24,28},{28,24},{1,5},{5... | collective-permute-start | bytes 393224 | tf_op jit(solution)/shard_map/ppermute | solution.py:92
  123.8 18.4 %collective-permute-start.33 = (bf16[512,128]{1,0:T(8,128)(2,1)S(1)}, bf16[512,128]{1,0:T(8,128)(2,1)S(1)}, u32[]{:S(2)}, u32[]{:S(2)}) collective-permute-start(bf16[512,128]{1,0:T(8,128)(2,1)S(1)} %collective-permute-done.29.refs_11_), channel_id=1, source_target_pairs={{0,4},{4,0},{8,12},{12,8},{16,20},{20,16},{24,28},{28,24},{1,5},{5... | collective-permute-start | bytes 393224 | tf_op jit(solution)/shard_map/ppermute | solution.py:92
  123.8 18.4 %collective-permute-start.32 = (bf16[512,128]{1,0:T(8,128)(2,1)S(1)}, bf16[512,128]{1,0:T(8,128)(2,1)S(1)}, u32[]{:S(2)}, u32[]{:S(2)}) collective-permute-start(bf16[512,128]{1,0:T(8,128)(2,1)S(1)} %collective-permute-done.28.refs_10_), channel_id=1, source_target_pairs={{0,4},{4,0},{8,12},{12,8},{16,20},{20,16},{24,28},{28,24},{1,5},{5... | collective-permute-start | bytes 393224 | tf_op jit(solution)/shard_map/ppermute | solution.py:92
  124.3 17.9 %collective-permute-start.31 = (bf16[512,128]{1,0:T(8,128)(2,1)S(1)}, bf16[512,128]{1,0:T(8,128)(2,1)S(1)}, u32[]{:S(2)}, u32[]{:S(2)}) collective-permute-start(bf16[512,128]{1,0:T(8,128)(2,1)S(1)} %collective-permute-done.27.refs_9_), channel_id=1, source_target_pairs={{0,4},{4,0},{8,12},{12,8},{16,20},{20,16},{24,28},{28,24},{1,5},{5... | collective-permute-start | bytes 393224 | tf_op jit(solution)/shard_map/ppermute | solution.py:92
  142.2 10.5 %copy-start.1 = (f32[2048,4096]{1,0:T(8,128)S(1)}, f32[2048,4096]{1,0:T(8,128)}, u32[]{:S(2)}) copy-start(f32[2048,4096]{1,0:T(8,128)} %copy-done) | copy-start | bytes 100663296

commit v2 on v1

--- a/solution.py
+++ b/solution.py
@@ -103,18 +103,6 @@
     return lax.ppermute(x, ("row", "col"), pairs)
 
 
-def total(x):
-    step = 1
-    while step < lax.axis_size("row"):
-        x = x + lax.ppermute(x, "row", [(i, i ^ step) for i in range(lax.axis_size("row"))])
-        step *= 2
-    step = 1
-    while step < lax.axis_size("col"):
-        x = x + swap_col(x, step)
-        step *= 2
-    return x
-
-
 def places():
     cols = lax.axis_size("col")
     inner = lax.axis_size("row") // cols
@@ -126,7 +114,7 @@
     return pl.ds(pl.multiple_of(index * size, size), size)
 
 
-def call(kernel, name, limit, operands, in_specs, out_specs, out_shape, scratch_shapes=(), flops=0, size=0):
+def call(kernel, name, operands, in_specs, out_specs, out_shape, scratch_shapes=(), flops=0, size=0):
     return pl.pallas_call(
         kernel,
         in_specs=in_specs,
@@ -134,26 +122,27 @@
         out_shape=out_shape,
         scratch_shapes=scratch_shapes,
         cost_estimate=pl.CostEstimate(flops=flops, bytes_accessed=size, transcendentals=0),
-        compiler_params=pltpu.CompilerParams(vmem_limit_bytes=limit * MIB),
+        compiler_params=pltpu.CompilerParams(vmem_limit_bytes=14 * MIB),
         name=name,
     )(*operands)
 
 
-def hold_kernel(in_ref, out_ref, sem):
+def hold_kernel(in_ref, *refs):
+    out_ref, token_ref, sem = refs[-3:]
     copy = pltpu.make_async_copy(in_ref, out_ref, sem)
     copy.start()
+    token_ref[...] = jnp.zeros_like(token_ref)
     copy.wait()
 
 
-def hold(x, name):
+def hold(x, name, *after):
     return call(
         hold_kernel,
         name,
-        1,
-        (x,),
-        [pl.BlockSpec(memory_space=pl.ANY)],
-        pl.BlockSpec(memory_space=pltpu.VMEM),
-        pltpu.VMEM(x.shape, x.dtype),
+        (x, *after),
+        [pl.BlockSpec(memory_space=pl.ANY)] * (1 + len(after)),
+        vmem(2),
+        [pltpu.VMEM(x.shape, x.dtype), jax.ShapeDtypeStruct((8, 128), F32)],
         [pltpu.SemaphoreType.DMA],
         size=x.size * x.dtype.itemsize,
     )
@@ -183,7 +172,6 @@
     return call(
         functools.partial(preact_kernel, step),
         "preact_part",
-        8,
         (*blocks, in_vmem(weight)),
         vmem(n + 1),
         vmem(1)[0],
@@ -207,25 +195,24 @@
     rows, width = sums[0].shape
     shape = jax.ShapeDtypeStruct((rows, width // count), F32)
     return call(
-        functools.partial(scatter_kernel, len(sums)), "scatter", 8, sums, vmem(len(sums)), vmem(count), [shape] * count, size=8 * rows * width
-    )
-
-
-def feature_kernel(bias_ref, *refs):
+        functools.partial(scatter_kernel, len(sums)), "scatter", sums, vmem(len(sums)), vmem(count), [shape] * count, size=8 * rows * width
+    )
+
+
+def feature_kernel(_, bias_ref, *refs):
     *parts, out_ref = refs
     outer, inner_index, _, _, cols = places()
     here = span(inner_index * cols + outer, out_ref.shape[1])
     out_ref[...] = jnp.tanh(sum(p[...] for p in parts) + bias_ref[:, here]).astype(BF16)
 
 
-def features_of(bias, parts):
+def features_of(token, bias, parts):
     rows, width = parts[0].shape
     return call(
         feature_kernel,
         "features",
-        8,
-        (bias.reshape(1, bias.shape[0]), *parts),
-        vmem(1 + len(parts)),
+        (token, bias.reshape(1, bias.shape[0]), *parts),
+        vmem(2 + len(parts)),
         vmem(1)[0],
         jax.ShapeDtypeStruct((rows, width), BF16),
         size=16 * rows * width,
@@ -240,7 +227,7 @@
     outs = rest[-cols:] if last else rest[-1:]
     width = shards[0].shape[1]
     quarter = c_ref.shape[0] // cols
-    rows = min(256, quarter)
+    rows = min(512, quarter)
     per = quarter // rows
     for q in range(cols):
         block = (col ^ q) if last else q
@@ -273,7 +260,6 @@
     outs = call(
         functools.partial(panel_kernel, tuple(steps), send is not None),
         "panel_part",
-        12,
         operands,
         vmem(len(operands)),
         vmem(len(shape)),
@@ -285,7 +271,7 @@
     return outs[0] if send is None else outs
 
 
-def gram_kernel(phi_ref, mean_ref, *refs):
+def gram_kernel(_, phi_ref, mean_ref, *refs):
     *parts, panel_ref, gram_ref = refs
     _, _, col, _, _ = places()
     panel = parts[0][...]
@@ -299,60 +285,120 @@
     gram_ref[batch:, :] = sum(dot(piece, phi, NT) for piece in split3(mean))
 
 
-def gram_part(phi, mean, parts):
+def gram_part(held, phi, mean, parts):
     rows, batch = parts[0].shape
     return call(
         gram_kernel,
         "gram_part",
-        8,
-        (phi, mean.reshape(1, mean.shape[0]), *parts),
-        vmem(2 + len(parts)),
+        (in_vmem(held), phi, mean.reshape(1, mean.shape[0]), *parts),
+        vmem(3 + len(parts)),
         vmem(2),
         [jax.ShapeDtypeStruct((rows, batch), BF16), jax.ShapeDtypeStruct((batch + 8, batch), F32)],
     )
 
 
-def inverse_kernel(gram_ref, rewards_ref, inverse_ref, coeffs_ref, held):
+def join_kernel(count, _, x_ref, y_ref, *refs):
+    out_ref = refs[count]
+    out_ref[...] = x_ref[...] + y_ref[...]
+    for source, target in zip(refs[:count], refs[count + 1 :]):
+        target[...] = source[...]
+
+
+def join(held, x, y, *others):
+    outs = call(
+        functools.partial(join_kernel, len(others)),
+        "join",
+        (in_vmem(held), x, y, *others),
+        vmem(3 + len(others)),
+        vmem(1 + len(others)),
+        [jax.ShapeDtypeStruct(a.shape, a.dtype) for a in (x, *others)],
+    )
+    return outs if others else outs[0]
+
+
+def total_row(held, x, *others):
+    step, size = 1, lax.axis_size("row")
+    while step < size:
+        y = lax.ppermute(x, "row", [(i, i ^ step) for i in range(size)])
+        step *= 2
+        if step == size and others:
+            return join(held, x, y, *others)
+        x = join(held, x, y)
+    return x
+
+
+def total_col(held, x, *others):
+    step, size = 1, lax.axis_size("col")
+    while step < size:
+        y = swap_col(x, step)
+        step *= 2
+        if step == size and others:
+            return join(held, x, y, *others)
+        x = join(held, x, y)
+    return x
+
+
+def inverse_kernel(_, gram_ref, rewards_ref, inverse_ref, coeffs_ref):
     n = rewards_ref.shape[1]
-    highest = lax.Precision.HIGHEST
     lane = lax.broadcasted_iota(jnp.int32, (8, n), 1)
     sub = lax.broadcasted_iota(jnp.int32, (8, n), 0)
-    i = lax.broadcasted_iota(jnp.int32, (n, n), 0)
-    j = lax.broadcasted_iota(jnp.int32, (n, n), 1)
-    held[...] = gram_ref[:n, :] + jnp.where(i == j, 1.0, 0.0)
-    for first in range(0, n, 8):
-        block = held[first : first + 8, :]
+
+    def row(x, t):
+        return jnp.broadcast_to(x[t : t + 1, :], (8, n))
+
+    def column(x, t):
+        return jnp.broadcast_to(x[:, t : t + 1], (8, n))
+
+    groups = [
+        gram_ref[first : first + 8, :] + jnp.where(lane == sub + first, 1.0, 0.0) for first in range(0, n, 8)
+    ]
+    for g in range(n // 8):
+        first = 8 * g
         inside = (lane >= first) & (lane < first + 8)
         eye = jnp.where(lane == sub + first, 1.0, 0.0)
-        x, y = block, eye
+        columns = [column(groups[g], first + t) for t in range(8)]
+        swept = jnp.where(inside, eye, groups[g])
         for t in range(8):
-            column = jnp.broadcast_to(x[:, first + t : first + t + 1], (8, n))
-            pivot = 1.0 / jnp.broadcast_to(x[t : t + 1, first + t : first + t + 1], (8, n))
-            row_x = jnp.broadcast_to(x[t : t + 1, :], (8, n)) * pivot
-            row_y = jnp.broadcast_to(y[t : t + 1, :], (8, n)) * pivot
-            x = jnp.where(sub == t, row_x, x - column * row_x)
-            y = jnp.where(sub == t, row_y, y - column * row_y)
-        spread = jnp.where(inside, -y, x)
-        rest = jnp.where((j >= first) & (j < first + 8), 0.0, held[...])
-        held[...] = rest - lax.dot_general(block, spread, TN, precision=highest, preferred_element_type=F32)
-        held[first : first + 8, :] = spread
-    inverse = -held[...]
-    inverse_ref[...] = inverse
+            scale = 1.0 / row(columns[t], t)
+            factor = columns[t]
+
+            def eliminate(x):
+                mine = row(x, t) * scale
+                return jnp.where(sub == t, mine, x - factor * mine)
+
+            swept = eliminate(swept)
+            for u in range(t + 1, 8):
+                columns[u] = eliminate(columns[u])
+        swept = jnp.where(inside, -swept, swept)
+        rows = [row(swept, t) for t in range(8)]
+        order = [h % (n // 8) for h in range(g + 1, g + n // 8)]
+        for h in order:
+            x = jnp.where(inside, 0.0, groups[h])
+            for t in range(8):
+                x = x - column(groups[h], first + t) * rows[t]
+            groups[h] = x
+        groups[g] = swept
+    for g in range(n // 8):
+        inverse_ref[8 * g : 8 * g + 8, :] = -groups[g]
     gap = jnp.broadcast_to(rewards_ref[...] - gram_ref[n : n + 1, :], (8, n))
-    coeffs_ref[...] = lax.dot_general(gap, inverse, (((1,), (0,)), ((), ())), precision=highest, preferred_element_type=F32)
-
-
-def inverse_and_coeffs(gram, rewards):
+    coeffs_ref[...] = lax.dot_general(
+        gap,
+        inverse_ref[...],
+        (((1,), (0,)), ((), ())),
+        precision=lax.Precision.HIGHEST,
+        preferred_element_type=F32,
+    )
+
+
+def inverse_and_coeffs(held, gram, rewards):
     n = rewards.shape[0]
     return call(
         inverse_kernel,
         "inverse",
-        8,
-        (gram, rewards.reshape(1, n)),
-        vmem(2),
+        (in_vmem(held), gram, rewards.reshape(1, n)),
+        vmem(3),
         vmem(2),
         [jax.ShapeDtypeStruct((n, n), F32), jax.ShapeDtypeStruct((8, n), F32)],
-        [pltpu.VMEM((n, n), F32)],
     )
 
 
@@ -380,13 +426,13 @@
 
     def body(step, block):
         here = span(step.index[0], tile)
-        block[...] = c_ref[here, :] - dot(gain[here, :], other[...], NT)
+        block[...] = c_ref[:, here] - dot(gain[...], other[here, :], NT)
 
     pltpu.emit_pipeline(
         body,
-        grid=(c_ref.shape[0] // tile,),
+        grid=(c_ref.shape[1] // tile,),
         in_specs=[],
-        out_specs=[pl.BlockSpec((tile, c_ref.shape[1]), lambda i: (i, 0))],
+        out_specs=[pl.BlockSpec((c_ref.shape[0], tile), lambda i: (0, i))],
         _explicit_indices=True,
     )(out_ref)
 
@@ -395,9 +441,8 @@
     rows, cols = covariance.shape
     batch = inverse.shape[0]
     return call(
-        functools.partial(update_kernel, len(near), len(far), min(256, rows)),
+        functools.partial(update_kernel, len(near), len(far), min(256, cols)),
         "update",
-        20,
         (in_vmem(covariance), inverse, coeffs, mean.reshape(1, rows), *near, *far),
         vmem(4 + len(near) + len(far)),
         [pl.BlockSpec(memory_space=pl.ANY), vmem(1)[0]],
@@ -419,34 +464,34 @@
         return plain(context, weight, feature_bias, covariance, prior_mean, rewards)
 
     blocks = [context] + [swap_col(context, s) for s in range(1, cols)]
-    w_held = hold(weight, "hold_weight")
+    w_held, _ = hold(weight, "hold_weight")
     sums = []
     for k in range(inner - 1, -1, -1):
         piece = preact_part(k, blocks, w_held, part)
         sums.append(swap_inner(piece, k) if k else piece)
     pieces = scatter(sums, cols)
     summed = [pieces[0]] + [swap_outer(pieces[s], s) for s in range(1, cols)]
-    features = features_of(feature_bias, summed)
-
-    held = hold(covariance, "hold_covariance")
+    held, token = hold(covariance, "hold_covariance", pieces[0])
+    features = features_of(token, feature_bias, summed)
+
     shards = [features] + [swap_outer(features, s) for s in range(1, cols)]
-    panel = panel_part(held, shards, [(s, 0) for s in range(cols)])
+    panel = panel_part(held, shards[:1], [(0, 0)])
+    panel = panel_part(held, shards[1:], [(s, 0) for s in range(1, cols)], panel)
     for k in range(1, inner):
         others = [swap_inner(s, k) for s in shards]
-        panel = panel_part(
-            held, others, [(s, k) for s in range(cols)], panel, F32 if k == inner - 1 else None
-        )
+        panel = panel_part(held, others, [(s, k) for s in range(cols)], panel, F32 if k == inner - 1 else None)
 
     far_features = transpose(features)
     parts = [panel[0]] + [swap_col(panel[s], s) for s in range(1, cols)]
-    own_panel, gram = gram_part(far_features, prior_mean, parts)
+    own_panel, gram = gram_part(held, far_features, prior_mean, parts)
+    gram, turned = total_row(held, gram, transpose(own_panel))
+    far = [turned] + [swap_outer(turned, s) for s in range(1, cols)]
+    gram, own_panel = total_col(held, gram, own_panel)
     near = [own_panel] + [swap_col(own_panel, s) for s in range(1, cols)]
-    turned = transpose(own_panel)
-    far = [turned] + [swap_outer(turned, s) for s in range(1, cols)]
     for k in range(1, inner):
         far += [swap_inner(f, k) for f in far[:cols]]
 
-    inverse, coeffs = inverse_and_coeffs(total(gram), rewards)
+    inverse, coeffs = inverse_and_coeffs(held, gram, rewards)
     new_cov, new_mean = update(held, inverse, coeffs, prior_mean, near, far)
     return new_cov, new_mean.reshape(rows)
 

time: 167 us -> 144 us (0.86)
  starting transfers between devices: 46.8 us -> 33.3 us
  Pallas kernels: 56.6 us -> 44.1 us
  local copies, waits for them, and re-layouts: 15.6 us -> 27.3 us
  waiting for transfers between devices: 47 us -> 38 us
    ppermute x9, waiting for transfers between devices: 23.7 us -> 7.65 us  [swap_outer(): return lax.ppermute(x, 'row', [(i, i ^ step * inner) for i in range(n)])]
    pallas_call x11 -> x17, Pallas kernels: 56.6 us -> 44.1 us  [call(): pl.pallas_call(kernel, in_specs=in_specs, out_specs=out_specs, out_shape=...]
    unnamed x16, local copies, waits for them, and re-layouts: 15.6 us -> 27.3 us
    ppermute x9, starting transfers between devices: 18.5 us -> 10.2 us  [swap_outer(): return lax.ppermute(x, 'row', [(i, i ^ step * inner) for i in range(n)])]
    ppermute x11, starting transfers between devices: 21.7 us -> 15.4 us  [swap_col(): return lax.ppermute(x, 'col', [(i, i ^ step) for i in range(n)])]
    ppermute x3, waiting for transfers between devices: 7.43 us -> 13.3 us  [total_row(): y = lax.ppermute(x, 'row', [(i, i ^ step) for i in range(size)])]
  transfers between devices with their start and end apart: 34 -> 34, of which waited for: 11 -> 11; matrix products, arithmetic and copies ran while one was open for 0% -> 0% of each run, Pallas kernels for 21% -> 15%
where the time goes in v2:
time: 144 us
  Pallas kernels  44.1 us (31%)
  waiting for transfers between devices  38 us (26%)
  starting transfers between devices  33.3 us (23%)
  local copies, waits for them, and re-layouts  27.3 us (19%)
    pallas_call x17, Pallas kernels, call(): pl.pallas_call(kernel, in_specs=in_specs, out_specs=out_specs, out_shape=...  44.1 us
    unnamed x16, local copies, waits for them, and re-layouts  27.3 us
    ppermute x11, waiting for transfers between devices, swap_col(): return lax.ppermute(x, 'col', [(i, i ^ step) for i in range(n)])  16 us
    ppermute x11, starting transfers between devices, swap_col(): return lax.ppermute(x, 'col', [(i, i ^ step) for i in range(n)])  15.4 us
    ppermute x3, waiting for transfers between devices, total_row(): y = lax.ppermute(x, 'row', [(i, i ^ step) for i in range(size)])  13.3 us
    ppermute x9, starting transfers between devices, swap_outer(): return lax.ppermute(x, 'row', [(i, i ^ step * inner) for i in range(n)])  10.2 us
    ppermute x9, waiting for transfers between devices, swap_outer(): return lax.ppermute(x, 'row', [(i, i ^ step * inner) for i in range(n)])  7.65 us
    ppermute x3, starting transfers between devices, total_row(): y = lax.ppermute(x, 'row', [(i, i ^ step) for i in range(size)])  4.52 us
  transfers between devices with their start and end apart: 34, of which 11 were waited for; matrix products, arithmetic and copies ran while one was open for 0% of the time, Pallas kernels for 15%

profile of v2, /device:TPU:0, one launch (start us, length us, event | category | flops | bytes accessed | tf_op | source)
XLA Modules:
  0.0 143.6 jit_solution(6073400168405669511)
XLA Ops:
  0.6 4.0 %collective-permute-start.2 = (bf16[32,1024]{1,0:T(8,128)(2,1)}, bf16[32,1024]{1,0:T(8,128)(2,1)S(1)}, u32[]{:S(2)}, u32[]{:S(2)}) collective-permute-start(bf16[32,1024]{1,0:T(8,128)(2,1)} %refs_0_.3), channel_id=1, source_target_pairs={{0,3},{1,2},{2,1},{3,0},{4,7},{5,6},{6,5},{7,4},{8,11},{9,10},{10,... | collective-permute-start | bytes 196616 | tf_op jit(solution)/shard_map/ppermute | solution.py:83
  4.6 0.5 collective-permute-start.1
  5.1 0.1 collective-permute-start
  5.2 3.4 %copy-done.2 = bf16[1024,4096]{1,0:T(8,128)(2,1)S(1)} copy-done((bf16[1024,4096]{1,0:T(8,128)(2,1)S(1)}, bf16[1024,4096]{1,0:T(8,128)(2,1)}, u32[]{:S(2)}) %copy-start.2) | copy-done | bytes 8388632
  8.6 1.2 hold_weight.1
  9.8 0.0 collective-permute-done.refs_1_
  9.8 0.0 copy-start.3
  9.8 0.8 copy-done.3
  10.7 0.8 preact_part.2
  11.4 0.1 collective-permute-start.3
  11.5 0.0 copy-start.4
  11.5 0.8 copy-done.4
  12.4 0.8 preact_part.3.refs_1_
  13.1 1.0 collective-permute-done.3.refs_0_
  14.2 0.1 scatter.1
  14.3 2.0 %collective-permute-start.4 = (f32[128,512]{1,0:T(8,128)S(1)}, f32[128,512]{1,0:T(8,128)S(1)}, u32[]{:S(2)}, u32[]{:S(2)}) collective-permute-start(f32[128,512]{1,0:T(8,128)S(1)} %get-tuple-element.27), channel_id=1, source_target_pairs={{0,8},{4,12},{8,0},{12,4},{16,24},{20,28},{24,16},{28,20},{1,9},{5... | collective-permute-start | bytes 786440 | tf_op jit(solution)/shard_map/ppermute | solution.py:88
  16.3 2.6 %collective-permute-start.5 = (f32[128,512]{1,0:T(8,128)S(1)}, f32[128,512]{1,0:T(8,128)S(1)}, u32[]{:S(2)}, u32[]{:S(2)}) collective-permute-start(f32[128,512]{1,0:T(8,128)S(1)} %get-tuple-element.28), channel_id=1, source_target_pairs={{0,16},{4,20},{8,24},{12,28},{16,0},{20,4},{24,8},{28,12},{1,17},{... | collective-permute-start | bytes 786440 | tf_op jit(solution)/shard_map/ppermute | solution.py:88
  18.9 10.6 %hold_covariance.1 = (f32[2048,4096]{1,0:T(8,128)S(1)}, f32[8,128]{1,0:T(8,128)S(1)}) custom-call(f32[2048,4096]{1,0:T(8,128)} %in_ref.3, f32[128,512]{1,0:T(8,128)S(1)} %get-tuple-element.24.refs_0_), custom_call_target="tpu_custom_call" | custom-call | bytes 33554432 | tf_op jit(solution)/shard_map/hold_covariance/pallas_call | solution.py:118
  29.5 0.0 copy-start
  29.5 11.7 %copy-done = f32[2048,4096]{1,0:T(8,128)} copy-done((f32[2048,4096]{1,0:T(8,128)}, f32[2048,4096]{1,0:T(8,128)S(1)}, u32[]{:S(2)}) %copy-start) | copy-done | bytes 33554456
  41.1 0.0 collective-permute-done.4.refs_1_
  41.2 0.1 features.1.refs_0_
  41.3 3.9 %collective-permute-start.13 = (bf16[128,512]{1,0:T(8,128)(2,1)S(1)}, bf16[128,512]{1,0:T(8,128)(2,1)S(1)}, u32[]{:S(2)}, u32[]{:S(2)}) collective-permute-start(bf16[128,512]{1,0:T(8,128)(2,1)S(1)} %features.1.refs_0_), channel_id=1, source_target_pairs={{0,24},{4,28},{8,16},{12,20},{16,8},{20,12},{24,0},{28,4},{1,25},{... | collective-permute-start | bytes 393224 | tf_op jit(solution)/shard_map/ppermute | solution.py:88
  45.1 0.0 collective-permute-start.11
  45.1 0.6 collective-permute-start.9
  45.8 0.0 collective-permute-start.8
  45.8 10.5 %copy-done.1 = f32[2048,4096]{1,0:T(8,128)S(1)} copy-done((f32[2048,4096]{1,0:T(8,128)S(1)}, f32[2048,4096]{1,0:T(8,128)}, u32[]{:S(2)}) %copy-start.1) | copy-done | bytes 33554456
  56.3 1.2 panel_part.3.refs_3_
  57.6 0.0 copy-start.5
  57.6 0.6 collective-permute-start.14
  58.2 0.1 collective-permute-start.12
  58.3 0.4 collective-permute-start.10
  58.7 3.4 %panel_part.4.refs_4_ = f32[2048,128]{1,0:T(8,128)S(1)} custom-call(f32[2048,4096]{1,0:T(8,128)S(1)} %copy-done.1, bf16[128,512]{1,0:T(8,128)(2,1)S(1)} %collective-permute-done.9.refs_0_, bf16[128,512]{1,0:T(8,128)(2,1)S(1)} %collective-permute-done.11.refs_1_, bf16[128,512]{1,0:T(8,128)(2,1)S(1)} %collective-permute-done.13.refs_2_, ...), custom_call_target="tpu_custom_call" | custom-call | flops 1610612736 | bytes 12582912 | tf_op jit(solution)/shard_map/panel_part/pallas_call | solution.py:118
  62.2 4.5 %panel_part.5 = (f32[512,128]{1,0:T(8,128)S(1)}, f32[512,128]{1,0:T(8,128)S(1)}, f32[512,128]{1,0:T(8,128)S(1)}, f32[512,128]{1,0:T(8,128)S(1)}) custom-call(f32[2048,4096]{1,0:T(8,128)S(1)} %copy-done.1, bf16[128,512]{1,0:T(8,128)(2,1)S(1)} %collective-permute-done.8.refs_0_, bf16[128,512]{1,0:T(8,128)(2,1)S(1)} %collective-permute-done.10.refs_1_, ...), custom_call_target="tpu_custom_call" | custom-call | flops 2147483648 | bytes 16777216 | tf_op jit(solution)/shard_map/panel_part/pallas_call | solution.py:118
  66.7 1.7 %collective-permute-start.15 = (f32[512,128]{1,0:T(8,128)S(1)}, f32[512,128]{1,0:T(8,128)S(1)}, u32[]{:S(2)}, u32[]{:S(2)}) collective-permute-start(f32[512,128]{1,0:T(8,128)S(1)} %get-tuple-element.31), channel_id=1, source_target_pairs={{0,1},{1,0},{2,3},{3,2},{4,5},{5,4},{6,7},{7,6},{8,9},{9,8},{10,11... | collective-permute-start | bytes 786440 | tf_op jit(solution)/shard_map/ppermute | solution.py:83
  68.4 1.5 %collective-permute-start.16 = (f32[512,128]{1,0:T(8,128)S(1)}, f32[512,128]{1,0:T(8,128)S(1)}, u32[]{:S(2)}, u32[]{:S(2)}) collective-permute-start(f32[512,128]{1,0:T(8,128)S(1)} %get-tuple-element.32), channel_id=1, source_target_pairs={{0,2},{1,3},{2,0},{3,1},{4,6},{5,7},{6,4},{7,5},{8,10},{9,11},{10,... | collective-permute-start | bytes 786440 | tf_op jit(solution)/shard_map/ppermute | solution.py:83
  69.9 0.3 collective-permute-start.17
  70.2 0.7 collective-permute-start.7
  70.9 5.2 %collective-permute-done.15.refs_1_ = f32[512,128]{1,0:T(8,128)S(1)} collective-permute-done((f32[512,128]{1,0:T(8,128)S(1)}, f32[512,128]{1,0:T(8,128)S(1)}, u32[]{:S(2)}, u32[]{:S(2)}) %collective-permute-start.15) | collective-permute-done | bytes 262176 | tf_op jit(solution)/shard_map/ppermute | solution.py:83
  76.1 7.8 %collective-permute-done.16.refs_2_ = f32[512,128]{1,0:T(8,128)S(1)} collective-permute-done((f32[512,128]{1,0:T(8,128)S(1)}, f32[512,128]{1,0:T(8,128)S(1)}, u32[]{:S(2)}, u32[]{:S(2)}) %collective-permute-start.16) | collective-permute-done | bytes 262176 | tf_op jit(solution)/shard_map/ppermute | solution.py:83
  83.8 1.6 %collective-permute-done.17.refs_3_ = f32[512,128]{1,0:T(8,128)S(1)} collective-permute-done((f32[512,128]{1,0:T(8,128)S(1)}, f32[512,128]{1,0:T(8,128)S(1)}, u32[]{:S(2)}, u32[]{:S(2)}) %collective-permute-start.17) | collective-permute-done | bytes 262176 | tf_op jit(solution)/shard_map/ppermute | solution.py:83
  85.4 0.4 gram_part.1
  85.8 0.1 collective-permute-start.18
  85.9 1.2 collective-permute-done.18.y_ref
  87.1 0.1 collective-permute-start.19
  87.2 0.8 collective-permute-start.21
  88.1 3.4 %collective-permute-done.19.y_ref = f32[136,128]{1,0:T(8,128)S(1)} collective-permute-done((f32[136,128]{1,0:T(8,128)S(1)}, f32[136,128]{1,0:T(8,128)S(1)}, u32[]{:S(2)}, u32[]{:S(2)}) %collective-permute-start.19) | collective-permute-done | bytes 69664 | tf_op jit(solution)/shard_map/ppermute | solution.py:322
  91.5 4.4 %collective-permute-start.20 = (f32[136,128]{1,0:T(8,128)S(1)}, f32[136,128]{1,0:T(8,128)S(1)}, u32[]{:S(2)}, u32[]{:S(2)}) collective-permute-start(f32[136,128]{1,0:T(8,128)S(1)} %join.6.x_ref), channel_id=1, source_target_pairs={{0,16},{4,20},{8,24},{12,28},{16,0},{20,4},{24,8},{28,12},{1,17},{... | collective-permute-start | bytes 208904 | tf_op jit(solution)/shard_map/ppermute | solution.py:322
  95.9 8.6 %collective-permute-done.20.y_ref = f32[136,128]{1,0:T(8,128)S(1)} collective-permute-done((f32[136,128]{1,0:T(8,128)S(1)}, f32[136,128]{1,0:T(8,128)S(1)}, u32[]{:S(2)}, u32[]{:S(2)}) %collective-permute-start.20) | collective-permute-done | bytes 69664 | tf_op jit(solution)/shard_map/ppermute | solution.py:322
  104.6 0.2 collective-permute-start.29
  104.8 3.6 %collective-permute-start.22 = (f32[136,128]{1,0:T(8,128)S(1)}, f32[136,128]{1,0:T(8,128)S(1)}, u32[]{:S(2)}, u32[]{:S(2)}) collective-permute-start(f32[136,128]{1,0:T(8,128)S(1)} %get-tuple-element.36.x_ref), channel_id=1, source_target_pairs={{0,1},{1,0},{2,3},{3,2},{4,5},{5,4},{6,7},{7,6},{8,9},{9,8},{10,11... | collective-permute-start | bytes 208904 | tf_op jit(solution)/shard_map/ppermute | solution.py:83
  108.4 0.8 collective-permute-start.27
  109.2 3.8 %collective-permute-done.29.refs_11_ = bf16[512,128]{1,0:T(8,128)(2,1)S(1)} collective-permute-done((bf16[512,128]{1,0:T(8,128)(2,1)S(1)}, bf16[512,128]{1,0:T(8,128)(2,1)S(1)}, u32[]{:S(2)}, u32[]{:S(2)}) %collective-permute-start.29) | collective-permute-done | bytes 131104 | tf_op jit(solution)/shard_map/ppermute | solution.py:88
  112.9 0.1 collective-permute-start.23
  113.1 3.9 %collective-permute-done.28.refs_10_ = bf16[512,128]{1,0:T(8,128)(2,1)S(1)} collective-permute-done((bf16[512,128]{1,0:T(8,128)(2,1)S(1)}, bf16[512,128]{1,0:T(8,128)(2,1)S(1)}, u32[]{:S(2)}, u32[]{:S(2)}) %collective-permute-start.28) | collective-permute-done | bytes 131104 | tf_op jit(solution)/shard_map/ppermute | solution.py:88
  117.0 0.5 collective-permute-start.31
  117.5 0.1 collective-permute-done.23.y_ref
  117.6 1.6 %collective-permute-start.26 = (bf16[512,128]{1,0:T(8,128)(2,1)S(1)}, bf16[512,128]{1,0:T(8,128)(2,1)S(1)}, u32[]{:S(2)}, u32[]{:S(2)}) collective-permute-start(bf16[512,128]{1,0:T(8,128)(2,1)S(1)} %get-tuple-element.40.refs_4_), channel_id=1, source_target_pairs={{0,3},{1,2},{2,1},{3,0},{4,7},{5,6},{6,5},{7,4},{8,11},{9,10},{10,... | collective-permute-start | bytes 393224 | tf_op jit(solution)/shard_map/ppermute | solution.py:83
  119.2 1.1 collective-permute-start.25
  120.3 0.9 collective-permute-start.24
  121.2 4.1 %inverse.1 = (f32[128,128]{1,0:T(8,128)S(1)}, f32[8,128]{1,0:T(8,128)S(1)}) custom-call(f32[2048,4096]{1,0:T(8,128)S(1)} %copy-done.1, f32[136,128]{1,0:T(8,128)S(1)} %get-tuple-element.37.gram_ref, f32[1,128]{1,0:T(1,128)S(1)} %bitcast.7), custom_call_target="tpu_custom_call" | custom-call | tf_op jit(solution)/shard_map/inverse/pallas_call | solution.py:118
  125.3 0.0 collective-permute-done.26.refs_7_
  125.4 1.3 collective-permute-done.25.refs_6_
  126.7 16.9 %update.1 = (f32[2048,4096]{1,0:T(8,128)}, f32[1,2048]{1,0:T(1,128)}) custom-call(f32[2048,4096]{1,0:T(8,128)S(1)} %copy-done.1, f32[128,128]{1,0:T(8,128)S(1)} %get-tuple-element.38.refs_1_, f32[8,128]{1,0:T(8,128)S(1)} %get-tuple-element.39.refs_2_, f32[1,2048]{1,0:T(1,128)S(1)} %bitcast.5, bf16[512,128]{1,0:T(8,128)(2,1)S(1)} %get-tuple-element.40.refs_4_, ...), custom_call_target="tpu_custom_call" | custom-call | tf_op jit(solution)/shard_map/update/pallas_call | solution.py:118
  (37 shorter events, 0.1 us)
Async XLA Ops:
  0.6 9.2 %collective-permute-start.2 = (bf16[32,1024]{1,0:T(8,128)(2,1)}, bf16[32,1024]{1,0:T(8,128)(2,1)S(1)}, u32[]{:S(2)}, u32[]{:S(2)}) collective-permute-start(bf16[32,1024]{1,0:T(8,128)(2,1)} %refs_0_.3), channel_id=1, source_target_pairs={{0,3},{1,2},{2,1},{3,0},{4,7},{5,6},{6,5},{7,4},{8,11},{9,10},{10,... | collective-permute-start | bytes 196616 | tf_op jit(solution)/shard_map/ppermute | solution.py:83
  4.6 5.2 %collective-permute-start.1 = (bf16[32,1024]{1,0:T(8,128)(2,1)}, bf16[32,1024]{1,0:T(8,128)(2,1)S(1)}, u32[]{:S(2)}, u32[]{:S(2)}) collective-permute-start(bf16[32,1024]{1,0:T(8,128)(2,1)} %refs_0_.3), channel_id=1, source_target_pairs={{0,2},{1,3},{2,0},{3,1},{4,6},{5,7},{6,4},{7,5},{8,10},{9,11},{10,... | collective-permute-start | bytes 196616 | tf_op jit(solution)/shard_map/ppermute | solution.py:83
  5.1 4.7 %collective-permute-start = (bf16[32,1024]{1,0:T(8,128)(2,1)}, bf16[32,1024]{1,0:T(8,128)(2,1)S(1)}, u32[]{:S(2)}, u32[]{:S(2)}) collective-permute-start(bf16[32,1024]{1,0:T(8,128)(2,1)} %refs_0_.3), channel_id=1, source_target_pairs={{0,1},{1,0},{2,3},{3,2},{4,5},{5,4},{6,7},{7,6},{8,9},{9,8},{10,11... | collective-permute-start | bytes 196616 | tf_op jit(solution)/shard_map/ppermute | solution.py:83
  5.2 3.4 %copy-start.2 = (bf16[1024,4096]{1,0:T(8,128)(2,1)S(1)}, bf16[1024,4096]{1,0:T(8,128)(2,1)}, u32[]{:S(2)}) copy-start(bf16[1024,4096]{1,0:T(8,128)(2,1)} %in_ref.2) | copy-start | bytes 25165828
  8.6 32.5 %copy-start.6 = (f32[4096]{0:T(1024)S(1)}, f32[4096]{0:T(1024)}, u32[]{:S(2)}) copy-start(f32[4096]{0:T(1024)} %param.8) | copy-start | bytes 49156
  9.8 0.8 copy-start.3
  11.4 2.7 %collective-permute-start.3 = (f32[128,2048]{1,0:T(8,128)S(1)}, f32[128,2048]{1,0:T(8,128)S(1)}, u32[]{:S(2)}, u32[]{:S(2)}) collective-permute-start(f32[128,2048]{1,0:T(8,128)S(1)} %preact_part.2), channel_id=1, source_target_pairs={{0,4},{4,0},{8,12},{12,8},{16,20},{20,16},{24,28},{28,24},{1,5},{5... | collective-permute-start | bytes 3145736 | tf_op jit(solution)/shard_map/ppermute | solution.py:92
  11.5 0.8 copy-start.4
  14.3 26.9 %collective-permute-start.4 = (f32[128,512]{1,0:T(8,128)S(1)}, f32[128,512]{1,0:T(8,128)S(1)}, u32[]{:S(2)}, u32[]{:S(2)}) collective-permute-start(f32[128,512]{1,0:T(8,128)S(1)} %get-tuple-element.27), channel_id=1, source_target_pairs={{0,8},{4,12},{8,0},{12,4},{16,24},{20,28},{24,16},{28,20},{1,9},{5... | collective-permute-start | bytes 786440 | tf_op jit(solution)/shard_map/ppermute | solution.py:88
  16.3 24.8 %collective-permute-start.5 = (f32[128,512]{1,0:T(8,128)S(1)}, f32[128,512]{1,0:T(8,128)S(1)}, u32[]{:S(2)}, u32[]{:S(2)}) collective-permute-start(f32[128,512]{1,0:T(8,128)S(1)} %get-tuple-element.28), channel_id=1, source_target_pairs={{0,16},{4,20},{8,24},{12,28},{16,0},{20,4},{24,8},{28,12},{1,17},{... | collective-permute-start | bytes 786440 | tf_op jit(solution)/shard_map/ppermute | solution.py:88
  18.9 22.3 %collective-permute-start.6 = (f32[128,512]{1,0:T(8,128)S(1)}, f32[128,512]{1,0:T(8,128)S(1)}, u32[]{:S(2)}, u32[]{:S(2)}) collective-permute-start(f32[128,512]{1,0:T(8,128)S(1)} %get-tuple-element.29), channel_id=1, source_target_pairs={{0,24},{4,28},{8,16},{12,20},{16,8},{20,12},{24,0},{28,4},{1,25},{... | collective-permute-start | bytes 786440 | tf_op jit(solution)/shard_map/ppermute | solution.py:88
  29.5 11.7 %copy-start = (f32[2048,4096]{1,0:T(8,128)}, f32[2048,4096]{1,0:T(8,128)S(1)}, u32[]{:S(2)}) copy-start(f32[2048,4096]{1,0:T(8,128)S(1)} %get-tuple-element.25.c_ref._.refs_0_) | copy-start | bytes 100663296
  41.3 16.3 %collective-permute-start.13 = (bf16[128,512]{1,0:T(8,128)(2,1)S(1)}, bf16[128,512]{1,0:T(8,128)(2,1)S(1)}, u32[]{:S(2)}, u32[]{:S(2)}) collective-permute-start(bf16[128,512]{1,0:T(8,128)(2,1)S(1)} %features.1.refs_0_), channel_id=1, source_target_pairs={{0,24},{4,28},{8,16},{12,20},{16,8},{20,12},{24,0},{28,4},{1,25},{... | collective-permute-start | bytes 393224 | tf_op jit(solution)/shard_map/ppermute | solution.py:88
  45.1 13.0 %collective-permute-start.11 = (bf16[128,512]{1,0:T(8,128)(2,1)S(1)}, bf16[128,512]{1,0:T(8,128)(2,1)S(1)}, u32[]{:S(2)}, u32[]{:S(2)}) collective-permute-start(bf16[128,512]{1,0:T(8,128)(2,1)S(1)} %features.1.refs_0_), channel_id=1, source_target_pairs={{0,16},{4,20},{8,24},{12,28},{16,0},{20,4},{24,8},{28,12},{1,17},{... | collective-permute-start | bytes 393224 | tf_op jit(solution)/shard_map/ppermute | solution.py:88
  45.1 13.1 %collective-permute-start.9 = (bf16[128,512]{1,0:T(8,128)(2,1)S(1)}, bf16[128,512]{1,0:T(8,128)(2,1)S(1)}, u32[]{:S(2)}, u32[]{:S(2)}) collective-permute-start(bf16[128,512]{1,0:T(8,128)(2,1)S(1)} %features.1.refs_0_), channel_id=1, source_target_pairs={{0,8},{4,12},{8,0},{12,4},{16,24},{20,28},{24,16},{28,20},{1,9},{5... | collective-permute-start | bytes 393224 | tf_op jit(solution)/shard_map/ppermute | solution.py:88
  45.8 16.3 %collective-permute-start.8 = (bf16[128,512]{1,0:T(8,128)(2,1)S(1)}, bf16[128,512]{1,0:T(8,128)(2,1)S(1)}, u32[]{:S(2)}, u32[]{:S(2)}) collective-permute-start(bf16[128,512]{1,0:T(8,128)(2,1)S(1)} %features.1.refs_0_), channel_id=1, source_target_pairs={{0,4},{4,0},{8,12},{12,8},{16,20},{20,16},{24,28},{28,24},{1,5},{5... | collective-permute-start | bytes 393224 | tf_op jit(solution)/shard_map/ppermute | solution.py:92
  45.8 10.5 %copy-start.1 = (f32[2048,4096]{1,0:T(8,128)S(1)}, f32[2048,4096]{1,0:T(8,128)}, u32[]{:S(2)}) copy-start(f32[2048,4096]{1,0:T(8,128)} %copy-done) | copy-start | bytes 100663296
  57.6 27.8 %copy-start.5 = (f32[2048]{0:T(1024)S(1)}, f32[2048]{0:T(1024)}, u32[]{:S(2)}) copy-start(f32[2048]{0:T(1024)} %param.10) | copy-start | bytes 24580
  57.6 4.5 %collective-permute-start.14 = (bf16[128,512]{1,0:T(8,128)(2,1)S(1)}, bf16[128,512]{1,0:T(8,128)(2,1)S(1)}, u32[]{:S(2)}, u32[]{:S(2)}) collective-permute-start(bf16[128,512]{1,0:T(8,128)(2,1)S(1)} %collective-permute-done.13.refs_2_), channel_id=1, source_target_pairs={{0,4},{4,0},{8,12},{12,8},{16,20},{20,16},{24,28},{28,24},{1,5},{5... | collective-permute-start | bytes 393224 | tf_op jit(solution)/shard_map/ppermute | solution.py:92
  58.2 4.0 %collective-permute-start.12 = (bf16[128,512]{1,0:T(8,128)(2,1)S(1)}, bf16[128,512]{1,0:T(8,128)(2,1)S(1)}, u32[]{:S(2)}, u32[]{:S(2)}) collective-permute-start(bf16[128,512]{1,0:T(8,128)(2,1)S(1)} %collective-permute-done.11.refs_1_), channel_id=1, source_target_pairs={{0,4},{4,0},{8,12},{12,8},{16,20},{20,16},{24,28},{28,24},{1,5},{5... | collective-permute-start | bytes 393224 | tf_op jit(solution)/shard_map/ppermute | solution.py:92
  58.3 3.9 %collective-permute-start.10 = (bf16[128,512]{1,0:T(8,128)(2,1)S(1)}, bf16[128,512]{1,0:T(8,128)(2,1)S(1)}, u32[]{:S(2)}, u32[]{:S(2)}) collective-permute-start(bf16[128,512]{1,0:T(8,128)(2,1)S(1)} %collective-permute-done.9.refs_0_), channel_id=1, source_target_pairs={{0,4},{4,0},{8,12},{12,8},{16,20},{20,16},{24,28},{28,24},{1,5},{5... | collective-permute-start | bytes 393224 | tf_op jit(solution)/shard_map/ppermute | solution.py:92
  66.7 9.4 %collective-permute-start.15 = (f32[512,128]{1,0:T(8,128)S(1)}, f32[512,128]{1,0:T(8,128)S(1)}, u32[]{:S(2)}, u32[]{:S(2)}) collective-permute-start(f32[512,128]{1,0:T(8,128)S(1)} %get-tuple-element.31), channel_id=1, source_target_pairs={{0,1},{1,0},{2,3},{3,2},{4,5},{5,4},{6,7},{7,6},{8,9},{9,8},{10,11... | collective-permute-start | bytes 786440 | tf_op jit(solution)/shard_map/ppermute | solution.py:83
  68.4 15.5 %collective-permute-start.16 = (f32[512,128]{1,0:T(8,128)S(1)}, f32[512,128]{1,0:T(8,128)S(1)}, u32[]{:S(2)}, u32[]{:S(2)}) collective-permute-start(f32[512,128]{1,0:T(8,128)S(1)} %get-tuple-element.32), channel_id=1, source_target_pairs={{0,2},{1,3},{2,0},{3,1},{4,6},{5,7},{6,4},{7,5},{8,10},{9,11},{10,... | collective-permute-start | bytes 786440 | tf_op jit(solution)/shard_map/ppermute | solution.py:83
  69.9 15.5 %collective-permute-start.17 = (f32[512,128]{1,0:T(8,128)S(1)}, f32[512,128]{1,0:T(8,128)S(1)}, u32[]{:S(2)}, u32[]{:S(2)}) collective-permute-start(f32[512,128]{1,0:T(8,128)S(1)} %get-tuple-element.33), channel_id=1, source_target_pairs={{0,3},{1,2},{2,1},{3,0},{4,7},{5,6},{6,5},{7,4},{8,11},{9,10},{10,... | collective-permute-start | bytes 786440 | tf_op jit(solution)/shard_map/ppermute | solution.py:83
  70.2 0.7 collective-permute-start.7
  85.8 1.3 collective-permute-start.18
  87.1 4.4 %collective-permute-start.19 = (f32[136,128]{1,0:T(8,128)S(1)}, f32[136,128]{1,0:T(8,128)S(1)}, u32[]{:S(2)}, u32[]{:S(2)}) collective-permute-start(f32[136,128]{1,0:T(8,128)S(1)} %join.5.x_ref), channel_id=1, source_target_pairs={{0,8},{4,12},{8,0},{12,4},{16,24},{20,28},{24,16},{28,20},{1,9},{5... | collective-permute-start | bytes 208904 | tf_op jit(solution)/shard_map/ppermute | solution.py:322
  87.2 8.7 %collective-permute-start.21 = (bf16[512,128]{1,0:T(8,128)(2,1)S(1)}, bf16[512,128]{1,0:T(8,128)(2,1)S(1)}, u32[]{:S(2)}, u32[]{:S(2)}) collective-permute-start(bf16[512,128]{1,0:T(8,128)(2,1)S(1)} %get-tuple-element.35.refs_0_), channel_id=1, source_target_pairs={{0,0},{1,8},{2,16},{3,24},{4,4},{5,12},{6,20},{7,28},{8,1},{9,9},{... | collective-permute-start | bytes 393224 | tf_op jit(solution)/shard_map/ppermute | solution.py:103
  91.5 13.0 %collective-permute-start.20 = (f32[136,128]{1,0:T(8,128)S(1)}, f32[136,128]{1,0:T(8,128)S(1)}, u32[]{:S(2)}, u32[]{:S(2)}) collective-permute-start(f32[136,128]{1,0:T(8,128)S(1)} %join.6.x_ref), channel_id=1, source_target_pairs={{0,16},{4,20},{8,24},{12,28},{16,0},{20,4},{24,8},{28,12},{1,17},{... | collective-permute-start | bytes 208904 | tf_op jit(solution)/shard_map/ppermute | solution.py:322
  104.6 8.4 %collective-permute-start.29 = (bf16[512,128]{1,0:T(8,128)(2,1)S(1)}, bf16[512,128]{1,0:T(8,128)(2,1)S(1)}, u32[]{:S(2)}, u32[]{:S(2)}) collective-permute-start(bf16[512,128]{1,0:T(8,128)(2,1)S(1)} %get-tuple-element.41.refs_8_), channel_id=1, source_target_pairs={{0,24},{4,28},{8,16},{12,20},{16,8},{20,12},{24,0},{28,4},{1,25},{... | collective-permute-start | bytes 393224 | tf_op jit(solution)/shard_map/ppermute | solution.py:88
  104.8 16.4 %copy-start.7 = (f32[128]{0:T(128)S(1)}, f32[128]{0:T(128)}, u32[]{:S(2)}) copy-start(f32[128]{0:T(128)} %param.11) | copy-start | bytes 1540
  104.8 8.2 %collective-permute-start.22 = (f32[136,128]{1,0:T(8,128)S(1)}, f32[136,128]{1,0:T(8,128)S(1)}, u32[]{:S(2)}, u32[]{:S(2)}) collective-permute-start(f32[136,128]{1,0:T(8,128)S(1)} %get-tuple-element.36.x_ref), channel_id=1, source_target_pairs={{0,1},{1,0},{2,3},{3,2},{4,5},{5,4},{6,7},{7,6},{8,9},{9,8},{10,11... | collective-permute-start | bytes 208904 | tf_op jit(solution)/shard_map/ppermute | solution.py:83
  108.3 8.6 %collective-permute-start.28 = (bf16[512,128]{1,0:T(8,128)(2,1)S(1)}, bf16[512,128]{1,0:T(8,128)(2,1)S(1)}, u32[]{:S(2)}, u32[]{:S(2)}) collective-permute-start(bf16[512,128]{1,0:T(8,128)(2,1)S(1)} %get-tuple-element.41.refs_8_), channel_id=1, source_target_pairs={{0,16},{4,20},{8,24},{12,28},{16,0},{20,4},{24,8},{28,12},{1,17},{... | collective-permute-start | bytes 393224 | tf_op jit(solution)/shard_map/ppermute | solution.py:88
  108.4 8.6 %collective-permute-start.27 = (bf16[512,128]{1,0:T(8,128)(2,1)S(1)}, bf16[512,128]{1,0:T(8,128)(2,1)S(1)}, u32[]{:S(2)}, u32[]{:S(2)}) collective-permute-start(bf16[512,128]{1,0:T(8,128)(2,1)S(1)} %get-tuple-element.41.refs_8_), channel_id=1, source_target_pairs={{0,8},{4,12},{8,0},{12,4},{16,24},{20,28},{24,16},{28,20},{1,9},{5... | collective-permute-start | bytes 393224 | tf_op jit(solution)/shard_map/ppermute | solution.py:88
  109.2 10.0 %collective-permute-start.30 = (bf16[512,128]{1,0:T(8,128)(2,1)S(1)}, bf16[512,128]{1,0:T(8,128)(2,1)S(1)}, u32[]{:S(2)}, u32[]{:S(2)}) collective-permute-start(bf16[512,128]{1,0:T(8,128)(2,1)S(1)} %get-tuple-element.41.refs_8_), channel_id=1, source_target_pairs={{0,4},{4,0},{8,12},{12,8},{16,20},{20,16},{24,28},{28,24},{1,5},{5... | collective-permute-start | bytes 393224 | tf_op jit(solution)/shard_map/ppermute | solution.py:92
  112.9 7.3 %collective-permute-start.33 = (bf16[512,128]{1,0:T(8,128)(2,1)S(1)}, bf16[512,128]{1,0:T(8,128)(2,1)S(1)}, u32[]{:S(2)}, u32[]{:S(2)}) collective-permute-start(bf16[512,128]{1,0:T(8,128)(2,1)S(1)} %collective-permute-done.29.refs_11_), channel_id=1, source_target_pairs={{0,4},{4,0},{8,12},{12,8},{16,20},{20,16},{24,28},{28,24},{1,5},{5... | collective-permute-start | bytes 393224 | tf_op jit(solution)/shard_map/ppermute | solution.py:92
  112.9 4.7 %collective-permute-start.23 = (f32[136,128]{1,0:T(8,128)S(1)}, f32[136,128]{1,0:T(8,128)S(1)}, u32[]{:S(2)}, u32[]{:S(2)}) collective-permute-start(f32[136,128]{1,0:T(8,128)S(1)} %join.8.x_ref), channel_id=1, source_target_pairs={{0,2},{1,3},{2,0},{3,1},{4,6},{5,7},{6,4},{7,5},{8,10},{9,11},{10,... | collective-permute-start | bytes 208904 | tf_op jit(solution)/shard_map/ppermute | solution.py:83
  116.9 8.4 %collective-permute-start.32 = (bf16[512,128]{1,0:T(8,128)(2,1)S(1)}, bf16[512,128]{1,0:T(8,128)(2,1)S(1)}, u32[]{:S(2)}, u32[]{:S(2)}) collective-permute-start(bf16[512,128]{1,0:T(8,128)(2,1)S(1)} %collective-permute-done.28.refs_10_), channel_id=1, source_target_pairs={{0,4},{4,0},{8,12},{12,8},{16,20},{20,16},{24,28},{28,24},{1,5},{5... | collective-permute-start | bytes 393224 | tf_op jit(solution)/shard_map/ppermute | solution.py:92
  117.0 8.4 %collective-permute-start.31 = (bf16[512,128]{1,0:T(8,128)(2,1)S(1)}, bf16[512,128]{1,0:T(8,128)(2,1)S(1)}, u32[]{:S(2)}, u32[]{:S(2)}) collective-permute-start(bf16[512,128]{1,0:T(8,128)(2,1)S(1)} %collective-permute-done.27.refs_9_), channel_id=1, source_target_pairs={{0,4},{4,0},{8,12},{12,8},{16,20},{20,16},{24,28},{28,24},{1,5},{5... | collective-permute-start | bytes 393224 | tf_op jit(solution)/shard_map/ppermute | solution.py:92
  117.6 7.7 %collective-permute-start.26 = (bf16[512,128]{1,0:T(8,128)(2,1)S(1)}, bf16[512,128]{1,0:T(8,128)(2,1)S(1)}, u32[]{:S(2)}, u32[]{:S(2)}) collective-permute-start(bf16[512,128]{1,0:T(8,128)(2,1)S(1)} %get-tuple-element.40.refs_4_), channel_id=1, source_target_pairs={{0,3},{1,2},{2,1},{3,0},{4,7},{5,6},{6,5},{7,4},{8,11},{9,10},{10,... | collective-permute-start | bytes 393224 | tf_op jit(solution)/shard_map/ppermute | solution.py:83
  119.2 7.5 %collective-permute-start.25 = (bf16[512,128]{1,0:T(8,128)(2,1)S(1)}, bf16[512,128]{1,0:T(8,128)(2,1)S(1)}, u32[]{:S(2)}, u32[]{:S(2)}) collective-permute-start(bf16[512,128]{1,0:T(8,128)(2,1)S(1)} %get-tuple-element.40.refs_4_), channel_id=1, source_target_pairs={{0,2},{1,3},{2,0},{3,1},{4,6},{5,7},{6,4},{7,5},{8,10},{9,11},{10,... | collective-permute-start | bytes 393224 | tf_op jit(solution)/shard_map/ppermute | solution.py:83
  120.3 6.4 %collective-permute-start.24 = (bf16[512,128]{1,0:T(8,128)(2,1)S(1)}, bf16[512,128]{1,0:T(8,128)(2,1)S(1)}, u32[]{:S(2)}, u32[]{:S(2)}) collective-permute-start(bf16[512,128]{1,0:T(8,128)(2,1)S(1)} %get-tuple-element.40.refs_4_), channel_id=1, source_target_pairs={{0,1},{1,0},{2,3},{3,2},{4,5},{5,4},{6,7},{7,6},{8,9},{9,8},{10,11... | collective-permute-start | bytes 393224 | tf_op jit(solution)/shard_map/ppermute | solution.py:83

commit v3 on v2

--- a/solution.py
+++ b/solution.py
@@ -92,14 +92,14 @@
     return lax.ppermute(x, "row", [(i, i ^ step) for i in range(lax.axis_size("row"))])
 
 
-def transpose(x):
+def transpose(x, step=0):
     cols = lax.axis_size("col")
     inner = lax.axis_size("row") // cols
     pairs = []
     for outer in range(cols):
         for k in range(inner):
             for col in range(cols):
-                pairs.append(((outer * inner + k) * cols + col, (col * inner + k) * cols + outer))
+                pairs.append(((outer * inner + k) * cols + col, ((col ^ step) * inner + k) * cols + outer))
     return lax.ppermute(x, ("row", "col"), pairs)
 
 
@@ -127,25 +127,46 @@
     )(*operands)
 
 
-def hold_kernel(in_ref, *refs):
-    out_ref, token_ref, sem = refs[-3:]
-    copy = pltpu.make_async_copy(in_ref, out_ref, sem)
-    copy.start()
-    token_ref[...] = jnp.zeros_like(token_ref)
-    copy.wait()
-
-
-def hold(x, name, *after):
+def hold_kernel(*refs):
+    n = len(refs) // 2
+    copies = [pltpu.make_async_copy(refs[i], refs[n + i], refs[-1].at[i]) for i in range(n)]
+    for copy in copies:
+        copy.start()
+    for copy in copies:
+        copy.wait()
+
+
+def hold(*arrays):
     return call(
         hold_kernel,
-        name,
-        (x, *after),
-        [pl.BlockSpec(memory_space=pl.ANY)] * (1 + len(after)),
-        vmem(2),
-        [pltpu.VMEM(x.shape, x.dtype), jax.ShapeDtypeStruct((8, 128), F32)],
-        [pltpu.SemaphoreType.DMA],
-        size=x.size * x.dtype.itemsize,
-    )
+        "hold_weight",
+        [in_hbm(x) for x in arrays],
+        [pl.BlockSpec(memory_space=pl.ANY)] * len(arrays),
+        vmem(len(arrays)),
+        [pltpu.VMEM(x.shape, x.dtype) for x in arrays[:1]]
+        + [jax.ShapeDtypeStruct(x.shape, x.dtype) for x in arrays[1:]],
+        [pltpu.SemaphoreType.DMA((len(arrays),))],
+        size=arrays[0].size * arrays[0].dtype.itemsize,
+    )
+
+
+def touch_kernel(*refs):
+    refs[-1][...] = jnp.zeros_like(refs[-1])
+
+
+def touch(x, *after):
+    return call(
+        touch_kernel,
+        "touch",
+        (in_vmem(x), *after),
+        vmem(1) + [pl.BlockSpec(memory_space=pl.ANY)] * len(after),
+        vmem(1)[0],
+        jax.ShapeDtypeStruct((8, 128), F32),
+    )
+
+
+def in_hbm(x):
+    return pltpu.with_memory_space_constraint(x, pltpu.HBM)
 
 
 def in_vmem(x):
@@ -211,7 +232,7 @@
     return call(
         feature_kernel,
         "features",
-        (token, bias.reshape(1, bias.shape[0]), *parts),
+        (token, bias, *parts),
         vmem(2 + len(parts)),
         vmem(1)[0],
         jax.ShapeDtypeStruct((rows, width), BF16),
@@ -219,12 +240,15 @@
     )
 
 
-def panel_kernel(steps, last, c_ref, *refs):
+def panel_kernel(steps, kind, c_ref, *refs):
     n = len(steps)
+    last = kind == "last"
     shards, rest = refs[:n], refs[n:]
     outer, inner_index, col, _, cols = places()
-    acc_ref = None if len(rest) == (cols if last else 1) else rest[0]
-    outs = rest[-cols:] if last else rest[-1:]
+    acc_ref = None if kind == "first" else rest[0]
+    outs = rest[0 if acc_ref is None else 1 :]
+    if kind == "first":
+        outs[1][...] = shards[0][...]
     width = shards[0].shape[1]
     quarter = c_ref.shape[0] // cols
     rows = min(512, quarter)
@@ -247,18 +271,19 @@
                 outs[0][here, :] = sums
 
 
-def panel_part(covariance, shards, steps, acc=None, send=None):
+def panel_part(covariance, shards, steps, kind, acc=None):
     n = len(shards)
     batch, width = shards[0].shape
     rows = covariance.shape[0]
     cols = lax.axis_size("col")
     operands = [in_vmem(covariance), *shards] + ([] if acc is None else [acc])
-    if send is None:
-        shape = [jax.ShapeDtypeStruct((rows, batch), F32)]
-    else:
-        shape = [jax.ShapeDtypeStruct((rows // cols, batch), send if s else F32) for s in range(cols)]
+    shape = [jax.ShapeDtypeStruct((rows, batch), F32)]
+    if kind == "last":
+        shape = [jax.ShapeDtypeStruct((rows // cols, batch), F32)] * cols
+    if kind == "first":
+        shape.append(jax.ShapeDtypeStruct((batch, width), BF16))
     outs = call(
-        functools.partial(panel_kernel, tuple(steps), send is not None),
+        functools.partial(panel_kernel, tuple(steps), kind),
         "panel_part",
         operands,
         vmem(len(operands)),
@@ -268,7 +293,7 @@
         4 * rows * width * n * batch,
         4 * rows * width * n,
     )
-    return outs[0] if send is None else outs
+    return outs if len(shape) > 1 else outs[0]
 
 
 def gram_kernel(_, phi_ref, mean_ref, *refs):
@@ -297,45 +322,27 @@
     )
 
 
-def join_kernel(count, _, x_ref, y_ref, *refs):
-    out_ref = refs[count]
-    out_ref[...] = x_ref[...] + y_ref[...]
-    for source, target in zip(refs[:count], refs[count + 1 :]):
-        target[...] = source[...]
-
-
-def join(held, x, y, *others):
-    outs = call(
-        functools.partial(join_kernel, len(others)),
+def join_kernel(_, x_ref, y_ref, *refs):
+    refs[-1][...] = x_ref[...] + y_ref[...]
+
+
+def join(held, x, y, *after):
+    return call(
+        join_kernel,
         "join",
-        (in_vmem(held), x, y, *others),
-        vmem(3 + len(others)),
-        vmem(1 + len(others)),
-        [jax.ShapeDtypeStruct(a.shape, a.dtype) for a in (x, *others)],
-    )
-    return outs if others else outs[0]
-
-
-def total_row(held, x, *others):
-    step, size = 1, lax.axis_size("row")
-    while step < size:
-        y = lax.ppermute(x, "row", [(i, i ^ step) for i in range(size)])
-        step *= 2
-        if step == size and others:
-            return join(held, x, y, *others)
-        x = join(held, x, y)
-    return x
-
-
-def total_col(held, x, *others):
-    step, size = 1, lax.axis_size("col")
-    while step < size:
-        y = swap_col(x, step)
-        step *= 2
-        if step == size and others:
-            return join(held, x, y, *others)
-        x = join(held, x, y)
-    return x
+        (in_vmem(held), x, y, *after),
+        vmem(3) + [pl.BlockSpec(memory_space=pl.ANY)] * len(after),
+        vmem(1)[0],
+        jax.ShapeDtypeStruct(x.shape, x.dtype),
+    )
+
+
+def doublings(axis):
+    return [1 << i for i in range(lax.axis_size(axis).bit_length() - 1)]
+
+
+def swap(x, axis, step):
+    return lax.ppermute(x, axis, [(i, i ^ step) for i in range(lax.axis_size(axis))])
 
 
 def inverse_kernel(_, gram_ref, rewards_ref, inverse_ref, coeffs_ref):
@@ -402,11 +409,11 @@
     )
 
 
-def update_kernel(near, far, tile, *refs):
+def update_kernel(near, far, *refs):
     c_ref, inverse_ref, coeffs_ref, mean_ref = refs[:4]
     near_refs = refs[4 : 4 + near]
     far_refs = refs[4 + near : 4 + near + far]
-    out_ref, new_mean_ref, gain, panel, other = refs[4 + near + far :]
+    out_ref, new_mean_ref, gain, panel, other, buffers, sems = refs[4 + near + far :]
     outer, inner_index, col, _, cols = places()
     batch = inverse_ref.shape[0]
     quarter = near_refs[0].shape[0]
@@ -424,24 +431,31 @@
     gain[:, batch:] = lo
     new_mean_ref[...] = mean_ref[...] + sum(dot(p, rows, NT) for p in split3(coeffs_ref[...]))[:1]
 
-    def body(step, block):
-        here = span(step.index[0], tile)
-        block[...] = c_ref[:, here] - dot(gain[...], other[here, :], NT)
-
-    pltpu.emit_pipeline(
-        body,
-        grid=(c_ref.shape[1] // tile,),
-        in_specs=[],
-        out_specs=[pl.BlockSpec((c_ref.shape[0], tile), lambda i: (0, i))],
-        _explicit_indices=True,
-    )(out_ref)
+    slots, rows, width = buffers.shape
+    across = c_ref.shape[1] // width
+    steps = c_ref.shape[0] // rows * across
+
+    def copy(n):
+        i, j = n // across, n % across
+        there = out_ref.at[pl.ds(i * rows, rows), pl.ds(j * width, width)]
+        return pltpu.make_async_copy(buffers.at[n % slots], there, sems.at[n % slots])
+
+    for n in range(steps):
+        here = pl.ds(n // across * rows, rows)
+        there = pl.ds(n % across * width, width)
+        if n >= slots:
+            copy(n - slots).wait()
+        buffers[n % slots] = c_ref[here, there] - dot(gain[here, :], other[there, :], NT)
+        copy(n).start()
+    for n in range(max(0, steps - slots), steps):
+        copy(n).wait()
 
 
 def update(covariance, inverse, coeffs, mean, near, far):
     rows, cols = covariance.shape
     batch = inverse.shape[0]
     return call(
-        functools.partial(update_kernel, len(near), len(far), min(256, cols)),
+        functools.partial(update_kernel, len(near), len(far)),
         "update",
         (in_vmem(covariance), inverse, coeffs, mean.reshape(1, rows), *near, *far),
         vmem(4 + len(near) + len(far)),
@@ -451,6 +465,8 @@
             pltpu.VMEM((rows, 2 * batch), BF16),
             pltpu.VMEM((rows, batch), BF16),
             pltpu.VMEM((cols, 2 * batch), BF16),
+            pltpu.VMEM((6, min(512, rows), min(512, cols)), F32),
+            pltpu.SemaphoreType.DMA((6,)),
         ],
     )
 
@@ -464,30 +480,34 @@
         return plain(context, weight, feature_bias, covariance, prior_mean, rewards)
 
     blocks = [context] + [swap_col(context, s) for s in range(1, cols)]
-    w_held, _ = hold(weight, "hold_weight")
+    bias = feature_bias.reshape(1, block)
+    w_held, blocks[0], bias = hold(weight, context, bias)
     sums = []
     for k in range(inner - 1, -1, -1):
         piece = preact_part(k, blocks, w_held, part)
         sums.append(swap_inner(piece, k) if k else piece)
     pieces = scatter(sums, cols)
-    summed = [pieces[0]] + [swap_outer(pieces[s], s) for s in range(1, cols)]
-    held, token = hold(covariance, "hold_covariance", pieces[0])
-    features = features_of(token, feature_bias, summed)
+    summed = [pieces[0]] + [swap_outer(pieces[s], s) for s in range(cols - 1, 0, -1)]
+    token = touch(covariance, pieces[0])
+    features = features_of(token, bias, summed)
 
     shards = [features] + [swap_outer(features, s) for s in range(1, cols)]
-    panel = panel_part(held, shards[:1], [(0, 0)])
-    panel = panel_part(held, shards[1:], [(s, 0) for s in range(1, cols)], panel)
+    held = covariance
+    panel, sent = panel_part(held, shards[:1], [(0, 0)], "first")
+    far_features = transpose(sent)
+    panel = panel_part(held, shards[1:], [(s, 0) for s in range(1, cols)], "next", panel)
     for k in range(1, inner):
         others = [swap_inner(s, k) for s in shards]
-        panel = panel_part(held, others, [(s, k) for s in range(cols)], panel, F32 if k == inner - 1 else None)
-
-    far_features = transpose(features)
+        kind = "last" if k == inner - 1 else "next"
+        panel = panel_part(held, others, [(s, k) for s in range(cols)], kind, panel)
+
     parts = [panel[0]] + [swap_col(panel[s], s) for s in range(1, cols)]
     own_panel, gram = gram_part(held, far_features, prior_mean, parts)
-    gram, turned = total_row(held, gram, transpose(own_panel))
-    far = [turned] + [swap_outer(turned, s) for s in range(1, cols)]
-    gram, own_panel = total_col(held, gram, own_panel)
+    steps = [("row", step) for step in doublings("row")] + [("col", step) for step in doublings("col")]
+    far = [transpose(own_panel, s) for s in range(cols)]
     near = [own_panel] + [swap_col(own_panel, s) for s in range(1, cols)]
+    for i, (axis, step) in enumerate(steps):
+        gram = join(held, gram, swap(gram, axis, step), *(far + near[1:] if i == len(steps) - 1 else []))
     for k in range(1, inner):
         far += [swap_inner(f, k) for f in far[:cols]]
 

time: 144 us -> 131 us (0.910)
  Pallas kernels: 44.1 us -> 31.5 us
  local copies, waits for them, and re-layouts: 27.3 us -> 21.1 us
  starting transfers between devices: 33.3 us -> 36.9 us
  waiting for transfers between devices: 38 us -> 40.6 us
    pallas_call x17, Pallas kernels: 44.1 us -> 31.5 us  [call(): pl.pallas_call(kernel, in_specs=in_specs, out_specs=out_specs, out_shape=...]
    unnamed x16 -> x8, local copies, waits for them, and re-layouts: 27.3 us -> 21.1 us
    ppermute x2 -> x5, starting transfers between devices: 1.51 us -> 6.51 us  [transpose(): return lax.ppermute(x, ('row', 'col'), pairs)]
    ppermute x3 -> x5, waiting for transfers between devices: 13.3 us -> 9.24 us  [swap(): lax.ppermute(x, axis, [(i, i ^ step) for i in range(lax.axis_size(axis))])]
    ppermute x9 -> x6, waiting for transfers between devices: 7.65 us -> 11.3 us  [swap_outer(): return lax.ppermute(x, 'row', [(i, i ^ step * inner) for i in range(n)])]
    ppermute x11 -> x9, starting transfers between devices: 15.4 us -> 13.9 us  [swap_col(): return lax.ppermute(x, 'col', [(i, i ^ step) for i in range(n)])]
    ppermute x3 -> x5, starting transfers between devices: 4.52 us -> 5.91 us  [swap(): lax.ppermute(x, axis, [(i, i ^ step) for i in range(lax.axis_size(axis))])]
    ppermute x9 -> x6, starting transfers between devices: 10.2 us -> 8.91 us  [swap_outer(): return lax.ppermute(x, 'row', [(i, i ^ step * inner) for i in range(n)])]
  transfers between devices with their start and end apart: 34 -> 34, of which waited for: 11 -> 12; matrix products, arithmetic and copies ran while one was open for 0% -> 0% of each run, Pallas kernels for 15% -> 10%
where the time goes in v3:
time: 131 us
  waiting for transfers between devices  40.6 us (31%)
  starting transfers between devices  36.9 us (28%)
  Pallas kernels  31.5 us (24%)
  local copies, waits for them, and re-layouts  21.1 us (16%)
    pallas_call x17, Pallas kernels, call(): pl.pallas_call(kernel, in_specs=in_specs, out_specs=out_specs, out_shape=...  31.5 us
    unnamed x8, local copies, waits for them, and re-layouts  21.1 us
    ppermute x9, waiting for transfers between devices, swap_col(): return lax.ppermute(x, 'col', [(i, i ^ step) for i in range(n)])  17.1 us
    ppermute x9, starting transfers between devices, swap_col(): return lax.ppermute(x, 'col', [(i, i ^ step) for i in range(n)])  13.9 us
    ppermute x6, waiting for transfers between devices, swap_outer(): return lax.ppermute(x, 'row', [(i, i ^ step * inner) for i in range(n)])  11.3 us
    ppermute x5, waiting for transfers between devices, swap(): lax.ppermute(x, axis, [(i, i ^ step) for i in range(lax.axis_size(axis))])  9.24 us
    ppermute x6, starting transfers between devices, swap_outer(): return lax.ppermute(x, 'row', [(i, i ^ step * inner) for i in range(n)])  8.91 us
    ppermute x5, starting transfers between devices, transpose(): return lax.ppermute(x, ('row', 'col'), pairs)  6.51 us
  transfers between devices with their start and end apart: 34, of which 12 were waited for; matrix products, arithmetic and copies ran while one was open for 0% of the time, Pallas kernels for 10%

profile of v3, /device:TPU:0, one launch (start us, length us, event | category | flops | bytes accessed | tf_op | source)
XLA Modules:
  0.0 131.1 jit_solution(3225150325402175292)
XLA Ops:
  0.6 3.0 %collective-permute-start = (bf16[32,1024]{1,0:T(8,128)(2,1)}, bf16[32,1024]{1,0:T(8,128)(2,1)S(1)}, u32[]{:S(2)}, u32[]{:S(2)}) collective-permute-start(bf16[32,1024]{1,0:T(8,128)(2,1)} %refs_1_.1), channel_id=1, source_target_pairs={{0,1},{1,0},{2,3},{3,2},{4,5},{5,4},{6,7},{7,6},{8,9},{9,8},{10,11... | collective-permute-start | bytes 196616 | tf_op jit(solution)/shard_map/ppermute | solution.py:83
  3.6 1.5 %collective-permute-start.2 = (bf16[32,1024]{1,0:T(8,128)(2,1)}, bf16[32,1024]{1,0:T(8,128)(2,1)S(1)}, u32[]{:S(2)}, u32[]{:S(2)}) collective-permute-start(bf16[32,1024]{1,0:T(8,128)(2,1)} %refs_1_.1), channel_id=1, source_target_pairs={{0,3},{1,2},{2,1},{3,0},{4,7},{5,6},{6,5},{7,4},{8,11},{9,10},{10,... | collective-permute-start | bytes 196616 | tf_op jit(solution)/shard_map/ppermute | solution.py:83
  5.1 0.0 collective-permute-start.1
  5.2 3.4 %hold_weight.1 = (bf16[1024,4096]{1,0:T(8,128)(2,1)S(1)}, bf16[32,1024]{1,0:T(8,128)(2,1)S(1)}, f32[1,4096]{1,0:T(1,128)S(1)}) custom-call(bf16[1024,4096]{1,0:T(8,128)(2,1)} %refs_0_.3, bf16[32,1024]{1,0:T(8,128)(2,1)} %refs_1_.1, f32[1,4096]{1,0:T(1,128)} %bitcast.7), custom_call_target="tpu_custom_call" | custom-call | bytes 8388608 | tf_op jit(solution)/shard_map/hold_weight/pallas_call | solution.py:118
  8.6 0.5 collective-permute-done.2.refs_3_
  9.1 0.8 collective-permute-done.1.refs_2_
  9.9 0.8 preact_part.2
  10.6 0.1 collective-permute-start.3
  10.7 0.8 preact_part.3.refs_1_
  11.5 1.9 %collective-permute-done.3.refs_0_ = f32[128,2048]{1,0:T(8,128)S(1)} collective-permute-done((f32[128,2048]{1,0:T(8,128)S(1)}, f32[128,2048]{1,0:T(8,128)S(1)}, u32[]{:S(2)}, u32[]{:S(2)}) %collective-permute-start.3) | collective-permute-done | bytes 1048608 | tf_op jit(solution)/shard_map/ppermute | solution.py:92
  13.4 0.1 scatter.1
  13.5 3.7 %collective-permute-start.4 = (f32[128,512]{1,0:T(8,128)S(1)}, f32[128,512]{1,0:T(8,128)S(1)}, u32[]{:S(2)}, u32[]{:S(2)}) collective-permute-start(f32[128,512]{1,0:T(8,128)S(1)} %get-tuple-element.25), channel_id=1, source_target_pairs={{0,24},{4,28},{8,16},{12,20},{16,8},{20,12},{24,0},{28,4},{1,25},{... | collective-permute-start | bytes 786440 | tf_op jit(solution)/shard_map/ppermute | solution.py:88
  17.1 0.0 collective-permute-start.5
  17.1 0.8 collective-permute-start.6
  17.9 10.5 %copy-done = f32[2048,4096]{1,0:T(8,128)S(1)} copy-done((f32[2048,4096]{1,0:T(8,128)S(1)}, f32[2048,4096]{1,0:T(8,128)}, u32[]{:S(2)}) %copy-start) | copy-done | bytes 33554456
  28.5 11.3 %collective-permute-done.5.refs_2_ = f32[128,512]{1,0:T(8,128)S(1)} collective-permute-done((f32[128,512]{1,0:T(8,128)S(1)}, f32[128,512]{1,0:T(8,128)S(1)}, u32[]{:S(2)}, u32[]{:S(2)}) %collective-permute-start.5) | collective-permute-done | bytes 262176 | tf_op jit(solution)/shard_map/ppermute | solution.py:88
  39.8 0.1 features.1.refs_0_
  39.8 2.5 %collective-permute-start.13 = (bf16[128,512]{1,0:T(8,128)(2,1)S(1)}, bf16[128,512]{1,0:T(8,128)(2,1)S(1)}, u32[]{:S(2)}, u32[]{:S(2)}) collective-permute-start(bf16[128,512]{1,0:T(8,128)(2,1)S(1)} %features.1.refs_0_), channel_id=1, source_target_pairs={{0,24},{4,28},{8,16},{12,20},{16,8},{20,12},{24,0},{28,4},{1,25},{... | collective-permute-start | bytes 393224 | tf_op jit(solution)/shard_map/ppermute | solution.py:88
  42.4 0.0 collective-permute-start.11
  42.4 1.9 %collective-permute-start.9 = (bf16[128,512]{1,0:T(8,128)(2,1)S(1)}, bf16[128,512]{1,0:T(8,128)(2,1)S(1)}, u32[]{:S(2)}, u32[]{:S(2)}) collective-permute-start(bf16[128,512]{1,0:T(8,128)(2,1)S(1)} %features.1.refs_0_), channel_id=1, source_target_pairs={{0,8},{4,12},{8,0},{12,4},{16,24},{20,28},{24,16},{28,20},{1,9},{5... | collective-permute-start | bytes 393224 | tf_op jit(solution)/shard_map/ppermute | solution.py:88
  44.3 10.5 %copy-done.1 = f32[2048,4096]{1,0:T(8,128)S(1)} copy-done((f32[2048,4096]{1,0:T(8,128)S(1)}, f32[2048,4096]{1,0:T(8,128)}, u32[]{:S(2)}) %copy-start.1) | copy-done | bytes 33554456
  54.8 1.3 panel_part.3
  56.1 0.0 collective-permute-done.13.refs_2_
  56.1 0.6 collective-permute-start.14
  56.7 0.0 collective-permute-done.11.refs_1_
  56.7 0.1 collective-permute-start.12
  56.8 0.4 collective-permute-start.10
  57.2 3.4 %panel_part.4.refs_4_ = f32[2048,128]{1,0:T(8,128)S(1)} custom-call(f32[2048,4096]{1,0:T(8,128)S(1)} %copy-done.1, bf16[128,512]{1,0:T(8,128)(2,1)S(1)} %collective-permute-done.9.refs_0_, bf16[128,512]{1,0:T(8,128)(2,1)S(1)} %collective-permute-done.11.refs_1_, bf16[128,512]{1,0:T(8,128)(2,1)S(1)} %collective-permute-done.13.refs_2_, ...), custom_call_target="tpu_custom_call" | custom-call | flops 1610612736 | bytes 12582912 | tf_op jit(solution)/shard_map/panel_part/pallas_call | solution.py:118
  60.6 0.0 collective-permute-done.14.refs_3_
  60.6 4.5 %panel_part.5 = (f32[512,128]{1,0:T(8,128)S(1)}, f32[512,128]{1,0:T(8,128)S(1)}, f32[512,128]{1,0:T(8,128)S(1)}, f32[512,128]{1,0:T(8,128)S(1)}) custom-call(f32[2048,4096]{1,0:T(8,128)S(1)} %copy-done.1, bf16[128,512]{1,0:T(8,128)(2,1)S(1)} %collective-permute-done.8.refs_0_, bf16[128,512]{1,0:T(8,128)(2,1)S(1)} %collective-permute-done.10.refs_1_, ...), custom_call_target="tpu_custom_call" | custom-call | flops 2147483648 | bytes 16777216 | tf_op jit(solution)/shard_map/panel_part/pallas_call | solution.py:118
  65.2 1.3 collective-permute-start.15
  66.5 1.0 collective-permute-start.16
  67.5 1.2 collective-permute-start.17
  68.7 0.7 collective-permute-start.7
  69.4 5.0 %collective-permute-done.15.refs_1_ = f32[512,128]{1,0:T(8,128)S(1)} collective-permute-done((f32[512,128]{1,0:T(8,128)S(1)}, f32[512,128]{1,0:T(8,128)S(1)}, u32[]{:S(2)}, u32[]{:S(2)}) %collective-permute-start.15) | collective-permute-done | bytes 262176 | tf_op jit(solution)/shard_map/ppermute | solution.py:83
  74.4 7.0 %collective-permute-done.16.refs_2_ = f32[512,128]{1,0:T(8,128)S(1)} collective-permute-done((f32[512,128]{1,0:T(8,128)S(1)}, f32[512,128]{1,0:T(8,128)S(1)}, u32[]{:S(2)}, u32[]{:S(2)}) %collective-permute-start.16) | collective-permute-done | bytes 262176 | tf_op jit(solution)/shard_map/ppermute | solution.py:83
  81.4 2.1 %collective-permute-done.17.refs_3_ = f32[512,128]{1,0:T(8,128)S(1)} collective-permute-done((f32[512,128]{1,0:T(8,128)S(1)}, f32[512,128]{1,0:T(8,128)S(1)}, u32[]{:S(2)}, u32[]{:S(2)}) %collective-permute-start.17) | collective-permute-done | bytes 262176 | tf_op jit(solution)/shard_map/ppermute | solution.py:83
  83.5 0.4 gram_part.1
  83.9 0.1 collective-permute-start.18
  84.0 3.4 %collective-permute-start.29 = (bf16[512,128]{1,0:T(8,128)(2,1)S(1)}, bf16[512,128]{1,0:T(8,128)(2,1)S(1)}, u32[]{:S(2)}, u32[]{:S(2)}) collective-permute-start(bf16[512,128]{1,0:T(8,128)(2,1)S(1)} %get-tuple-element.35.refs_4_), channel_id=1, source_target_pairs={{0,3},{1,2},{2,1},{3,0},{4,7},{5,6},{6,5},{7,4},{8,11},{9,10},{10,... | collective-permute-start | bytes 393224 | tf_op jit(solution)/shard_map/ppermute | solution.py:83
  87.4 0.0 collective-permute-start.28
  87.4 0.0 collective-permute-done.18.y_ref
  87.4 0.1 collective-permute-start.19
  87.5 3.5 %collective-permute-start.26 = (bf16[512,128]{1,0:T(8,128)(2,1)S(1)}, bf16[512,128]{1,0:T(8,128)(2,1)S(1)}, u32[]{:S(2)}, u32[]{:S(2)}) collective-permute-start(bf16[512,128]{1,0:T(8,128)(2,1)S(1)} %get-tuple-element.35.refs_4_), channel_id=1, source_target_pairs={{0,24},{1,16},{2,8},{3,0},{4,28},{5,20},{6,12},{7,4},{8,25},{9,17}... | collective-permute-start | bytes 393224 | tf_op jit(solution)/shard_map/ppermute | solution.py:103
  91.0 0.8 collective-permute-done.19.y_ref
  91.8 2.1 %collective-permute-start.20 = (f32[136,128]{1,0:T(8,128)S(1)}, f32[136,128]{1,0:T(8,128)S(1)}, u32[]{:S(2)}, u32[]{:S(2)}) collective-permute-start(f32[136,128]{1,0:T(8,128)S(1)} %join.6.x_ref), channel_id=1, source_target_pairs={{0,16},{4,20},{8,24},{12,28},{16,0},{20,4},{24,8},{28,12},{1,17},{... | collective-permute-start | bytes 208904 | tf_op jit(solution)/shard_map/ppermute | solution.py:345
  93.9 0.9 collective-permute-start.25
  94.8 0.6 collective-permute-start.24
  95.4 1.7 %collective-permute-done.28.refs_5_.refs_6_ = bf16[512,128]{1,0:T(8,128)(2,1)S(1)} collective-permute-done((bf16[512,128]{1,0:T(8,128)(2,1)S(1)}, bf16[512,128]{1,0:T(8,128)(2,1)S(1)}, u32[]{:S(2)}, u32[]{:S(2)}) %collective-permute-start.28) | collective-permute-done | bytes 131104 | tf_op jit(solution)/shard_map/ppermute | solution.py:83
  97.2 0.8 collective-permute-start.23
  98.0 2.3 %collective-permute-start.27 = (bf16[512,128]{1,0:T(8,128)(2,1)S(1)}, bf16[512,128]{1,0:T(8,128)(2,1)S(1)}, u32[]{:S(2)}, u32[]{:S(2)}) collective-permute-start(bf16[512,128]{1,0:T(8,128)(2,1)S(1)} %get-tuple-element.35.refs_4_), channel_id=1, source_target_pairs={{0,1},{1,0},{2,3},{3,2},{4,5},{5,4},{6,7},{7,6},{8,9},{9,8},{10,11... | collective-permute-start | bytes 393224 | tf_op jit(solution)/shard_map/ppermute | solution.py:83
  100.4 0.0 copy-start.3
  100.4 0.0 collective-permute-done.26.refs_3_.refs_11_
  100.4 0.1 collective-permute-start.21
  100.5 0.1 collective-permute-start.33
  100.6 1.0 collective-permute-done.24.refs_1_.refs_9_
  101.6 0.0 collective-permute-start.32
  101.6 0.5 collective-permute-start.31
  102.1 6.0 %collective-permute-done.21.y_ref = f32[136,128]{1,0:T(8,128)S(1)} collective-permute-done((f32[136,128]{1,0:T(8,128)S(1)}, f32[136,128]{1,0:T(8,128)S(1)}, u32[]{:S(2)}, u32[]{:S(2)}) %collective-permute-start.21) | collective-permute-done | bytes 69664 | tf_op jit(solution)/shard_map/ppermute | solution.py:345
  108.1 3.6 %collective-permute-start.22 = (f32[136,128]{1,0:T(8,128)S(1)}, f32[136,128]{1,0:T(8,128)S(1)}, u32[]{:S(2)}, u32[]{:S(2)}) collective-permute-start(f32[136,128]{1,0:T(8,128)S(1)} %join.8.x_ref), channel_id=1, source_target_pairs={{0,2},{1,3},{2,0},{3,1},{4,6},{5,7},{6,4},{7,5},{8,10},{9,11},{10,... | collective-permute-start | bytes 208904 | tf_op jit(solution)/shard_map/ppermute | solution.py:345
  111.7 2.4 %collective-permute-done.22.y_ref = f32[136,128]{1,0:T(8,128)S(1)} collective-permute-done((f32[136,128]{1,0:T(8,128)S(1)}, f32[136,128]{1,0:T(8,128)S(1)}, u32[]{:S(2)}, u32[]{:S(2)}) %collective-permute-start.22) | collective-permute-done | bytes 69664 | tf_op jit(solution)/shard_map/ppermute | solution.py:345
  114.2 4.1 %inverse.1 = (f32[128,128]{1,0:T(8,128)S(1)}, f32[8,128]{1,0:T(8,128)S(1)}) custom-call(f32[2048,4096]{1,0:T(8,128)S(1)} %copy-done.1, f32[136,128]{1,0:T(8,128)S(1)} %join.9.gram_ref, f32[1,128]{1,0:T(1,128)S(1)} %bitcast.6), custom_call_target="tpu_custom_call" | custom-call | tf_op jit(solution)/shard_map/inverse/pallas_call | solution.py:118
  118.3 0.0 collective-permute-done.31.refs_13_
  118.3 12.6 %update.1 = (f32[2048,4096]{1,0:T(8,128)}, f32[1,2048]{1,0:T(1,128)}) custom-call(f32[2048,4096]{1,0:T(8,128)S(1)} %copy-done.1, f32[128,128]{1,0:T(8,128)S(1)} %get-tuple-element.36.refs_1_, f32[8,128]{1,0:T(8,128)S(1)} %get-tuple-element.37.refs_2_, f32[1,2048]{1,0:T(1,128)S(1)} %bitcast.5, bf16[512,128]{1,0:T(8,128)(2,1)S(1)} %get-tuple-element.35.refs_4_, ...), custom_call_target="tpu_custom_call" | custom-call | tf_op jit(solution)/shard_map/update/pallas_call | solution.py:118
  (29 shorter events, 0.1 us)
Async XLA Ops:
  0.6 8.0 %collective-permute-start = (bf16[32,1024]{1,0:T(8,128)(2,1)}, bf16[32,1024]{1,0:T(8,128)(2,1)S(1)}, u32[]{:S(2)}, u32[]{:S(2)}) collective-permute-start(bf16[32,1024]{1,0:T(8,128)(2,1)} %refs_1_.1), channel_id=1, source_target_pairs={{0,1},{1,0},{2,3},{3,2},{4,5},{5,4},{6,7},{7,6},{8,9},{9,8},{10,11... | collective-permute-start | bytes 196616 | tf_op jit(solution)/shard_map/ppermute | solution.py:83
  3.6 5.4 %collective-permute-start.2 = (bf16[32,1024]{1,0:T(8,128)(2,1)}, bf16[32,1024]{1,0:T(8,128)(2,1)S(1)}, u32[]{:S(2)}, u32[]{:S(2)}) collective-permute-start(bf16[32,1024]{1,0:T(8,128)(2,1)} %refs_1_.1), channel_id=1, source_target_pairs={{0,3},{1,2},{2,1},{3,0},{4,7},{5,6},{6,5},{7,4},{8,11},{9,10},{10,... | collective-permute-start | bytes 196616 | tf_op jit(solution)/shard_map/ppermute | solution.py:83
  5.1 4.7 %collective-permute-start.1 = (bf16[32,1024]{1,0:T(8,128)(2,1)}, bf16[32,1024]{1,0:T(8,128)(2,1)S(1)}, u32[]{:S(2)}, u32[]{:S(2)}) collective-permute-start(bf16[32,1024]{1,0:T(8,128)(2,1)} %refs_1_.1), channel_id=1, source_target_pairs={{0,2},{1,3},{2,0},{3,1},{4,6},{5,7},{6,4},{7,5},{8,10},{9,11},{10,... | collective-permute-start | bytes 196616 | tf_op jit(solution)/shard_map/ppermute | solution.py:83
  10.6 2.7 %collective-permute-start.3 = (f32[128,2048]{1,0:T(8,128)S(1)}, f32[128,2048]{1,0:T(8,128)S(1)}, u32[]{:S(2)}, u32[]{:S(2)}) collective-permute-start(f32[128,2048]{1,0:T(8,128)S(1)} %preact_part.2), channel_id=1, source_target_pairs={{0,4},{4,0},{8,12},{12,8},{16,20},{20,16},{24,28},{28,24},{1,5},{5... | collective-permute-start | bytes 3145736 | tf_op jit(solution)/shard_map/ppermute | solution.py:92
  13.5 15.0 %collective-permute-start.4 = (f32[128,512]{1,0:T(8,128)S(1)}, f32[128,512]{1,0:T(8,128)S(1)}, u32[]{:S(2)}, u32[]{:S(2)}) collective-permute-start(f32[128,512]{1,0:T(8,128)S(1)} %get-tuple-element.25), channel_id=1, source_target_pairs={{0,24},{4,28},{8,16},{12,20},{16,8},{20,12},{24,0},{28,4},{1,25},{... | collective-permute-start | bytes 786440 | tf_op jit(solution)/shard_map/ppermute | solution.py:88
  17.1 22.6 %collective-permute-start.5 = (f32[128,512]{1,0:T(8,128)S(1)}, f32[128,512]{1,0:T(8,128)S(1)}, u32[]{:S(2)}, u32[]{:S(2)}) collective-permute-start(f32[128,512]{1,0:T(8,128)S(1)} %get-tuple-element.26), channel_id=1, source_target_pairs={{0,16},{4,20},{8,24},{12,28},{16,0},{20,4},{24,8},{28,12},{1,17},{... | collective-permute-start | bytes 786440 | tf_op jit(solution)/shard_map/ppermute | solution.py:88
  17.1 22.6 %collective-permute-start.6 = (f32[128,512]{1,0:T(8,128)S(1)}, f32[128,512]{1,0:T(8,128)S(1)}, u32[]{:S(2)}, u32[]{:S(2)}) collective-permute-start(f32[128,512]{1,0:T(8,128)S(1)} %get-tuple-element.27), channel_id=1, source_target_pairs={{0,8},{4,12},{8,0},{12,4},{16,24},{20,28},{24,16},{28,20},{1,9},{5... | collective-permute-start | bytes 786440 | tf_op jit(solution)/shard_map/ppermute | solution.py:88
  17.9 10.5 %copy-start = (f32[2048,4096]{1,0:T(8,128)S(1)}, f32[2048,4096]{1,0:T(8,128)}, u32[]{:S(2)}) copy-start(f32[2048,4096]{1,0:T(8,128)} %refs_0_.5) | copy-start | bytes 100663296
  39.8 16.3 %collective-permute-start.13 = (bf16[128,512]{1,0:T(8,128)(2,1)S(1)}, bf16[128,512]{1,0:T(8,128)(2,1)S(1)}, u32[]{:S(2)}, u32[]{:S(2)}) collective-permute-start(bf16[128,512]{1,0:T(8,128)(2,1)S(1)} %features.1.refs_0_), channel_id=1, source_target_pairs={{0,24},{4,28},{8,16},{12,20},{16,8},{20,12},{24,0},{28,4},{1,25},{... | collective-permute-start | bytes 393224 | tf_op jit(solution)/shard_map/ppermute | solution.py:88
  42.4 14.3 %collective-permute-start.11 = (bf16[128,512]{1,0:T(8,128)(2,1)S(1)}, bf16[128,512]{1,0:T(8,128)(2,1)S(1)}, u32[]{:S(2)}, u32[]{:S(2)}) collective-permute-start(bf16[128,512]{1,0:T(8,128)(2,1)S(1)} %features.1.refs_0_), channel_id=1, source_target_pairs={{0,16},{4,20},{8,24},{12,28},{16,0},{20,4},{24,8},{28,12},{1,17},{... | collective-permute-start | bytes 393224 | tf_op jit(solution)/shard_map/ppermute | solution.py:88
  42.4 14.4 %collective-permute-start.9 = (bf16[128,512]{1,0:T(8,128)(2,1)S(1)}, bf16[128,512]{1,0:T(8,128)(2,1)S(1)}, u32[]{:S(2)}, u32[]{:S(2)}) collective-permute-start(bf16[128,512]{1,0:T(8,128)(2,1)S(1)} %features.1.refs_0_), channel_id=1, source_target_pairs={{0,8},{4,12},{8,0},{12,4},{16,24},{20,28},{24,16},{28,20},{1,9},{5... | collective-permute-start | bytes 393224 | tf_op jit(solution)/shard_map/ppermute | solution.py:88
  44.3 16.3 %collective-permute-start.8 = (bf16[128,512]{1,0:T(8,128)(2,1)S(1)}, bf16[128,512]{1,0:T(8,128)(2,1)S(1)}, u32[]{:S(2)}, u32[]{:S(2)}) collective-permute-start(bf16[128,512]{1,0:T(8,128)(2,1)S(1)} %features.1.refs_0_), channel_id=1, source_target_pairs={{0,4},{4,0},{8,12},{12,8},{16,20},{20,16},{24,28},{28,24},{1,5},{5... | collective-permute-start | bytes 393224 | tf_op jit(solution)/shard_map/ppermute | solution.py:92
  44.3 10.5 %copy-start.1 = (f32[2048,4096]{1,0:T(8,128)S(1)}, f32[2048,4096]{1,0:T(8,128)}, u32[]{:S(2)}) copy-start(f32[2048,4096]{1,0:T(8,128)} %refs_0_.5) | copy-start | bytes 100663296
  56.1 4.5 %collective-permute-start.14 = (bf16[128,512]{1,0:T(8,128)(2,1)S(1)}, bf16[128,512]{1,0:T(8,128)(2,1)S(1)}, u32[]{:S(2)}, u32[]{:S(2)}) collective-permute-start(bf16[128,512]{1,0:T(8,128)(2,1)S(1)} %collective-permute-done.13.refs_2_), channel_id=1, source_target_pairs={{0,4},{4,0},{8,12},{12,8},{16,20},{20,16},{24,28},{28,24},{1,5},{5... | collective-permute-start | bytes 393224 | tf_op jit(solution)/shard_map/ppermute | solution.py:92
  56.7 4.0 %collective-permute-start.12 = (bf16[128,512]{1,0:T(8,128)(2,1)S(1)}, bf16[128,512]{1,0:T(8,128)(2,1)S(1)}, u32[]{:S(2)}, u32[]{:S(2)}) collective-permute-start(bf16[128,512]{1,0:T(8,128)(2,1)S(1)} %collective-permute-done.11.refs_1_), channel_id=1, source_target_pairs={{0,4},{4,0},{8,12},{12,8},{16,20},{20,16},{24,28},{28,24},{1,5},{5... | collective-permute-start | bytes 393224 | tf_op jit(solution)/shard_map/ppermute | solution.py:92
  56.8 3.9 %collective-permute-start.10 = (bf16[128,512]{1,0:T(8,128)(2,1)S(1)}, bf16[128,512]{1,0:T(8,128)(2,1)S(1)}, u32[]{:S(2)}, u32[]{:S(2)}) collective-permute-start(bf16[128,512]{1,0:T(8,128)(2,1)S(1)} %collective-permute-done.9.refs_0_), channel_id=1, source_target_pairs={{0,4},{4,0},{8,12},{12,8},{16,20},{20,16},{24,28},{28,24},{1,5},{5... | collective-permute-start | bytes 393224 | tf_op jit(solution)/shard_map/ppermute | solution.py:92
  57.2 26.3 %copy-start.2 = (f32[2048]{0:T(1024)S(1)}, f32[2048]{0:T(1024)}, u32[]{:S(2)}) copy-start(f32[2048]{0:T(1024)} %param.10) | copy-start | bytes 24580
  65.2 9.2 %collective-permute-start.15 = (f32[512,128]{1,0:T(8,128)S(1)}, f32[512,128]{1,0:T(8,128)S(1)}, u32[]{:S(2)}, u32[]{:S(2)}) collective-permute-start(f32[512,128]{1,0:T(8,128)S(1)} %get-tuple-element.31), channel_id=1, source_target_pairs={{0,1},{1,0},{2,3},{3,2},{4,5},{5,4},{6,7},{7,6},{8,9},{9,8},{10,11... | collective-permute-start | bytes 786440 | tf_op jit(solution)/shard_map/ppermute | solution.py:83
  66.5 15.0 %collective-permute-start.16 = (f32[512,128]{1,0:T(8,128)S(1)}, f32[512,128]{1,0:T(8,128)S(1)}, u32[]{:S(2)}, u32[]{:S(2)}) collective-permute-start(f32[512,128]{1,0:T(8,128)S(1)} %get-tuple-element.32), channel_id=1, source_target_pairs={{0,2},{1,3},{2,0},{3,1},{4,6},{5,7},{6,4},{7,5},{8,10},{9,11},{10,... | collective-permute-start | bytes 786440 | tf_op jit(solution)/shard_map/ppermute | solution.py:83
  67.5 16.0 %collective-permute-start.17 = (f32[512,128]{1,0:T(8,128)S(1)}, f32[512,128]{1,0:T(8,128)S(1)}, u32[]{:S(2)}, u32[]{:S(2)}) collective-permute-start(f32[512,128]{1,0:T(8,128)S(1)} %get-tuple-element.33), channel_id=1, source_target_pairs={{0,3},{1,2},{2,1},{3,0},{4,7},{5,6},{6,5},{7,4},{8,11},{9,10},{10,... | collective-permute-start | bytes 786440 | tf_op jit(solution)/shard_map/ppermute | solution.py:83
  68.7 0.7 collective-permute-start.7
  83.9 3.5 %collective-permute-start.18 = (f32[136,128]{1,0:T(8,128)S(1)}, f32[136,128]{1,0:T(8,128)S(1)}, u32[]{:S(2)}, u32[]{:S(2)}) collective-permute-start(f32[136,128]{1,0:T(8,128)S(1)} %get-tuple-element.34.x_ref), channel_id=1, source_target_pairs={{0,4},{4,0},{8,12},{12,8},{16,20},{20,16},{24,28},{28,24},{1,5},{5... | collective-permute-start | bytes 208904 | tf_op jit(solution)/shard_map/ppermute | solution.py:345
  84.0 10.8 %collective-permute-start.29 = (bf16[512,128]{1,0:T(8,128)(2,1)S(1)}, bf16[512,128]{1,0:T(8,128)(2,1)S(1)}, u32[]{:S(2)}, u32[]{:S(2)}) collective-permute-start(bf16[512,128]{1,0:T(8,128)(2,1)S(1)} %get-tuple-element.35.refs_4_), channel_id=1, source_target_pairs={{0,3},{1,2},{2,1},{3,0},{4,7},{5,6},{6,5},{7,4},{8,11},{9,10},{10,... | collective-permute-start | bytes 393224 | tf_op jit(solution)/shard_map/ppermute | solution.py:83
  87.4 9.8 %collective-permute-start.28 = (bf16[512,128]{1,0:T(8,128)(2,1)S(1)}, bf16[512,128]{1,0:T(8,128)(2,1)S(1)}, u32[]{:S(2)}, u32[]{:S(2)}) collective-permute-start(bf16[512,128]{1,0:T(8,128)(2,1)S(1)} %get-tuple-element.35.refs_4_), channel_id=1, source_target_pairs={{0,2},{1,3},{2,0},{3,1},{4,6},{5,7},{6,4},{7,5},{8,10},{9,11},{10,... | collective-permute-start | bytes 393224 | tf_op jit(solution)/shard_map/ppermute | solution.py:83
  87.4 4.4 %collective-permute-start.19 = (f32[136,128]{1,0:T(8,128)S(1)}, f32[136,128]{1,0:T(8,128)S(1)}, u32[]{:S(2)}, u32[]{:S(2)}) collective-permute-start(f32[136,128]{1,0:T(8,128)S(1)} %join.5.x_ref), channel_id=1, source_target_pairs={{0,8},{4,12},{8,0},{12,4},{16,24},{20,28},{24,16},{28,20},{1,9},{5... | collective-permute-start | bytes 208904 | tf_op jit(solution)/shard_map/ppermute | solution.py:345
  87.5 12.9 %collective-permute-start.26 = (bf16[512,128]{1,0:T(8,128)(2,1)S(1)}, bf16[512,128]{1,0:T(8,128)(2,1)S(1)}, u32[]{:S(2)}, u32[]{:S(2)}) collective-permute-start(bf16[512,128]{1,0:T(8,128)(2,1)S(1)} %get-tuple-element.35.refs_4_), channel_id=1, source_target_pairs={{0,24},{1,16},{2,8},{3,0},{4,28},{5,20},{6,12},{7,4},{8,25},{9,17}... | collective-permute-start | bytes 393224 | tf_op jit(solution)/shard_map/ppermute | solution.py:103
  91.8 6.2 %collective-permute-start.20 = (f32[136,128]{1,0:T(8,128)S(1)}, f32[136,128]{1,0:T(8,128)S(1)}, u32[]{:S(2)}, u32[]{:S(2)}) collective-permute-start(f32[136,128]{1,0:T(8,128)S(1)} %join.6.x_ref), channel_id=1, source_target_pairs={{0,16},{4,20},{8,24},{12,28},{16,0},{20,4},{24,8},{28,12},{1,17},{... | collective-permute-start | bytes 208904 | tf_op jit(solution)/shard_map/ppermute | solution.py:345
  93.9 6.6 %collective-permute-start.25 = (bf16[512,128]{1,0:T(8,128)(2,1)S(1)}, bf16[512,128]{1,0:T(8,128)(2,1)S(1)}, u32[]{:S(2)}, u32[]{:S(2)}) collective-permute-start(bf16[512,128]{1,0:T(8,128)(2,1)S(1)} %get-tuple-element.35.refs_4_), channel_id=1, source_target_pairs={{0,16},{1,24},{2,0},{3,8},{4,20},{5,28},{6,4},{7,12},{8,17},{9,25}... | collective-permute-start | bytes 393224 | tf_op jit(solution)/shard_map/ppermute | solution.py:103
  94.8 6.8 %collective-permute-start.24 = (bf16[512,128]{1,0:T(8,128)(2,1)S(1)}, bf16[512,128]{1,0:T(8,128)(2,1)S(1)}, u32[]{:S(2)}, u32[]{:S(2)}) collective-permute-start(bf16[512,128]{1,0:T(8,128)(2,1)S(1)} %get-tuple-element.35.refs_4_), channel_id=1, source_target_pairs={{0,8},{1,0},{2,24},{3,16},{4,12},{5,4},{6,28},{7,20},{8,9},{9,1},{... | collective-permute-start | bytes 393224 | tf_op jit(solution)/shard_map/ppermute | solution.py:103
  97.2 4.4 %collective-permute-start.23 = (bf16[512,128]{1,0:T(8,128)(2,1)S(1)}, bf16[512,128]{1,0:T(8,128)(2,1)S(1)}, u32[]{:S(2)}, u32[]{:S(2)}) collective-permute-start(bf16[512,128]{1,0:T(8,128)(2,1)S(1)} %get-tuple-element.35.refs_4_), channel_id=1, source_target_pairs={{0,0},{1,8},{2,16},{3,24},{4,4},{5,12},{6,20},{7,28},{8,1},{9,9},{... | collective-permute-start | bytes 393224 | tf_op jit(solution)/shard_map/ppermute | solution.py:103
  98.0 10.1 %collective-permute-start.27 = (bf16[512,128]{1,0:T(8,128)(2,1)S(1)}, bf16[512,128]{1,0:T(8,128)(2,1)S(1)}, u32[]{:S(2)}, u32[]{:S(2)}) collective-permute-start(bf16[512,128]{1,0:T(8,128)(2,1)S(1)} %get-tuple-element.35.refs_4_), channel_id=1, source_target_pairs={{0,1},{1,0},{2,3},{3,2},{4,5},{5,4},{6,7},{7,6},{8,9},{9,8},{10,11... | collective-permute-start | bytes 393224 | tf_op jit(solution)/shard_map/ppermute | solution.py:83
  100.4 13.8 %copy-start.3 = (f32[128]{0:T(128)S(1)}, f32[128]{0:T(128)}, u32[]{:S(2)}) copy-start(f32[128]{0:T(128)} %param.11) | copy-start | bytes 1540
  100.4 7.7 %collective-permute-start.21 = (f32[136,128]{1,0:T(8,128)S(1)}, f32[136,128]{1,0:T(8,128)S(1)}, u32[]{:S(2)}, u32[]{:S(2)}) collective-permute-start(f32[136,128]{1,0:T(8,128)S(1)} %join.7.x_ref), channel_id=1, source_target_pairs={{0,1},{1,0},{2,3},{3,2},{4,5},{5,4},{6,7},{7,6},{8,9},{9,8},{10,11... | collective-permute-start | bytes 208904 | tf_op jit(solution)/shard_map/ppermute | solution.py:345
  100.5 17.8 %collective-permute-start.33 = (bf16[512,128]{1,0:T(8,128)(2,1)S(1)}, bf16[512,128]{1,0:T(8,128)(2,1)S(1)}, u32[]{:S(2)}, u32[]{:S(2)}) collective-permute-start(bf16[512,128]{1,0:T(8,128)(2,1)S(1)} %collective-permute-done.26.refs_3_.refs_11_), channel_id=1, source_target_pairs={{0,4},{4,0},{8,12},{12,8},{16,20},{20,16},{24,28},{28,24},{1,5},{5... | collective-permute-start | bytes 393224 | tf_op jit(solution)/shard_map/ppermute | solution.py:92
  101.6 16.7 %collective-permute-start.32 = (bf16[512,128]{1,0:T(8,128)(2,1)S(1)}, bf16[512,128]{1,0:T(8,128)(2,1)S(1)}, u32[]{:S(2)}, u32[]{:S(2)}) collective-permute-start(bf16[512,128]{1,0:T(8,128)(2,1)S(1)} %collective-permute-done.25.refs_2_.refs_10_), channel_id=1, source_target_pairs={{0,4},{4,0},{8,12},{12,8},{16,20},{20,16},{24,28},{28,24},{1,5},{5... | collective-permute-start | bytes 393224 | tf_op jit(solution)/shard_map/ppermute | solution.py:92
  101.6 16.7 %collective-permute-start.31 = (bf16[512,128]{1,0:T(8,128)(2,1)S(1)}, bf16[512,128]{1,0:T(8,128)(2,1)S(1)}, u32[]{:S(2)}, u32[]{:S(2)}) collective-permute-start(bf16[512,128]{1,0:T(8,128)(2,1)S(1)} %collective-permute-done.24.refs_1_.refs_9_), channel_id=1, source_target_pairs={{0,4},{4,0},{8,12},{12,8},{16,20},{20,16},{24,28},{28,24},{1,5},{5... | collective-permute-start | bytes 393224 | tf_op jit(solution)/shard_map/ppermute | solution.py:92
  108.1 10.2 %collective-permute-start.30 = (bf16[512,128]{1,0:T(8,128)(2,1)S(1)}, bf16[512,128]{1,0:T(8,128)(2,1)S(1)}, u32[]{:S(2)}, u32[]{:S(2)}) collective-permute-start(bf16[512,128]{1,0:T(8,128)(2,1)S(1)} %collective-permute-done.23.refs_0_.refs_8_), channel_id=1, source_target_pairs={{0,4},{4,0},{8,12},{12,8},{16,20},{20,16},{24,28},{28,24},{1,5},{5... | collective-permute-start | bytes 393224 | tf_op jit(solution)/shard_map/ppermute | solution.py:92
  108.1 6.0 %collective-permute-start.22 = (f32[136,128]{1,0:T(8,128)S(1)}, f32[136,128]{1,0:T(8,128)S(1)}, u32[]{:S(2)}, u32[]{:S(2)}) collective-permute-start(f32[136,128]{1,0:T(8,128)S(1)} %join.8.x_ref), channel_id=1, source_target_pairs={{0,2},{1,3},{2,0},{3,1},{4,6},{5,7},{6,4},{7,5},{8,10},{9,11},{10,... | collective-permute-start | bytes 208904 | tf_op jit(solution)/shard_map/ppermute | solution.py:345

commit v4 on v3

--- a/solution.py
+++ b/solution.py
@@ -423,13 +423,7 @@
         here = span((inner_index ^ (s // cols)) * cols + (outer ^ (s % cols)), quarter)
         other[here, :batch] = part[...]
         other[here, batch:] = part[...]
-    hi, lo = split2(inverse_ref[...])
-    rows = panel[...]
-    product = dot(rows, hi) + dot(rows, lo)
-    hi, lo = split2(product)
-    gain[:, :batch] = hi
-    gain[:, batch:] = lo
-    new_mean_ref[...] = mean_ref[...] + sum(dot(p, rows, NT) for p in split3(coeffs_ref[...]))[:1]
+    inverse = split2(inverse_ref[...])
 
     slots, rows, width = buffers.shape
     across = c_ref.shape[1] // width
@@ -443,10 +437,17 @@
     for n in range(steps):
         here = pl.ds(n // across * rows, rows)
         there = pl.ds(n % across * width, width)
+        if n % across == 0:
+            mine = panel[here, :]
+            hi, lo = split2(sum(dot(mine, piece) for piece in inverse))
+            gain[here, :batch] = hi
+            gain[here, batch:] = lo
         if n >= slots:
             copy(n - slots).wait()
         buffers[n % slots] = c_ref[here, there] - dot(gain[here, :], other[there, :], NT)
         copy(n).start()
+    change = sum(dot(piece, panel[...], NT) for piece in split3(coeffs_ref[...]))
+    new_mean_ref[...] = mean_ref[...] + change[:1]
     for n in range(max(0, steps - slots), steps):
         copy(n).wait()
 

time: 131 us -> 131 us (level)
  no operation moved by 1% of the time
where the time goes in v4:
time: 131 us
  waiting for transfers between devices  40.6 us (31%)
  starting transfers between devices  36.9 us (28%)
  Pallas kernels  31.2 us (24%)
  local copies, waits for them, and re-layouts  21.1 us (16%)
    pallas_call x17, Pallas kernels, call(): pl.pallas_call(kernel, in_specs=in_specs, out_specs=out_specs, out_shape=...  31.2 us
    unnamed x8, local copies, waits for them, and re-layouts  21.1 us
    ppermute x9, waiting for transfers between devices, swap_col(): return lax.ppermute(x, 'col', [(i, i ^ step) for i in range(n)])  17.1 us
    ppermute x9, starting transfers between devices, swap_col(): return lax.ppermute(x, 'col', [(i, i ^ step) for i in range(n)])  13.9 us
    ppermute x6, waiting for transfers between devices, swap_outer(): return lax.ppermute(x, 'row', [(i, i ^ step * inner) for i in range(n)])  11.3 us
    ppermute x5, waiting for transfers between devices, swap(): lax.ppermute(x, axis, [(i, i ^ step) for i in range(lax.axis_size(axis))])  9.24 us
    ppermute x6, starting transfers between devices, swap_outer(): return lax.ppermute(x, 'row', [(i, i ^ step * inner) for i in range(n)])  8.91 us
    ppermute x5, starting transfers between devices, transpose(): return lax.ppermute(x, ('row', 'col'), pairs)  6.51 us
  transfers between devices with their start and end apart: 34, of which 12 were waited for; matrix products, arithmetic and copies ran while one was open for 0% of the time, Pallas kernels for 10%

profile of v4, /device:TPU:0, one launch (start us, length us, event | category | flops | bytes accessed | tf_op | source)
XLA Modules:
  0.0 130.9 jit_solution(359769871038309818)
XLA Ops:
  0.6 3.0 %collective-permute-start = (bf16[32,1024]{1,0:T(8,128)(2,1)}, bf16[32,1024]{1,0:T(8,128)(2,1)S(1)}, u32[]{:S(2)}, u32[]{:S(2)}) collective-permute-start(bf16[32,1024]{1,0:T(8,128)(2,1)} %refs_1_.1), channel_id=1, source_target_pairs={{0,1},{1,0},{2,3},{3,2},{4,5},{5,4},{6,7},{7,6},{8,9},{9,8},{10,11... | collective-permute-start | bytes 196616 | tf_op jit(solution)/shard_map/ppermute | solution.py:83
  3.6 1.5 %collective-permute-start.2 = (bf16[32,1024]{1,0:T(8,128)(2,1)}, bf16[32,1024]{1,0:T(8,128)(2,1)S(1)}, u32[]{:S(2)}, u32[]{:S(2)}) collective-permute-start(bf16[32,1024]{1,0:T(8,128)(2,1)} %refs_1_.1), channel_id=1, source_target_pairs={{0,3},{1,2},{2,1},{3,0},{4,7},{5,6},{6,5},{7,4},{8,11},{9,10},{10,... | collective-permute-start | bytes 196616 | tf_op jit(solution)/shard_map/ppermute | solution.py:83
  5.1 0.0 collective-permute-start.1
  5.2 3.4 %hold_weight.1 = (bf16[1024,4096]{1,0:T(8,128)(2,1)S(1)}, bf16[32,1024]{1,0:T(8,128)(2,1)S(1)}, f32[1,4096]{1,0:T(1,128)S(1)}) custom-call(bf16[1024,4096]{1,0:T(8,128)(2,1)} %refs_0_.3, bf16[32,1024]{1,0:T(8,128)(2,1)} %refs_1_.1, f32[1,4096]{1,0:T(1,128)} %bitcast.7), custom_call_target="tpu_custom_call" | custom-call | bytes 8388608 | tf_op jit(solution)/shard_map/hold_weight/pallas_call | solution.py:118
  8.6 0.0 collective-permute-done.refs_1_
  8.6 0.5 collective-permute-done.2.refs_3_
  9.1 0.8 collective-permute-done.1.refs_2_
  9.9 0.8 preact_part.2
  10.6 0.1 collective-permute-start.3
  10.7 0.8 preact_part.3.refs_1_
  11.5 1.9 %collective-permute-done.3.refs_0_ = f32[128,2048]{1,0:T(8,128)S(1)} collective-permute-done((f32[128,2048]{1,0:T(8,128)S(1)}, f32[128,2048]{1,0:T(8,128)S(1)}, u32[]{:S(2)}, u32[]{:S(2)}) %collective-permute-start.3) | collective-permute-done | bytes 1048608 | tf_op jit(solution)/shard_map/ppermute | solution.py:92
  13.4 0.1 scatter.1
  13.5 3.7 %collective-permute-start.4 = (f32[128,512]{1,0:T(8,128)S(1)}, f32[128,512]{1,0:T(8,128)S(1)}, u32[]{:S(2)}, u32[]{:S(2)}) collective-permute-start(f32[128,512]{1,0:T(8,128)S(1)} %get-tuple-element.25), channel_id=1, source_target_pairs={{0,24},{4,28},{8,16},{12,20},{16,8},{20,12},{24,0},{28,4},{1,25},{... | collective-permute-start | bytes 786440 | tf_op jit(solution)/shard_map/ppermute | solution.py:88
  17.1 0.8 collective-permute-start.6
  17.9 10.5 %copy-done = f32[2048,4096]{1,0:T(8,128)S(1)} copy-done((f32[2048,4096]{1,0:T(8,128)S(1)}, f32[2048,4096]{1,0:T(8,128)}, u32[]{:S(2)}) %copy-start) | copy-done | bytes 33554456
  28.5 0.0 collective-permute-done.4.refs_1_
  28.5 11.3 %collective-permute-done.5.refs_2_ = f32[128,512]{1,0:T(8,128)S(1)} collective-permute-done((f32[128,512]{1,0:T(8,128)S(1)}, f32[128,512]{1,0:T(8,128)S(1)}, u32[]{:S(2)}, u32[]{:S(2)}) %collective-permute-start.5) | collective-permute-done | bytes 262176 | tf_op jit(solution)/shard_map/ppermute | solution.py:88
  39.7 0.0 collective-permute-done.6.refs_3_
  39.8 0.1 features.1.refs_0_
  39.8 2.5 %collective-permute-start.13 = (bf16[128,512]{1,0:T(8,128)(2,1)S(1)}, bf16[128,512]{1,0:T(8,128)(2,1)S(1)}, u32[]{:S(2)}, u32[]{:S(2)}) collective-permute-start(bf16[128,512]{1,0:T(8,128)(2,1)S(1)} %features.1.refs_0_), channel_id=1, source_target_pairs={{0,24},{4,28},{8,16},{12,20},{16,8},{20,12},{24,0},{28,4},{1,25},{... | collective-permute-start | bytes 393224 | tf_op jit(solution)/shard_map/ppermute | solution.py:88
  42.4 0.0 collective-permute-start.11
  42.4 1.9 %collective-permute-start.9 = (bf16[128,512]{1,0:T(8,128)(2,1)S(1)}, bf16[128,512]{1,0:T(8,128)(2,1)S(1)}, u32[]{:S(2)}, u32[]{:S(2)}) collective-permute-start(bf16[128,512]{1,0:T(8,128)(2,1)S(1)} %features.1.refs_0_), channel_id=1, source_target_pairs={{0,8},{4,12},{8,0},{12,4},{16,24},{20,28},{24,16},{28,20},{1,9},{5... | collective-permute-start | bytes 393224 | tf_op jit(solution)/shard_map/ppermute | solution.py:88
  44.3 0.0 collective-permute-start.8
  44.3 10.5 %copy-done.1 = f32[2048,4096]{1,0:T(8,128)S(1)} copy-done((f32[2048,4096]{1,0:T(8,128)S(1)}, f32[2048,4096]{1,0:T(8,128)}, u32[]{:S(2)}) %copy-start.1) | copy-done | bytes 33554456
  54.8 1.3 panel_part.3
  56.1 0.6 collective-permute-start.14
  56.7 0.1 collective-permute-start.12
  56.8 0.0 collective-permute-done.9.refs_0_
  56.8 0.4 collective-permute-start.10
  57.2 3.4 %panel_part.4.refs_4_ = f32[2048,128]{1,0:T(8,128)S(1)} custom-call(f32[2048,4096]{1,0:T(8,128)S(1)} %copy-done.1, bf16[128,512]{1,0:T(8,128)(2,1)S(1)} %collective-permute-done.9.refs_0_, bf16[128,512]{1,0:T(8,128)(2,1)S(1)} %collective-permute-done.11.refs_1_, bf16[128,512]{1,0:T(8,128)(2,1)S(1)} %collective-permute-done.13.refs_2_, ...), custom_call_target="tpu_custom_call" | custom-call | flops 1610612736 | bytes 12582912 | tf_op jit(solution)/shard_map/panel_part/pallas_call | solution.py:118
  60.6 0.0 collective-permute-done.12.refs_2_
  60.6 4.5 %panel_part.5 = (f32[512,128]{1,0:T(8,128)S(1)}, f32[512,128]{1,0:T(8,128)S(1)}, f32[512,128]{1,0:T(8,128)S(1)}, f32[512,128]{1,0:T(8,128)S(1)}) custom-call(f32[2048,4096]{1,0:T(8,128)S(1)} %copy-done.1, bf16[128,512]{1,0:T(8,128)(2,1)S(1)} %collective-permute-done.8.refs_0_, bf16[128,512]{1,0:T(8,128)(2,1)S(1)} %collective-permute-done.10.refs_1_, ...), custom_call_target="tpu_custom_call" | custom-call | flops 2147483648 | bytes 16777216 | tf_op jit(solution)/shard_map/panel_part/pallas_call | solution.py:118
  65.2 1.3 collective-permute-start.15
  66.5 1.0 collective-permute-start.16
  67.5 1.2 collective-permute-start.17
  68.7 0.7 collective-permute-start.7
  69.4 0.0 collective-permute-done.7.phi_ref
  69.4 5.0 %collective-permute-done.15.refs_1_ = f32[512,128]{1,0:T(8,128)S(1)} collective-permute-done((f32[512,128]{1,0:T(8,128)S(1)}, f32[512,128]{1,0:T(8,128)S(1)}, u32[]{:S(2)}, u32[]{:S(2)}) %collective-permute-start.15) | collective-permute-done | bytes 262176 | tf_op jit(solution)/shard_map/ppermute | solution.py:83
  74.4 7.0 %collective-permute-done.16.refs_2_ = f32[512,128]{1,0:T(8,128)S(1)} collective-permute-done((f32[512,128]{1,0:T(8,128)S(1)}, f32[512,128]{1,0:T(8,128)S(1)}, u32[]{:S(2)}, u32[]{:S(2)}) %collective-permute-start.16) | collective-permute-done | bytes 262176 | tf_op jit(solution)/shard_map/ppermute | solution.py:83
  81.4 2.1 %collective-permute-done.17.refs_3_ = f32[512,128]{1,0:T(8,128)S(1)} collective-permute-done((f32[512,128]{1,0:T(8,128)S(1)}, f32[512,128]{1,0:T(8,128)S(1)}, u32[]{:S(2)}, u32[]{:S(2)}) %collective-permute-start.17) | collective-permute-done | bytes 262176 | tf_op jit(solution)/shard_map/ppermute | solution.py:83
  83.5 0.4 gram_part.1
  83.9 0.1 collective-permute-start.18
  84.0 3.4 %collective-permute-start.29 = (bf16[512,128]{1,0:T(8,128)(2,1)S(1)}, bf16[512,128]{1,0:T(8,128)(2,1)S(1)}, u32[]{:S(2)}, u32[]{:S(2)}) collective-permute-start(bf16[512,128]{1,0:T(8,128)(2,1)S(1)} %get-tuple-element.35.refs_4_), channel_id=1, source_target_pairs={{0,3},{1,2},{2,1},{3,0},{4,7},{5,6},{6,5},{7,4},{8,11},{9,10},{10,... | collective-permute-start | bytes 393224 | tf_op jit(solution)/shard_map/ppermute | solution.py:83
  87.4 0.0 collective-permute-start.28
  87.4 0.1 collective-permute-start.19
  87.5 3.5 %collective-permute-start.26 = (bf16[512,128]{1,0:T(8,128)(2,1)S(1)}, bf16[512,128]{1,0:T(8,128)(2,1)S(1)}, u32[]{:S(2)}, u32[]{:S(2)}) collective-permute-start(bf16[512,128]{1,0:T(8,128)(2,1)S(1)} %get-tuple-element.35.refs_4_), channel_id=1, source_target_pairs={{0,24},{1,16},{2,8},{3,0},{4,28},{5,20},{6,12},{7,4},{8,25},{9,17}... | collective-permute-start | bytes 393224 | tf_op jit(solution)/shard_map/ppermute | solution.py:103
  91.0 0.8 collective-permute-done.19.y_ref
  91.8 2.1 %collective-permute-start.20 = (f32[136,128]{1,0:T(8,128)S(1)}, f32[136,128]{1,0:T(8,128)S(1)}, u32[]{:S(2)}, u32[]{:S(2)}) collective-permute-start(f32[136,128]{1,0:T(8,128)S(1)} %join.6.x_ref), channel_id=1, source_target_pairs={{0,16},{4,20},{8,24},{12,28},{16,0},{20,4},{24,8},{28,12},{1,17},{... | collective-permute-start | bytes 208904 | tf_op jit(solution)/shard_map/ppermute | solution.py:345
  93.9 0.9 collective-permute-start.25
  94.8 0.6 collective-permute-start.24
  95.4 1.7 %collective-permute-done.28.refs_5_.refs_6_ = bf16[512,128]{1,0:T(8,128)(2,1)S(1)} collective-permute-done((bf16[512,128]{1,0:T(8,128)(2,1)S(1)}, bf16[512,128]{1,0:T(8,128)(2,1)S(1)}, u32[]{:S(2)}, u32[]{:S(2)}) %collective-permute-start.28) | collective-permute-done | bytes 131104 | tf_op jit(solution)/shard_map/ppermute | solution.py:83
  97.2 0.8 collective-permute-start.23
  98.0 2.3 %collective-permute-start.27 = (bf16[512,128]{1,0:T(8,128)(2,1)S(1)}, bf16[512,128]{1,0:T(8,128)(2,1)S(1)}, u32[]{:S(2)}, u32[]{:S(2)}) collective-permute-start(bf16[512,128]{1,0:T(8,128)(2,1)S(1)} %get-tuple-element.35.refs_4_), channel_id=1, source_target_pairs={{0,1},{1,0},{2,3},{3,2},{4,5},{5,4},{6,7},{7,6},{8,9},{9,8},{10,11... | collective-permute-start | bytes 393224 | tf_op jit(solution)/shard_map/ppermute | solution.py:83
  100.4 0.0 copy-start.3
  100.4 0.1 collective-permute-start.21
  100.5 0.1 collective-permute-start.33
  100.6 1.0 collective-permute-done.24.refs_1_.refs_9_
  101.6 0.5 collective-permute-start.31
  102.1 6.0 %collective-permute-done.21.y_ref = f32[136,128]{1,0:T(8,128)S(1)} collective-permute-done((f32[136,128]{1,0:T(8,128)S(1)}, f32[136,128]{1,0:T(8,128)S(1)}, u32[]{:S(2)}, u32[]{:S(2)}) %collective-permute-start.21) | collective-permute-done | bytes 69664 | tf_op jit(solution)/shard_map/ppermute | solution.py:345
  108.1 3.6 %collective-permute-start.22 = (f32[136,128]{1,0:T(8,128)S(1)}, f32[136,128]{1,0:T(8,128)S(1)}, u32[]{:S(2)}, u32[]{:S(2)}) collective-permute-start(f32[136,128]{1,0:T(8,128)S(1)} %join.8.x_ref), channel_id=1, source_target_pairs={{0,2},{1,3},{2,0},{3,1},{4,6},{5,7},{6,4},{7,5},{8,10},{9,11},{10,... | collective-permute-start | bytes 208904 | tf_op jit(solution)/shard_map/ppermute | solution.py:345
  111.7 2.4 %collective-permute-done.22.y_ref = f32[136,128]{1,0:T(8,128)S(1)} collective-permute-done((f32[136,128]{1,0:T(8,128)S(1)}, f32[136,128]{1,0:T(8,128)S(1)}, u32[]{:S(2)}, u32[]{:S(2)}) %collective-permute-start.22) | collective-permute-done | bytes 69664 | tf_op jit(solution)/shard_map/ppermute | solution.py:345
  114.2 4.1 %inverse.1 = (f32[128,128]{1,0:T(8,128)S(1)}, f32[8,128]{1,0:T(8,128)S(1)}) custom-call(f32[2048,4096]{1,0:T(8,128)S(1)} %copy-done.1, f32[136,128]{1,0:T(8,128)S(1)} %join.9.gram_ref, f32[1,128]{1,0:T(1,128)S(1)} %bitcast.6), custom_call_target="tpu_custom_call" | custom-call | tf_op jit(solution)/shard_map/inverse/pallas_call | solution.py:118
  118.3 0.0 collective-permute-done.31.refs_13_
  118.3 12.4 %update.1 = (f32[2048,4096]{1,0:T(8,128)}, f32[1,2048]{1,0:T(1,128)}) custom-call(f32[2048,4096]{1,0:T(8,128)S(1)} %copy-done.1, f32[128,128]{1,0:T(8,128)S(1)} %get-tuple-element.36.refs_1_, f32[8,128]{1,0:T(8,128)S(1)} %get-tuple-element.37.refs_2_, f32[1,2048]{1,0:T(1,128)S(1)} %bitcast.5, bf16[512,128]{1,0:T(8,128)(2,1)S(1)} %get-tuple-element.35.refs_4_, ...), custom_call_target="tpu_custom_call" | custom-call | tf_op jit(solution)/shard_map/update/pallas_call | solution.py:118
  (29 shorter events, 0.1 us)
Async XLA Ops:
  0.6 8.0 %collective-permute-start = (bf16[32,1024]{1,0:T(8,128)(2,1)}, bf16[32,1024]{1,0:T(8,128)(2,1)S(1)}, u32[]{:S(2)}, u32[]{:S(2)}) collective-permute-start(bf16[32,1024]{1,0:T(8,128)(2,1)} %refs_1_.1), channel_id=1, source_target_pairs={{0,1},{1,0},{2,3},{3,2},{4,5},{5,4},{6,7},{7,6},{8,9},{9,8},{10,11... | collective-permute-start | bytes 196616 | tf_op jit(solution)/shard_map/ppermute | solution.py:83
  3.6 5.4 %collective-permute-start.2 = (bf16[32,1024]{1,0:T(8,128)(2,1)}, bf16[32,1024]{1,0:T(8,128)(2,1)S(1)}, u32[]{:S(2)}, u32[]{:S(2)}) collective-permute-start(bf16[32,1024]{1,0:T(8,128)(2,1)} %refs_1_.1), channel_id=1, source_target_pairs={{0,3},{1,2},{2,1},{3,0},{4,7},{5,6},{6,5},{7,4},{8,11},{9,10},{10,... | collective-permute-start | bytes 196616 | tf_op jit(solution)/shard_map/ppermute | solution.py:83
  5.1 4.7 %collective-permute-start.1 = (bf16[32,1024]{1,0:T(8,128)(2,1)}, bf16[32,1024]{1,0:T(8,128)(2,1)S(1)}, u32[]{:S(2)}, u32[]{:S(2)}) collective-permute-start(bf16[32,1024]{1,0:T(8,128)(2,1)} %refs_1_.1), channel_id=1, source_target_pairs={{0,2},{1,3},{2,0},{3,1},{4,6},{5,7},{6,4},{7,5},{8,10},{9,11},{10,... | collective-permute-start | bytes 196616 | tf_op jit(solution)/shard_map/ppermute | solution.py:83
  10.6 2.7 %collective-permute-start.3 = (f32[128,2048]{1,0:T(8,128)S(1)}, f32[128,2048]{1,0:T(8,128)S(1)}, u32[]{:S(2)}, u32[]{:S(2)}) collective-permute-start(f32[128,2048]{1,0:T(8,128)S(1)} %preact_part.2), channel_id=1, source_target_pairs={{0,4},{4,0},{8,12},{12,8},{16,20},{20,16},{24,28},{28,24},{1,5},{5... | collective-permute-start | bytes 3145736 | tf_op jit(solution)/shard_map/ppermute | solution.py:92
  13.5 15.0 %collective-permute-start.4 = (f32[128,512]{1,0:T(8,128)S(1)}, f32[128,512]{1,0:T(8,128)S(1)}, u32[]{:S(2)}, u32[]{:S(2)}) collective-permute-start(f32[128,512]{1,0:T(8,128)S(1)} %get-tuple-element.25), channel_id=1, source_target_pairs={{0,24},{4,28},{8,16},{12,20},{16,8},{20,12},{24,0},{28,4},{1,25},{... | collective-permute-start | bytes 786440 | tf_op jit(solution)/shard_map/ppermute | solution.py:88
  17.1 22.6 %collective-permute-start.5 = (f32[128,512]{1,0:T(8,128)S(1)}, f32[128,512]{1,0:T(8,128)S(1)}, u32[]{:S(2)}, u32[]{:S(2)}) collective-permute-start(f32[128,512]{1,0:T(8,128)S(1)} %get-tuple-element.26), channel_id=1, source_target_pairs={{0,16},{4,20},{8,24},{12,28},{16,0},{20,4},{24,8},{28,12},{1,17},{... | collective-permute-start | bytes 786440 | tf_op jit(solution)/shard_map/ppermute | solution.py:88
  17.1 22.6 %collective-permute-start.6 = (f32[128,512]{1,0:T(8,128)S(1)}, f32[128,512]{1,0:T(8,128)S(1)}, u32[]{:S(2)}, u32[]{:S(2)}) collective-permute-start(f32[128,512]{1,0:T(8,128)S(1)} %get-tuple-element.27), channel_id=1, source_target_pairs={{0,8},{4,12},{8,0},{12,4},{16,24},{20,28},{24,16},{28,20},{1,9},{5... | collective-permute-start | bytes 786440 | tf_op jit(solution)/shard_map/ppermute | solution.py:88
  17.9 10.5 %copy-start = (f32[2048,4096]{1,0:T(8,128)S(1)}, f32[2048,4096]{1,0:T(8,128)}, u32[]{:S(2)}) copy-start(f32[2048,4096]{1,0:T(8,128)} %refs_0_.5) | copy-start | bytes 100663296
  39.8 16.3 %collective-permute-start.13 = (bf16[128,512]{1,0:T(8,128)(2,1)S(1)}, bf16[128,512]{1,0:T(8,128)(2,1)S(1)}, u32[]{:S(2)}, u32[]{:S(2)}) collective-permute-start(bf16[128,512]{1,0:T(8,128)(2,1)S(1)} %features.1.refs_0_), channel_id=1, source_target_pairs={{0,24},{4,28},{8,16},{12,20},{16,8},{20,12},{24,0},{28,4},{1,25},{... | collective-permute-start | bytes 393224 | tf_op jit(solution)/shard_map/ppermute | solution.py:88
  42.4 14.3 %collective-permute-start.11 = (bf16[128,512]{1,0:T(8,128)(2,1)S(1)}, bf16[128,512]{1,0:T(8,128)(2,1)S(1)}, u32[]{:S(2)}, u32[]{:S(2)}) collective-permute-start(bf16[128,512]{1,0:T(8,128)(2,1)S(1)} %features.1.refs_0_), channel_id=1, source_target_pairs={{0,16},{4,20},{8,24},{12,28},{16,0},{20,4},{24,8},{28,12},{1,17},{... | collective-permute-start | bytes 393224 | tf_op jit(solution)/shard_map/ppermute | solution.py:88
  42.4 14.4 %collective-permute-start.9 = (bf16[128,512]{1,0:T(8,128)(2,1)S(1)}, bf16[128,512]{1,0:T(8,128)(2,1)S(1)}, u32[]{:S(2)}, u32[]{:S(2)}) collective-permute-start(bf16[128,512]{1,0:T(8,128)(2,1)S(1)} %features.1.refs_0_), channel_id=1, source_target_pairs={{0,8},{4,12},{8,0},{12,4},{16,24},{20,28},{24,16},{28,20},{1,9},{5... | collective-permute-start | bytes 393224 | tf_op jit(solution)/shard_map/ppermute | solution.py:88
  44.3 16.3 %collective-permute-start.8 = (bf16[128,512]{1,0:T(8,128)(2,1)S(1)}, bf16[128,512]{1,0:T(8,128)(2,1)S(1)}, u32[]{:S(2)}, u32[]{:S(2)}) collective-permute-start(bf16[128,512]{1,0:T(8,128)(2,1)S(1)} %features.1.refs_0_), channel_id=1, source_target_pairs={{0,4},{4,0},{8,12},{12,8},{16,20},{20,16},{24,28},{28,24},{1,5},{5... | collective-permute-start | bytes 393224 | tf_op jit(solution)/shard_map/ppermute | solution.py:92
  44.3 10.5 %copy-start.1 = (f32[2048,4096]{1,0:T(8,128)S(1)}, f32[2048,4096]{1,0:T(8,128)}, u32[]{:S(2)}) copy-start(f32[2048,4096]{1,0:T(8,128)} %refs_0_.5) | copy-start | bytes 100663296
  56.1 4.5 %collective-permute-start.14 = (bf16[128,512]{1,0:T(8,128)(2,1)S(1)}, bf16[128,512]{1,0:T(8,128)(2,1)S(1)}, u32[]{:S(2)}, u32[]{:S(2)}) collective-permute-start(bf16[128,512]{1,0:T(8,128)(2,1)S(1)} %collective-permute-done.13.refs_2_), channel_id=1, source_target_pairs={{0,4},{4,0},{8,12},{12,8},{16,20},{20,16},{24,28},{28,24},{1,5},{5... | collective-permute-start | bytes 393224 | tf_op jit(solution)/shard_map/ppermute | solution.py:92
  56.7 4.0 %collective-permute-start.12 = (bf16[128,512]{1,0:T(8,128)(2,1)S(1)}, bf16[128,512]{1,0:T(8,128)(2,1)S(1)}, u32[]{:S(2)}, u32[]{:S(2)}) collective-permute-start(bf16[128,512]{1,0:T(8,128)(2,1)S(1)} %collective-permute-done.11.refs_1_), channel_id=1, source_target_pairs={{0,4},{4,0},{8,12},{12,8},{16,20},{20,16},{24,28},{28,24},{1,5},{5... | collective-permute-start | bytes 393224 | tf_op jit(solution)/shard_map/ppermute | solution.py:92
  56.8 3.9 %collective-permute-start.10 = (bf16[128,512]{1,0:T(8,128)(2,1)S(1)}, bf16[128,512]{1,0:T(8,128)(2,1)S(1)}, u32[]{:S(2)}, u32[]{:S(2)}) collective-permute-start(bf16[128,512]{1,0:T(8,128)(2,1)S(1)} %collective-permute-done.9.refs_0_), channel_id=1, source_target_pairs={{0,4},{4,0},{8,12},{12,8},{16,20},{20,16},{24,28},{28,24},{1,5},{5... | collective-permute-start | bytes 393224 | tf_op jit(solution)/shard_map/ppermute | solution.py:92
  57.2 26.3 %copy-start.2 = (f32[2048]{0:T(1024)S(1)}, f32[2048]{0:T(1024)}, u32[]{:S(2)}) copy-start(f32[2048]{0:T(1024)} %param.10) | copy-start | bytes 24580
  65.2 9.2 %collective-permute-start.15 = (f32[512,128]{1,0:T(8,128)S(1)}, f32[512,128]{1,0:T(8,128)S(1)}, u32[]{:S(2)}, u32[]{:S(2)}) collective-permute-start(f32[512,128]{1,0:T(8,128)S(1)} %get-tuple-element.31), channel_id=1, source_target_pairs={{0,1},{1,0},{2,3},{3,2},{4,5},{5,4},{6,7},{7,6},{8,9},{9,8},{10,11... | collective-permute-start | bytes 786440 | tf_op jit(solution)/shard_map/ppermute | solution.py:83
  66.5 15.0 %collective-permute-start.16 = (f32[512,128]{1,0:T(8,128)S(1)}, f32[512,128]{1,0:T(8,128)S(1)}, u32[]{:S(2)}, u32[]{:S(2)}) collective-permute-start(f32[512,128]{1,0:T(8,128)S(1)} %get-tuple-element.32), channel_id=1, source_target_pairs={{0,2},{1,3},{2,0},{3,1},{4,6},{5,7},{6,4},{7,5},{8,10},{9,11},{10,... | collective-permute-start | bytes 786440 | tf_op jit(solution)/shard_map/ppermute | solution.py:83
  67.5 16.0 %collective-permute-start.17 = (f32[512,128]{1,0:T(8,128)S(1)}, f32[512,128]{1,0:T(8,128)S(1)}, u32[]{:S(2)}, u32[]{:S(2)}) collective-permute-start(f32[512,128]{1,0:T(8,128)S(1)} %get-tuple-element.33), channel_id=1, source_target_pairs={{0,3},{1,2},{2,1},{3,0},{4,7},{5,6},{6,5},{7,4},{8,11},{9,10},{10,... | collective-permute-start | bytes 786440 | tf_op jit(solution)/shard_map/ppermute | solution.py:83
  68.7 0.7 collective-permute-start.7
  83.9 3.5 %collective-permute-start.18 = (f32[136,128]{1,0:T(8,128)S(1)}, f32[136,128]{1,0:T(8,128)S(1)}, u32[]{:S(2)}, u32[]{:S(2)}) collective-permute-start(f32[136,128]{1,0:T(8,128)S(1)} %get-tuple-element.34.x_ref), channel_id=1, source_target_pairs={{0,4},{4,0},{8,12},{12,8},{16,20},{20,16},{24,28},{28,24},{1,5},{5... | collective-permute-start | bytes 208904 | tf_op jit(solution)/shard_map/ppermute | solution.py:345
  84.0 10.8 %collective-permute-start.29 = (bf16[512,128]{1,0:T(8,128)(2,1)S(1)}, bf16[512,128]{1,0:T(8,128)(2,1)S(1)}, u32[]{:S(2)}, u32[]{:S(2)}) collective-permute-start(bf16[512,128]{1,0:T(8,128)(2,1)S(1)} %get-tuple-element.35.refs_4_), channel_id=1, source_target_pairs={{0,3},{1,2},{2,1},{3,0},{4,7},{5,6},{6,5},{7,4},{8,11},{9,10},{10,... | collective-permute-start | bytes 393224 | tf_op jit(solution)/shard_map/ppermute | solution.py:83
  87.4 9.8 %collective-permute-start.28 = (bf16[512,128]{1,0:T(8,128)(2,1)S(1)}, bf16[512,128]{1,0:T(8,128)(2,1)S(1)}, u32[]{:S(2)}, u32[]{:S(2)}) collective-permute-start(bf16[512,128]{1,0:T(8,128)(2,1)S(1)} %get-tuple-element.35.refs_4_), channel_id=1, source_target_pairs={{0,2},{1,3},{2,0},{3,1},{4,6},{5,7},{6,4},{7,5},{8,10},{9,11},{10,... | collective-permute-start | bytes 393224 | tf_op jit(solution)/shard_map/ppermute | solution.py:83
  87.4 4.4 %collective-permute-start.19 = (f32[136,128]{1,0:T(8,128)S(1)}, f32[136,128]{1,0:T(8,128)S(1)}, u32[]{:S(2)}, u32[]{:S(2)}) collective-permute-start(f32[136,128]{1,0:T(8,128)S(1)} %join.5.x_ref), channel_id=1, source_target_pairs={{0,8},{4,12},{8,0},{12,4},{16,24},{20,28},{24,16},{28,20},{1,9},{5... | collective-permute-start | bytes 208904 | tf_op jit(solution)/shard_map/ppermute | solution.py:345
  87.5 12.9 %collective-permute-start.26 = (bf16[512,128]{1,0:T(8,128)(2,1)S(1)}, bf16[512,128]{1,0:T(8,128)(2,1)S(1)}, u32[]{:S(2)}, u32[]{:S(2)}) collective-permute-start(bf16[512,128]{1,0:T(8,128)(2,1)S(1)} %get-tuple-element.35.refs_4_), channel_id=1, source_target_pairs={{0,24},{1,16},{2,8},{3,0},{4,28},{5,20},{6,12},{7,4},{8,25},{9,17}... | collective-permute-start | bytes 393224 | tf_op jit(solution)/shard_map/ppermute | solution.py:103
  91.8 6.2 %collective-permute-start.20 = (f32[136,128]{1,0:T(8,128)S(1)}, f32[136,128]{1,0:T(8,128)S(1)}, u32[]{:S(2)}, u32[]{:S(2)}) collective-permute-start(f32[136,128]{1,0:T(8,128)S(1)} %join.6.x_ref), channel_id=1, source_target_pairs={{0,16},{4,20},{8,24},{12,28},{16,0},{20,4},{24,8},{28,12},{1,17},{... | collective-permute-start | bytes 208904 | tf_op jit(solution)/shard_map/ppermute | solution.py:345
  93.9 6.6 %collective-permute-start.25 = (bf16[512,128]{1,0:T(8,128)(2,1)S(1)}, bf16[512,128]{1,0:T(8,128)(2,1)S(1)}, u32[]{:S(2)}, u32[]{:S(2)}) collective-permute-start(bf16[512,128]{1,0:T(8,128)(2,1)S(1)} %get-tuple-element.35.refs_4_), channel_id=1, source_target_pairs={{0,16},{1,24},{2,0},{3,8},{4,20},{5,28},{6,4},{7,12},{8,17},{9,25}... | collective-permute-start | bytes 393224 | tf_op jit(solution)/shard_map/ppermute | solution.py:103
  94.8 6.8 %collective-permute-start.24 = (bf16[512,128]{1,0:T(8,128)(2,1)S(1)}, bf16[512,128]{1,0:T(8,128)(2,1)S(1)}, u32[]{:S(2)}, u32[]{:S(2)}) collective-permute-start(bf16[512,128]{1,0:T(8,128)(2,1)S(1)} %get-tuple-element.35.refs_4_), channel_id=1, source_target_pairs={{0,8},{1,0},{2,24},{3,16},{4,12},{5,4},{6,28},{7,20},{8,9},{9,1},{... | collective-permute-start | bytes 393224 | tf_op jit(solution)/shard_map/ppermute | solution.py:103
  97.2 4.4 %collective-permute-start.23 = (bf16[512,128]{1,0:T(8,128)(2,1)S(1)}, bf16[512,128]{1,0:T(8,128)(2,1)S(1)}, u32[]{:S(2)}, u32[]{:S(2)}) collective-permute-start(bf16[512,128]{1,0:T(8,128)(2,1)S(1)} %get-tuple-element.35.refs_4_), channel_id=1, source_target_pairs={{0,0},{1,8},{2,16},{3,24},{4,4},{5,12},{6,20},{7,28},{8,1},{9,9},{... | collective-permute-start | bytes 393224 | tf_op jit(solution)/shard_map/ppermute | solution.py:103
  98.0 10.1 %collective-permute-start.27 = (bf16[512,128]{1,0:T(8,128)(2,1)S(1)}, bf16[512,128]{1,0:T(8,128)(2,1)S(1)}, u32[]{:S(2)}, u32[]{:S(2)}) collective-permute-start(bf16[512,128]{1,0:T(8,128)(2,1)S(1)} %get-tuple-element.35.refs_4_), channel_id=1, source_target_pairs={{0,1},{1,0},{2,3},{3,2},{4,5},{5,4},{6,7},{7,6},{8,9},{9,8},{10,11... | collective-permute-start | bytes 393224 | tf_op jit(solution)/shard_map/ppermute | solution.py:83
  100.4 13.8 %copy-start.3 = (f32[128]{0:T(128)S(1)}, f32[128]{0:T(128)}, u32[]{:S(2)}) copy-start(f32[128]{0:T(128)} %param.11) | copy-start | bytes 1540
  100.4 7.7 %collective-permute-start.21 = (f32[136,128]{1,0:T(8,128)S(1)}, f32[136,128]{1,0:T(8,128)S(1)}, u32[]{:S(2)}, u32[]{:S(2)}) collective-permute-start(f32[136,128]{1,0:T(8,128)S(1)} %join.7.x_ref), channel_id=1, source_target_pairs={{0,1},{1,0},{2,3},{3,2},{4,5},{5,4},{6,7},{7,6},{8,9},{9,8},{10,11... | collective-permute-start | bytes 208904 | tf_op jit(solution)/shard_map/ppermute | solution.py:345
  100.5 17.8 %collective-permute-start.33 = (bf16[512,128]{1,0:T(8,128)(2,1)S(1)}, bf16[512,128]{1,0:T(8,128)(2,1)S(1)}, u32[]{:S(2)}, u32[]{:S(2)}) collective-permute-start(bf16[512,128]{1,0:T(8,128)(2,1)S(1)} %collective-permute-done.26.refs_3_.refs_11_), channel_id=1, source_target_pairs={{0,4},{4,0},{8,12},{12,8},{16,20},{20,16},{24,28},{28,24},{1,5},{5... | collective-permute-start | bytes 393224 | tf_op jit(solution)/shard_map/ppermute | solution.py:92
  101.6 16.7 %collective-permute-start.32 = (bf16[512,128]{1,0:T(8,128)(2,1)S(1)}, bf16[512,128]{1,0:T(8,128)(2,1)S(1)}, u32[]{:S(2)}, u32[]{:S(2)}) collective-permute-start(bf16[512,128]{1,0:T(8,128)(2,1)S(1)} %collective-permute-done.25.refs_2_.refs_10_), channel_id=1, source_target_pairs={{0,4},{4,0},{8,12},{12,8},{16,20},{20,16},{24,28},{28,24},{1,5},{5... | collective-permute-start | bytes 393224 | tf_op jit(solution)/shard_map/ppermute | solution.py:92
  101.6 16.7 %collective-permute-start.31 = (bf16[512,128]{1,0:T(8,128)(2,1)S(1)}, bf16[512,128]{1,0:T(8,128)(2,1)S(1)}, u32[]{:S(2)}, u32[]{:S(2)}) collective-permute-start(bf16[512,128]{1,0:T(8,128)(2,1)S(1)} %collective-permute-done.24.refs_1_.refs_9_), channel_id=1, source_target_pairs={{0,4},{4,0},{8,12},{12,8},{16,20},{20,16},{24,28},{28,24},{1,5},{5... | collective-permute-start | bytes 393224 | tf_op jit(solution)/shard_map/ppermute | solution.py:92
  108.1 10.2 %collective-permute-start.30 = (bf16[512,128]{1,0:T(8,128)(2,1)S(1)}, bf16[512,128]{1,0:T(8,128)(2,1)S(1)}, u32[]{:S(2)}, u32[]{:S(2)}) collective-permute-start(bf16[512,128]{1,0:T(8,128)(2,1)S(1)} %collective-permute-done.23.refs_0_.refs_8_), channel_id=1, source_target_pairs={{0,4},{4,0},{8,12},{12,8},{16,20},{20,16},{24,28},{28,24},{1,5},{5... | collective-permute-start | bytes 393224 | tf_op jit(solution)/shard_map/ppermute | solution.py:92
  108.1 6.0 %collective-permute-start.22 = (f32[136,128]{1,0:T(8,128)S(1)}, f32[136,128]{1,0:T(8,128)S(1)}, u32[]{:S(2)}, u32[]{:S(2)}) collective-permute-start(f32[136,128]{1,0:T(8,128)S(1)} %join.8.x_ref), channel_id=1, source_target_pairs={{0,2},{1,3},{2,0},{3,1},{4,6},{5,7},{6,4},{7,5},{8,10},{9,11},{10,... | collective-permute-start | bytes 208904 | tf_op jit(solution)/shard_map/ppermute | solution.py:345
